TPU v7x, 32 devices: a whole 2x2x4 slice. The times are simulated.
32 devices in a mesh: expert: 8 (over z, y), tensor: 4 (over x, core).
Axes of the slice: x: 2, y: 2, z: 4, core: 2. Of those that a mesh axis runs over, the one named last changes fastest.
Arguments:
- tokens: bfloat16 [256, 1536], P('expert')
- attn_gain: bfloat16 [1536], replicated, may hold values from 0.099609375 to 1.8984375
- query_weight: bfloat16 [1536, 1536], P(None, 'tensor'), may hold values from -0.15625 to 0.15625
- key_value_weight: bfloat16 [4, 1536, 128], P('tensor'), may hold values from -0.15625 to 0.15625
- paired_cache: bfloat16 [8, 4, 768, 128], P('expert', 'tensor')
- prompt_length: int32 [8, 3], P('expert'), may hold values from 1 to 256, 640 in all within a row
- group_index: int32 [256], P('expert'), may hold values from 0 to 2
- offsets: int32 [256], P('expert'), may hold values from 0 to 127
- sink_logit: float32 [12], P('tensor'), may hold values from -2 to 4
- out_weight: bfloat16 [1536, 1536], P('tensor'), may hold values from -0.15625 to 0.15625
- mixer_gain: bfloat16 [1536], replicated, may hold values from 0.099609375 to 1.8984375
- routes: int32 [256, 4], P('expert'), may hold values from 0 to 31, all different within a row; in each aligned block of 32 rows (0 to 31, 32 to 63, ...) at most 8 rows name the same one
- route_weight: float32 [256, 4], P('expert'), may hold values from 0.05 to 1
- copy_slot: int32 [32], replicated, may hold values from 0 to 31, as said below
- gate_weight: bfloat16 [32, 1536, 768], P('expert', None, 'tensor'), as said below
- up_weight: bfloat16 [32, 1536, 768], P('expert', None, 'tensor'), as said below
- down_weight: bfloat16 [32, 768, 1536], P('expert', 'tensor'), as said below
- final_gain: bfloat16 [1536], P('tensor'), may hold values from 0.099609375 to 1.8984375
Outputs:
- normed: bfloat16 [256, 1536], P('expert', 'tensor')
Inputs may be any that keep to these rules, and one draw needn't show every extreme that they name: `routes`: in each aligned block of 32 rows no expert is named by more than 8 rows, and in some block one is named by exactly 8. `copy_slot`: a permutation: every slot appears once; slot s lies on expert-axis index s // 4 as its local copy s % 4. `prompt_length`: on every expert-axis index one prompt fills all 256 slots. `gate_weight`: all 1 replicas of an expert hold equal weights. `up_weight`: all 1 replicas of an expert hold equal weights. `down_weight`: all 1 replicas of an expert hold equal weights.
All inputs are finite; a program needn't handle non-finite values.
Results may differ from a plain program's by a relative error of at most 0.013.
Values may be sent and summed in bfloat16 or wider, within the bound.
No kernel may reach another device: no remote copies, remote signals or barrier semaphores. Data moves between devices by JAX's collectives and lax.ppermute only.
A program may use at most 64 MiB of HBM per device.

v0:
```python
import jax
import jax.numpy as jnp
from jax import lax
from jax.sharding import PartitionSpec as P

EXPERTS = 32
TOP = 4
PROMPT_CAP = 256
WINDOW = 192


EPSILON = 1e-06


def from_partner(block, axis, apart):
    count = lax.axis_size(axis)
    route = []
    for low in range(count):
        high = low | 1 << apart
        if high != low and high < count:
            route += [(low, high), (high, low)]
    return lax.ppermute(block, axis, route)


def rms_scale(values, gain_row):
    mean_square = jnp.mean(values * values, axis=-1, keepdims=True)
    return values * lax.rsqrt(mean_square + EPSILON) * gain_row.astype(jnp.float32)


def rotate(values, position):
    half_dim = values.shape[-1] // 2
    frequency = 10000.0 ** (-jnp.arange(half_dim, dtype=jnp.float32) / half_dim)
    angles = position.astype(jnp.float32)[:, None] * frequency[None, :]
    if values.ndim == 3:
        angles = angles[:, None, :]
    cosine_part = jnp.cos(angles)
    sine_part = jnp.sin(angles)
    front_half = values[..., :half_dim]
    back_half = values[..., half_dim:]
    return jnp.concatenate(
        [
            front_half * cosine_part - back_half * sine_part,
            front_half * sine_part + back_half * cosine_part,
        ],
        axis=-1,
    )


def slot_places(routes, copy_slot, replicas):
    row_count = routes.shape[0]
    flat_routes = routes.reshape(-1)
    slot_count = flat_routes.shape[0]
    block_of = jnp.arange(slot_count, dtype=jnp.int32) // TOP // (row_count // replicas)
    onehot = (flat_routes[:, None] == jnp.arange(EXPERTS, dtype=jnp.int32)[None, :]).astype(
        jnp.int32
    )
    grouped = onehot.reshape(replicas, slot_count // replicas, EXPERTS)
    earlier = jnp.cumsum(grouped, axis=1) - grouped
    slot_rank = jnp.sum(earlier * grouped, axis=-1).reshape(slot_count)
    holder = copy_slot[flat_routes * replicas + block_of]
    return (holder, slot_rank)


def on_device(
    tokens,
    attn_gain,
    query_weight,
    key_value_weight,
    paired_cache,
    prompt_length,
    group_index,
    offsets,
    sink_logit,
    out_weight,
    mixer_gain,
    routes,
    route_weight,
    copy_slot,
    gate_weight,
    up_weight,
    down_weight,
    final_gain,
):
    lanes = lax.axis_size("tensor")
    member = lax.axis_index("tensor")
    peers = lax.axis_size("expert")
    tok_rows, width = tokens.shape
    head_dim = key_value_weight.shape[2]
    local_heads = query_weight.shape[1] // head_dim
    score_scale = 1.0 / head_dim**0.5
    rows_f32 = tokens.astype(jnp.float32)
    normed_in = rms_scale(rows_f32, attn_gain).astype(jnp.bfloat16)
    lengths = prompt_length[0]
    prompt_slots = jnp.arange(lengths.shape[0], dtype=jnp.int32)
    row_length = jnp.sum(
        jnp.where(group_index[:, None] == prompt_slots[None, :], lengths[None, :], 0), axis=1
    )
    position = row_length + offsets
    queries = jnp.dot(normed_in, query_weight, preferred_element_type=jnp.float32).reshape(
        tok_rows, local_heads, head_dim
    )
    queries = rotate(queries, position).astype(jnp.bfloat16)
    projected = jnp.dot(normed_in, key_value_weight[0], preferred_element_type=jnp.float32)
    marks_key = member % 2 == 0
    own_projection = jnp.where(marks_key, rotate(projected, position), projected).astype(
        jnp.bfloat16
    )
    own_cache = paired_cache[0, 0]
    partner, partner_cache = from_partner((own_projection, own_cache), "tensor", 0)
    new_keys = jnp.where(marks_key, own_projection, partner)
    new_values = jnp.where(marks_key, partner, own_projection)
    cache_keys = jnp.where(marks_key, own_cache, partner_cache)
    cache_values = jnp.where(marks_key, partner_cache, own_cache)
    scores = (
        jnp.einsum("thd,cd->thc", queries, cache_keys, preferred_element_type=jnp.float32)
        * score_scale
    )
    self_score = (
        jnp.sum(queries.astype(jnp.float32) * new_keys.astype(jnp.float32)[:, None, :], axis=-1)
        * score_scale
    )
    slot_index = jnp.arange(cache_keys.shape[0], dtype=jnp.int32)
    slot_group = slot_index // PROMPT_CAP
    slot_pos = slot_index % PROMPT_CAP
    visible = (
        (slot_group[None, :] == group_index[:, None])
        & (slot_pos[None, :] < row_length[:, None])
        & (slot_pos[None, :] > position[:, None] - WINDOW)
    )
    visible = visible[:, None, :]
    masked = jnp.where(visible, scores, -jnp.inf)
    ceiling = jnp.maximum(jnp.maximum(jnp.max(masked, axis=-1), self_score), sink_logit[None, :])
    weights = jnp.where(visible, jnp.exp(scores - ceiling[..., None]), 0.0)
    own_weight = jnp.exp(self_score - ceiling)
    denominator = jnp.sum(weights, axis=-1) + own_weight + jnp.exp(sink_logit[None, :] - ceiling)
    probabilities = (weights / denominator[..., None]).astype(jnp.bfloat16)
    own_prob = (own_weight / denominator).astype(jnp.bfloat16)
    context = jnp.einsum(
        "thc,cd->thd", probabilities, cache_values, preferred_element_type=jnp.float32
    )
    context = (
        context
        + own_prob.astype(jnp.float32)[..., None] * new_values.astype(jnp.float32)[:, None, :]
    )
    context = context.astype(jnp.bfloat16).reshape(tok_rows, local_heads * head_dim)
    attended = jnp.dot(context, out_weight, preferred_element_type=jnp.float32)
    part_width = width // lanes
    feature_start = member * part_width
    copies = copy_slot.shape[0]
    hosted = gate_weight.shape[0]
    replicas = copies // EXPERTS
    capacity = 2 * tok_rows * TOP // (replicas * EXPERTS)
    holders, slot_ranks = slot_places(routes, copy_slot, replicas)
    places = holders * capacity + slot_ranks
    slot_rows = jnp.arange(tok_rows * TOP, dtype=jnp.int32) // TOP
    recv_rows = peers * capacity
    summed = lax.psum(attended.astype(jnp.bfloat16), "tensor").astype(jnp.float32)
    residual_full = (rows_f32 + summed).astype(jnp.bfloat16)
    residual = lax.dynamic_slice_in_dim(residual_full, feature_start, part_width, 1)
    mixed_in = rms_scale(residual_full.astype(jnp.float32), mixer_gain).astype(jnp.bfloat16)
    features = mixed_in.shape[1]
    outbox = (
        jnp.zeros((copies * capacity, features), jnp.bfloat16).at[places].set(mixed_in[slot_rows])
    )
    received = lax.all_to_all(
        outbox.reshape(peers, hosted * capacity, features),
        "expert",
        split_axis=0,
        concat_axis=0,
        tiled=True,
    )
    to_features = received.shape[2]
    received = (
        received.reshape(peers, hosted, capacity, to_features)
        .transpose(1, 0, 2, 3)
        .reshape(hosted, recv_rows, to_features)
    )
    gate_val = jnp.einsum("hrd,hdf->hrf", received, gate_weight, preferred_element_type=jnp.float32)
    up_val = jnp.einsum("hrd,hdf->hrf", received, up_weight, preferred_element_type=jnp.float32)
    hidden = (jnp.maximum(gate_val, 0.0) * up_val).astype(jnp.bfloat16)
    partial_sums = jnp.einsum(
        "hrf,hfd->hrd", hidden, down_weight, preferred_element_type=jnp.float32
    )
    shares = lax.psum_scatter(
        partial_sums.astype(jnp.bfloat16), "tensor", scatter_dimension=2, tiled=True
    )
    outgoing = (
        shares.reshape(hosted, peers, capacity, part_width)
        .transpose(1, 0, 2, 3)
        .reshape(peers, hosted * capacity, part_width)
    )
    returned = lax.all_to_all(outgoing, "expert", split_axis=0, concat_axis=0, tiled=True).reshape(
        copies * capacity, part_width
    )
    per_slot = returned[places].astype(jnp.float32).reshape(tok_rows, TOP, part_width)
    mixture = jnp.sum(route_weight[:, :, None] * per_slot, axis=1)
    combined = residual.astype(jnp.float32) + mixture
    totals = lax.psum(jnp.sum(combined * combined, axis=1), "tensor")
    return (
        combined
        * lax.rsqrt(totals[:, None] / width + EPSILON)
        * final_gain.astype(jnp.float32)[None, :]
    ).astype(jnp.bfloat16)


def solution(mesh):
    in_specs = (
        P("expert", None),
        P(),
        P(None, "tensor"),
        P("tensor", None, None),
        P("expert", "tensor", None, None),
        P("expert", None),
        P("expert"),
        P("expert"),
        P("tensor"),
        P("tensor", None),
        P(),
        P("expert", None),
        P("expert", None),
        P(),
        P("expert", None, "tensor"),
        P("expert", None, "tensor"),
        P("expert", "tensor", None),
        P("tensor"),
    )
    out_specs = P("expert", "tensor")
    return jax.shard_map(
        on_device, mesh=mesh, in_specs=in_specs, out_specs=out_specs, check_vma=False
    )
```

profile of v0, /device:TPU:0, one launch (start us, length us, event | category | flops | bytes accessed | tf_op | source)
XLA Modules:
  0.0 149.2 jit_solution(8604443287889550511)
XLA Ops:
  6.6 0.8 convert_element_type.101
  7.5 1.0 fusion.18
  8.5 0.8 select_reduce_fusion.2
  9.9 1.3 fusion.9
  12.1 0.8 copy.58
  13.1 1.7 %fusion.35 = f32[32,384]{1,0:T(8,128)S(1)} fusion(bf16[1536,384]{1,0:T(8,128)(2,1)} %param.20, bf16[32,1536]{1,0:T(8,128)(2,1)} %param.18, f32[1536]{0:T(1024)S(1)} %convert_element_type.101, f32[32]{0:T(128)S(1)} %add_rsqrt_fusion.2), kind=kOutput, calls=%fused_computation.62 | convolution fusion | flops 37945344 | bytes 1333376 | tf_op jit(solution)/shard_map/dot_general | solution.py:99
  15.4 1.2 gather_fusion
  18.0 2.2 %convolution_convert_fusion.1 = bf16[32,1536]{1,0:T(8,128)(2,1)} fusion(bf16[384,1536]{1,0:T(8,128)(2,1)} %param.27, bf16[3,4,8,128]{3,2,1,0:T(8,128)(2,1)S(1)} %fusion.2), kind=kOutput, calls=%fused_computation.5 | convolution fusion | flops 37797888 | bytes 1302528 | tf_op jit(solution)/shard_map/dot_general | solution.py:146
  20.4 34.0 %all-reduce.2.cloned.1.call-done = bf16[32,1536]{1,0:T(8,128)(2,1)} async-done(((bf16[32,1536]{1,0:T(8,128)(2,1)}), bf16[32,1536]{1,0:T(8,128)(2,1)}) %all-reduce.2.cloned.1.call-update) | async-done | bytes 98320 | tf_op jit(solution)/shard_map/psum | solution.py:157
  54.4 1.0 fusion.15
  55.6 3.4 %scatter_custom_fusion = bf16[256,1536]{1,0:T(8,128)(2,1)} fusion(s32[128]{0:T(128)S(1)} %fusion.48, bf16[32,1536]{1,0:T(8,128)(2,1)S(1)} %fusion.17, s32[1024]{0:T(1024)S(1)} %pad_clamp_fusion.1, bf16[]{:T(256)} %constant.109.clone.1), kind=kCustom, calls=%fused_computation.19 | custom fusion | bytes 786434 | tf_op jit(solution)/shard_map/scatter | solution.py:163
  59.0 24.6 %all_to_all.10 = bf16[8,32,1536]{2,1,0:T(8,128)(2,1)S(1)} all-to-all(bf16[8,32,1536]{2,1,0:T(8,128)(2,1)} %bitcast.70), channel_id=1, replica_groups=mesh['expert'=8,'tensor'=4] {'expert'}, dimensions={0} | all-to-all | bytes 1572864 | tf_op jit(solution)/shard_map/all_to_all | solution.py:165
  83.6 2.5 %convolution_maximum_fusion = f32[4,64,192]{2,1,0:T(8,128)S(1)} fusion(bf16[4,1536,192]{1,2,0:T(8,128)(2,1)} %param.32, bf16[8,32,1536]{2,1,0:T(8,128)(2,1)S(1)} %all_to_all.10), kind=kOutput, calls=%fused_computation.8 | convolution fusion | flops 151044096 | bytes 3342336 | tf_op jit(solution)/shard_map/hrd,hdf->hrf/dot_general | solution.py:178
  86.1 3.9 %convolution_convert_fusion = bf16[4,64,1536]{2,1,0:T(8,128)(2,1)} fusion(bf16[4,192,1536]{2,1,0:T(8,128)(2,1)S(1)} %copy-done, f32[4,64,192]{2,1,0:T(8,128)S(1)} %convolution_maximum_fusion, bf16[4,1536,192]{1,2,0:T(8,128)(2,1)} %param.33, bf16[8,32,1536]{2,1,0:T(8,128)(2,1)S(1)} %all_to_all.10), kind=kOutput, calls=%fused_computation.4 | convolution fusion | flops 302481408 | bytes 6488064 | tf_op jit(solution)/shard_map/hrf,hfd->hrd/dot_general | solution.py:181
  90.0 3.4 %copy.62 = bf16[4,64,1536]{1,0,2:T(4,128)(2,1)} copy(bf16[4,64,1536]{2,1,0:T(8,128)(2,1)} %convolution_convert_fusion) | data formatting | bytes 1572864
  93.4 3.6 %reshape.544 = bf16[1536,256]{1,0:T(8,128)(2,1)} reshape(bf16[1536,4,64]{2,1,0:T(4,128)(2,1)} %bitcast.68) | data formatting | bytes 1572864
  97.1 21.8 %reduce-scatter.4.cloned.1.call-done = bf16[384,256]{1,0:T(8,128)(2,1)} async-done(((bf16[1536,256]{1,0:T(8,128)(2,1)}), bf16[384,256]{1,0:T(8,128)(2,1)}) %reduce-scatter.4.cloned.1.call-update) | async-done | bytes 196624
  118.9 1.2 reshape.545
  120.3 0.7 copy_bitcast_fusion
  121.0 5.5 %all-to-all-start.1 = ((bf16[8,32,384]{2,1,0:T(8,128)(2,1)}), bf16[8,32,384]{2,1,0:T(8,128)(2,1)S(1)}, u32[]{:S(2)}, u32[]{:S(2)}) async-start(bf16[8,32,384]{2,1,0:T(8,128)(2,1)} %copy_bitcast_fusion), calls=%async_computation.1 | async-start | bytes 393216 | tf_op jit(solution)/shard_map/all_to_all | solution.py:192
  126.6 7.8 %all-to-all-done.1 = bf16[8,32,384]{2,1,0:T(8,128)(2,1)S(1)} async-done(((bf16[8,32,384]{2,1,0:T(8,128)(2,1)}), bf16[8,32,384]{2,1,0:T(8,128)(2,1)S(1)}, u32[]{:S(2)}, u32[]{:S(2)}) %all-to-all-start.1) | async-done | bytes 196640 | tf_op jit(solution)/shard_map/all_to_all | solution.py:192
  134.4 0.9 gather_fusion.1
  135.7 6.0 %psum.15 = f32[32]{0:T(128)S(1)} all-reduce(f32[32]{0:T(128)S(1)} %multiply_reduce_fusion.1), channel_id=1, replica_groups=mesh['expert'=8,'tensor'=4] {'tensor'}, use_global_device_ids=true, to_apply=%region_13.14 | all-reduce | flops 32 | bytes 256 | tf_op jit(solution)/shard_map/psum | solution.py:198
  141.6 0.7 multiply_convert_fusion
  (65 shorter events, 4.6 us)
Async XLA Ops:
  6.5 79.6 %copy-start = (bf16[4,192,1536]{2,1,0:T(8,128)(2,1)S(1)}, bf16[4,192,1536]{2,1,0:T(8,128)(2,1)}, u32[]{:S(2)}) copy-start(bf16[4,192,1536]{2,1,0:T(8,128)(2,1)} %param.34) | copy-start | bytes 7077892
  6.5 10.1 %copy-start.8 = (s32[32]{0:T(128)S(1)}, s32[32]{0:T(128)}, u32[]{:S(2)}) copy-start(s32[32]{0:T(128)} %param.24) | copy-start | bytes 388
  6.5 10.5 %copy-start.3 = (bf16[1,1,768,128]{3,2,1,0:T(8,128)(2,1)S(1)}, bf16[1,1,768,128]{3,2,1,0:T(8,128)(2,1)}, u32[]{:S(2)}) copy-start(bf16[1,1,768,128]{3,2,1,0:T(8,128)(2,1)} %param.22) | copy-start | bytes 589828
  6.5 8.9 %copy-start.1 = (s32[32]{0:T(128)S(1)}, s32[32]{0:T(128)}, u32[]{:S(2)}) copy-start(s32[32]{0:T(128)} %param.31) | copy-start | bytes 388
  6.5 10.8 %copy-start.6 = (f32[3]{0:T(128)S(1)}, f32[3]{0:T(128)}, u32[]{:S(2)}) copy-start(f32[3]{0:T(128)} %param.26) | copy-start | bytes 40
  6.5 47.9 %all-reduce.2.cloned.1.call-start = ((), (), s32[]{:S(2)}) async-start(), calls=%async_computation.3 | async-start | bytes 196608 | tf_op jit(solution)/shard_map/psum | solution.py:157
  11.4 5.4 %collective-permute-start.1 = (bf16[32,128]{1,0:T(8,128)(2,1)S(1)}, bf16[32,128]{1,0:T(8,128)(2,1)S(1)}, u32[]{:S(2)}, u32[]{:S(2)}) collective-permute-start(bf16[32,128]{1,0:T(8,128)(2,1)S(1)} %fusion.37), channel_id=1, source_target_pairs={{0,1},{1,0},{2,3},{3,2},{4,5},{5,4},{6,7},{7,6},{8,9},{9,8},{10,11... | collective-permute-start | bytes 24584 | tf_op jit(solution)/shard_map/ppermute | solution.py:22
  11.9 5.1 %collective-permute-start = (bf16[768,128]{1,0:T(8,128)(2,1)}, bf16[768,128]{1,0:T(8,128)(2,1)S(1)}, u32[]{:S(2)}, u32[]{:S(2)}) collective-permute-start(bf16[768,128]{1,0:T(8,128)(2,1)} %bitcast.72), channel_id=1, source_target_pairs={{0,1},{1,0},{2,3},{3,2},{4,5},{5,4},{6,7},{7,6},{8,9},{9,8},{10,11... | collective-permute-start | bytes 589832 | tf_op jit(solution)/shard_map/ppermute | solution.py:22
  16.8 3.6 %copy-start.4 = (bf16[1536]{0:T(1024)(128)(2,1)S(1)}, bf16[1536]{0:T(1024)(128)(2,1)}, u32[]{:S(2)}) copy-start(bf16[1536]{0:T(1024)(128)(2,1)} %param.28) | copy-start | bytes 9220
  16.8 37.6 %copy-start.2 = (bf16[32,1536]{1,0:T(8,128)(2,1)S(1)}, bf16[32,1536]{1,0:T(8,128)(2,1)}, u32[]{:S(2)}) copy-start(bf16[32,1536]{1,0:T(8,128)(2,1)} %param.18) | copy-start | bytes 294916
  20.3 98.6 %reduce-scatter.4.cloned.1.call-start = ((), (), s32[]{:S(2)}) async-start(), calls=%async_computation.4 | async-start | bytes 983040
  93.4 33.0 %copy-start.5 = (f32[32,4]{0,1:T(4,128)S(1)}, f32[32,4]{0,1:T(4,128)}, u32[]{:S(2)}) copy-start(f32[32,4]{0,1:T(4,128)} %param.30) | copy-start | bytes 1540
  93.4 33.1 %copy-start.7 = (bf16[384]{0:T(512)(128)(2,1)S(1)}, bf16[384]{0:T(512)(128)(2,1)}, u32[]{:S(2)}) copy-start(bf16[384]{0:T(512)(128)(2,1)} %param.35) | copy-start | bytes 2308
  121.0 13.5 %all-to-all-start.1 = ((bf16[8,32,384]{2,1,0:T(8,128)(2,1)}), bf16[8,32,384]{2,1,0:T(8,128)(2,1)S(1)}, u32[]{:S(2)}, u32[]{:S(2)}) async-start(bf16[8,32,384]{2,1,0:T(8,128)(2,1)} %copy_bitcast_fusion), calls=%async_computation.1 | async-start | bytes 393216 | tf_op jit(solution)/shard_map/all_to_all | solution.py:192
Sparse Core Ops, SparseCore 0:
  20.4 33.9 all-reduce.1
  97.2 21.6 reduce-scatter.3
where the time goes:
time: 150 us; the launch traced here: 149 us
  waiting for transfers between devices  63.7 us (42%)
  blocking collectives  30.6 us (20%)
  local copies, waits for them, and re-layouts  15.9 us (11%)
  between operations  13.7 us (9%)
  matrix products  12.2 us (8%)
  other arithmetic  6.95 us (5%)
  starting transfers between devices  6.14 us (4%)
    psum x1, waiting for transfers between devices, on_device(): lax.psum(attended.astype(jnp.bfloat16), 'tensor').astype(jnp.float32)  34 us
    all_to_all x1, blocking collectives, on_device(): lax.all_to_all(outbox.reshape(peers, hosted * capacity, features), 'exper...  24.6 us
    unnamed x3, waiting for transfers between devices  21.8 us
    unnamed x24, local copies, waits for them, and re-layouts  9.35 us
    all_to_all x1, waiting for transfers between devices, on_device(): lax.all_to_all(outgoing, 'expert', split_axis=0, concat_axis=0, tiled=True)  7.83 us
    psum x1, blocking collectives, on_device(): totals = lax.psum(jnp.sum(combined * combined, axis=1), 'tensor')  5.96 us
    all_to_all x1, starting transfers between devices, on_device(): lax.all_to_all(outgoing, 'expert', split_axis=0, concat_axis=0, tiled=True)  5.52 us
    dot_general x1, matrix products, on_device(): jnp.einsum('hrf,hfd->hrd', hidden, down_weight, preferred_element_type=jn...  3.86 us
  transfers between devices with their start and end apart: 5, of which 3 were waited for; matrix products, arithmetic and copies ran while one was open for 3% of the time, Pallas kernels for 0%

commit v1 on v0

v1 whole, which is shorter than its diff:
```python
import functools
import math

import jax
import jax.numpy as jnp
from jax import lax
from jax.experimental import pallas as pl
from jax.experimental.pallas import tpu as pltpu
from jax.sharding import PartitionSpec as P

EXPERTS = 32
TOP = 4
PROMPT_CAP = 256
WINDOW = 192
EPSILON = 1e-06
LANES = 128
HIDE = -1e30
F32 = jnp.float32
BF16 = jnp.bfloat16
I32 = jnp.int32


def swap(block, axis, bits):
    count = lax.axis_size(axis)
    return lax.ppermute(block, axis, [(i, i ^ bits) for i in range(count)])


def swap_both(block, expert_bits, tensor_bits):
    lanes = lax.axis_size("tensor")
    count = lax.axis_size("expert") * lanes
    bits = expert_bits * lanes + tensor_bits
    return lax.ppermute(block, ("expert", "tensor"), [(i, i ^ bits) for i in range(count)])


def iota(shape, dim):
    return lax.broadcasted_iota(I32, shape, dim)


def dot(a, b):
    return jnp.dot(a, b, preferred_element_type=F32)


def dot_t(a, b):
    return lax.dot_general(a, b, (((1,), (1,)), ((), ())), preferred_element_type=F32)


def call(body, outs, args, smem=(), vmem=None, cost=None, name=None):
    in_specs = [
        pl.BlockSpec(memory_space=pltpu.SMEM) if i in smem else pl.BlockSpec(memory_space=pltpu.VMEM)
        for i in range(len(args))
    ]
    single = not isinstance(outs, (list, tuple))
    listed = [outs] if single else list(outs)
    out_specs = [pl.BlockSpec(memory_space=pltpu.VMEM) for _ in listed]
    flops, nbytes = cost or (0, 0)
    result = pl.pallas_call(
        body,
        out_shape=listed,
        in_specs=in_specs,
        out_specs=out_specs,
        compiler_params=pltpu.CompilerParams(vmem_limit_bytes=vmem or 16 << 20),
        cost_estimate=pl.CostEstimate(flops=flops, bytes_accessed=nbytes, transcendentals=0),
        name=name,
    )(*args)
    return result[0] if single else result


def shape(dims, dtype):
    return jax.ShapeDtypeStruct(tuple(dims), dtype)


def spread(rows, values):
    index = iota((rows, LANES), 0)
    total = jnp.full((rows, LANES), values[0], I32)
    for i in range(1, rows):
        total = jnp.where(index == i, values[i], total)
    return total


def row_places(rows, length_ref, group_ref, offset_ref):
    groups = [group_ref[i] for i in range(rows)]
    lengths = [length_ref[0, g] for g in groups]
    row_length = spread(rows, lengths)
    position = spread(rows, [lengths[i] + offset_ref[i] for i in range(rows)])
    return spread(rows, groups), row_length, position


def project_body(member_ref, length_ref, group_ref, offset_ref, tok_ref, gain_ref, qw_ref, kvw_ref, q_ref, own_ref):
    rows, width = tok_ref.shape
    dim = kvw_ref.shape[2]
    heads = qw_ref.shape[1] // dim
    half = dim // 2
    tok = tok_ref[...].astype(F32)
    mean = jnp.sum(tok * tok, axis=1, keepdims=True) / width
    normed = (tok * lax.rsqrt(mean + EPSILON) * gain_ref[...].astype(F32)).astype(BF16)
    _, _, position = row_places(rows, length_ref, group_ref, offset_ref)
    lane = iota((rows, dim), 1)
    step = jnp.where(lane >= half, lane - half, lane).astype(F32)
    angle = position.astype(F32) * jnp.exp(step * (-math.log(10000.0) / half))
    cosine = jnp.cos(angle)
    sine = jnp.sin(angle)
    sine = jnp.where(lane < half, -sine, sine)
    own = dot(normed, kvw_ref[0])
    keyed = member_ref[0] % 2 == 0
    turned = own * cosine + pltpu.roll(own, half, 1) * sine
    own_ref[...] = jnp.where(keyed, turned, own).astype(BF16)
    q = dot(normed, qw_ref[...])
    for h in range(heads):
        part = q[:, h * dim : (h + 1) * dim]
        q_ref[h * rows : (h + 1) * rows, :] = (part * cosine + pltpu.roll(part, half, 1) * sine).astype(BF16)


def cached_body(
    member_ref, length_ref, group_ref, offset_ref, sink_ref, q_ref, mine_ref, theirs_ref,
    routes_ref, weight_ref, slot_ref, sums_ref, tops_ref, parts_ref, extra_ref,
):
    rows = routes_ref.shape[0]
    dim = q_ref.shape[1]
    heads = q_ref.shape[0] // rows
    slots = mine_ref.shape[0]
    scale = 1.0 / dim**0.5
    keyed = member_ref[0] % 2 == 0
    mine, theirs = mine_ref[...], theirs_ref[...]
    keys = jnp.where(keyed, mine, theirs)
    values = jnp.where(keyed, theirs, mine)
    group, row_length, position = row_places(rows, length_ref, group_ref, offset_ref)
    lane = iota((rows, LANES), 1)
    seen = []
    for start in range(0, slots, LANES):
        place = lane + start % PROMPT_CAP
        seen.append((group == start // PROMPT_CAP) & (place < row_length) & (place > position - WINDOW))
    scores = dot_t(q_ref[...], keys)
    probs = []
    for h in range(heads):
        span = slice(h * rows, (h + 1) * rows)
        masked = [
            jnp.where(seen[k], scores[span, k * LANES : (k + 1) * LANES] * scale, HIDE) for k in range(len(seen))
        ]
        top = functools.reduce(jnp.maximum, masked)
        top = jnp.maximum(jnp.max(top, axis=1, keepdims=True), sink_ref[h])
        part = [jnp.exp(m - top) for m in masked]
        total = jnp.sum(functools.reduce(jnp.add, part), axis=1, keepdims=True) + jnp.exp(sink_ref[h] - top)
        probs.append(jnp.concatenate([p.astype(BF16) for p in part], axis=1))
        tops_ref[span, :] = jnp.broadcast_to(top, (rows, LANES))
        parts_ref[span, :] = jnp.broadcast_to(total, (rows, LANES))
    sums_ref[...] = dot(jnp.concatenate(probs, axis=0), values)
    copies = slot_ref.shape[1]
    replicas = copies // EXPERTS
    block = iota((rows, copies), 0) // (rows // replicas)
    place = iota((rows, copies), 1)
    chosen = jnp.zeros((rows, copies), F32)
    for k in range(TOP):
        named = routes_ref[:, k : k + 1] * replicas + block
        chosen = chosen + jnp.where(named == place, weight_ref[:, k : k + 1], 0.0)
    order = (iota((copies, copies), 0) == slot_ref[...]).astype(F32).astype(BF16)
    high = chosen.astype(BF16)
    low = (chosen - high.astype(F32)).astype(BF16)
    packed = [dot_t(high, order), dot_t(low, order)]
    spare = extra_ref.shape[1] - 2 * copies
    extra_ref[...] = jnp.concatenate(packed + [jnp.zeros((rows, spare), F32)], axis=1)


def attend_body(
    member_ref, q_ref, mine_ref, theirs_ref, sums_ref, tops_ref, parts_ref, out_ref, tok_ref, extra_ref,
    send_ref, keep_ref,
):
    rows, width = tok_ref.shape
    dim = q_ref.shape[1]
    heads = q_ref.shape[0] // rows
    quarter = width // 4
    scale = 1.0 / dim**0.5
    member = member_ref[0]
    keyed = member % 2 == 0
    mine, theirs = mine_ref[...].astype(F32), theirs_ref[...].astype(F32)
    key = jnp.where(keyed, mine, theirs)
    value = jnp.where(keyed, theirs, mine)
    context = []
    for h in range(heads):
        span = slice(h * rows, (h + 1) * rows)
        score = jnp.sum(q_ref[span, :].astype(F32) * key, axis=1, keepdims=True) * scale
        top = jnp.maximum(tops_ref[span, :], score)
        old = jnp.exp(tops_ref[span, :] - top)
        own = jnp.exp(score - top)
        inverse = 1.0 / (parts_ref[span, :] * old + own)
        context.append(((sums_ref[span, :] * old + own * value) * inverse).astype(BF16))
    attended = dot(jnp.concatenate(context, axis=1), out_ref[...])
    part = [attended[:, i * quarter : (i + 1) * quarter] for i in range(4)]
    token = [tok_ref[:, i * quarter : (i + 1) * quarter].astype(F32) for i in range(4)]
    first = member < 2
    for i in range(2):
        span = slice(i * quarter, (i + 1) * quarter)
        send_ref[:, span] = jnp.where(keyed, part[2 * i + 1], part[2 * i]).astype(BF16)
        kept = jnp.where(keyed, part[2 * i], part[2 * i + 1])
        added = jnp.where(keyed, token[2 * i], token[2 * i + 1])
        keep_ref[:, span] = kept + jnp.where(first, added, 0.0)
    keep_ref[:, 2 * quarter :] = jnp.where(first, extra_ref[...], 0.0)


def chip_body(keep_ref, got_ref, out_ref):
    width = got_ref.shape[1]
    out_ref[:, :width] = (keep_ref[:, :width] + got_ref[...].astype(F32)).astype(BF16)
    out_ref[:, width:] = keep_ref[:, width:].astype(BF16)


def residual_body(copies, member_ref, gain_ref, own_ref, x_ref, y_ref, xy_ref, rows_ref, keep_ref):
    rows, total = own_ref.shape
    quarter = keep_ref.shape[1]
    width = 2 * quarter
    keyed = member_ref[0] % 2 == 0
    gain = [gain_ref[:, i * quarter : (i + 1) * quarter] for i in range(4)]
    gain = [jnp.where(keyed, gain[2 * i], gain[2 * i + 1]).astype(F32) for i in range(2)]
    lane = iota((rows, total - width), 1)
    for i, (a_ref, b_ref) in enumerate(((own_ref, x_ref), (y_ref, xy_ref))):
        span = slice(i * rows, (i + 1) * rows)
        parts = []
        squares = jnp.zeros((rows, 1), F32)
        for k in range(2):
            cols = slice(k * quarter, (k + 1) * quarter)
            part = (a_ref[:, cols].astype(F32) + b_ref[:, cols].astype(F32)).astype(BF16)
            wide = part.astype(F32)
            squares = squares + jnp.sum(wide * wide, axis=1, keepdims=True)
            rows_ref[span, cols] = (wide * gain[k]).astype(BF16)
            parts.append(part)
        extra = a_ref[:, width:].astype(F32) + b_ref[:, width:].astype(F32)
        high = squares.astype(BF16).astype(F32)
        extra = jnp.where(lane == 2 * copies, high, extra)
        extra = jnp.where(lane == 2 * copies + 1, squares - high, extra)
        rows_ref[span, width:] = extra.astype(BF16)
        if i == 0:
            keep_ref[...] = jnp.where(member_ref[0] < 2, parts[0], parts[1])


def expert_body(copies, blocks, member_ref, *refs):
    own_refs, other_refs = refs[:blocks], refs[blocks : 2 * blocks]
    gate_ref, up_ref, down_ref, hidden_ref, send_ref = refs[2 * blocks :]
    hosted, width, units = gate_ref.shape
    quarter = width // 4
    keyed = member_ref[0] % 2 == 0
    own = jnp.concatenate([r[...] for r in own_refs], axis=0)
    other = jnp.concatenate([r[...] for r in other_refs], axis=0)
    parts = []
    for i in range(4):
        span = slice(i // 2 * quarter, (i // 2 + 1) * quarter)
        mine = keyed if i % 2 == 0 else jnp.logical_not(keyed)
        parts.append(jnp.where(mine, own[:, span], other[:, span]))
    rows = jnp.concatenate(parts, axis=1)
    extra = own[:, 2 * quarter :].astype(F32)
    lane = iota(extra.shape, 1)
    squares = jnp.where((lane == 2 * copies) | (lane == 2 * copies + 1), extra + other[:, 2 * quarter :].astype(F32), 0.0)
    scale = lax.rsqrt(jnp.sum(squares, axis=1, keepdims=True) / width + EPSILON)
    tall = rows.shape[0] // blocks
    for j in range(hosted):
        slot = member_ref[1] * hosted + j
        weight = jnp.where((lane == slot) | (lane == slot + copies), extra, 0.0)
        weight = jnp.sum(weight, axis=1, keepdims=True)
        gate = dot(rows, gate_ref[j]) * scale
        up = dot(rows, up_ref[j]) * scale
        hidden = (jnp.maximum(gate, 0.0) * up * weight).astype(BF16)
        for b in range(blocks):
            hidden_ref[j, b] = hidden[b * tall : (b + 1) * tall]
    for k in range(2):
        start = pl.multiple_of((2 * k + 1 - member_ref[0] % 2) * quarter, LANES)
        total = None
        for j in range(hosted):
            hidden = jnp.concatenate([hidden_ref[j, b] for b in range(blocks)], axis=0)
            part = dot(hidden, down_ref[j, :, pl.ds(start, quarter)])
            total = part if total is None else total + part
        total = total.astype(BF16)
        for b in range(blocks):
            send_ref[b, :, k * quarter : (k + 1) * quarter] = total[b * tall : (b + 1) * tall]


def keep_body(blocks, member_ref, hidden_ref, down_ref, out_ref):
    hosted = down_ref.shape[0]
    quarter = down_ref.shape[2] // 4
    tall = hidden_ref.shape[2]
    for k in range(2):
        start = pl.multiple_of((2 * k + member_ref[0] % 2) * quarter, LANES)
        total = None
        for j in range(hosted):
            hidden = jnp.concatenate([hidden_ref[j, b] for b in range(blocks)], axis=0)
            part = dot(hidden, down_ref[j, :, pl.ds(start, quarter)])
            total = part if total is None else total + part
        for b in range(blocks):
            out_ref[b, :, k * quarter : (k + 1) * quarter] = total[b * tall : (b + 1) * tall]


def split_body(member_ref, keep_ref, got_ref, own_ref, x_ref, y_ref, xy_ref):
    rows, quarter = own_ref.shape[1:]
    first = member_ref[0] < 2
    near = keep_ref[:, :, :quarter] + got_ref[:, :, :quarter].astype(F32)
    far = keep_ref[:, :, quarter:] + got_ref[:, :, quarter:].astype(F32)
    mine = jnp.where(first, near, far)
    theirs = jnp.where(first, far, near)
    own_ref[...] = mine[:, :rows]
    x_ref[...] = theirs[:, :rows].astype(BF16)
    y_ref[...] = mine[:, rows:].astype(BF16)
    xy_ref[...] = theirs[:, rows:].astype(BF16)


def pass_body(terms, *refs):
    total = refs[0][...]
    for r in refs[1:terms]:
        total = total + r[...].astype(F32)
    outs = refs[terms:]
    tall = total.shape[0] // len(outs)
    for i, r in enumerate(outs):
        r[...] = total[i * tall : (i + 1) * tall].astype(r.dtype)


def combine_body(terms, *refs):
    residual_ref, combined_ref, square_ref = refs[terms:]
    total = refs[0][0]
    for r in refs[1:terms]:
        total = total + r[0].astype(F32)
    total = residual_ref[...].astype(F32) + total
    combined_ref[...] = total
    square_ref[...] = jnp.broadcast_to(jnp.sum(total * total, axis=1, keepdims=True), square_ref.shape)


def finish_body(width, combined_ref, gain_ref, a_ref, b_ref, c_ref, d_ref, out_ref):
    mean = (a_ref[...] + b_ref[...] + c_ref[...] + d_ref[...])[:, :1] / width
    out_ref[...] = (combined_ref[...] * lax.rsqrt(mean + EPSILON) * gain_ref[...].astype(F32)).astype(BF16)


def expert_calls(member, own, other, gate_weight, up_weight, down_weight, copies):
    blocks = len(own)
    tall, total = own[0].shape
    hosted, width, units = gate_weight.shape
    step = min(tall, 64)
    grid = (tall // step,)
    smem = pl.BlockSpec(memory_space=pltpu.SMEM)
    row_spec = pl.BlockSpec((step, total), lambda i: (i, 0))
    half_spec = pl.BlockSpec((blocks, step, width // 2), lambda i: (0, i, 0))
    hidden_spec = pl.BlockSpec((hosted, blocks, step, units), lambda i: (0, 0, i, 0))
    whole = pl.BlockSpec(memory_space=pltpu.VMEM)
    params = pltpu.CompilerParams(vmem_limit_bytes=40 << 20)
    flops = 2 * blocks * tall * hosted * width * units
    hidden, send = pl.pallas_call(
        functools.partial(expert_body, copies, blocks),
        grid=grid,
        out_shape=[shape((hosted, blocks, tall, units), BF16), shape((blocks, tall, width // 2), BF16)],
        in_specs=[smem] + [row_spec] * (2 * blocks) + [whole] * 3,
        out_specs=[hidden_spec, half_spec],
        compiler_params=params,
        cost_estimate=pl.CostEstimate(flops=5 * flops // 2, bytes_accessed=8 << 20, transcendentals=0),
        name="experts",
    )(member, *own, *other, gate_weight, up_weight, down_weight)
    got = swap(send, "tensor", 1)
    keep = pl.pallas_call(
        functools.partial(keep_body, blocks),
        grid=grid,
        out_shape=shape((blocks, tall, width // 2), F32),
        in_specs=[smem, hidden_spec, whole],
        out_specs=half_spec,
        compiler_params=params,
        cost_estimate=pl.CostEstimate(flops=flops // 2, bytes_accessed=4 << 20, transcendentals=0),
        name="experts_own_half",
    )(member, hidden, down_weight)
    return keep, got


def on_device(
    tokens, attn_gain, query_weight, key_value_weight, paired_cache, prompt_length, group_index, offsets,
    sink_logit, out_weight, mixer_gain, routes, route_weight, copy_slot, gate_weight, up_weight, down_weight,
    final_gain,
):
    rows, width = tokens.shape
    dim = key_value_weight.shape[2]
    heads = query_weight.shape[1] // dim
    half, quarter = width // 2, width // 4
    copies = copy_slot.shape[0]
    peers = lax.axis_size("expert")
    extra_width = -(-(2 * copies + 2) // LANES) * LANES
    member = jnp.stack([lax.axis_index("tensor"), lax.axis_index("expert")]).astype(I32)
    places = (prompt_length, group_index, offsets)

    own_cache = paired_cache[0, 0]
    other_cache = swap(own_cache, "tensor", 1)
    queries, own_new = call(
        project_body,
        [shape((heads * rows, dim), BF16), shape((rows, dim), BF16)],
        (member, *places, tokens, attn_gain[None, :], query_weight, key_value_weight),
        smem=range(4),
        name="project",
        cost=(2 * rows * width * (heads + 1) * dim, 2 << 20),
    )
    other_new = swap(own_new, "tensor", 1)
    sums, tops, parts, extra = call(
        cached_body,
        [shape((heads * rows, dim), F32)] + [shape((heads * rows, LANES), F32)] * 2 + [shape((rows, extra_width), F32)],
        (member, *places, sink_logit, queries, own_cache, other_cache, routes, route_weight, copy_slot[None, :]),
        smem=range(5),
        name="cached_attention",
        cost=(4 * heads * rows * dim * own_cache.shape[0], 1 << 20),
    )
    send, keep = call(
        attend_body,
        [shape((rows, half), BF16), shape((rows, half + extra_width), F32)],
        (member, queries, own_new, other_new, sums, tops, parts, out_weight, tokens, extra),
        smem=range(1),
        name="attention_out",
        cost=(2 * rows * heads * dim * width, 2 << 20),
    )
    own = call(
        chip_body, shape((rows, half + extra_width), BF16), (keep, swap(send, "tensor", 1)), name="chip_sum",
        cost=(rows * width, 1 << 18),
    )
    block, residual = call(
        functools.partial(residual_body, copies),
        [shape((2 * rows, half + extra_width), BF16), shape((rows, quarter), BF16)],
        (member, mixer_gain[None, :], own, swap(own, "tensor", 2), swap(own, "expert", 1), swap_both(own, 1, 2)),
        smem=range(1),
        name="residual",
        cost=(rows * width, 1 << 18),
    )

    bit, stages = 2, []
    while bit < peers:
        stages.append([bit] if 2 * bit >= peers else [bit, 2 * bit, 3 * bit])
        bit *= 4
    blocks = [block]
    for stage in stages:
        whole = blocks[0] if len(blocks) == 1 else jnp.concatenate(blocks, axis=0)
        blocks = [whole] + [swap(whole, "expert", b) for b in stage]
    others = [swap(b, "tensor", 1) for b in blocks]
    keep, got = expert_calls(member, blocks, others, gate_weight, up_weight, down_weight, copies)

    groups = peers // 2
    piece = (groups, rows, quarter)
    own, x_part, y_part, xy_part = call(
        split_body,
        [shape(piece, F32)] + [shape(piece, BF16)] * 3,
        (member, keep.reshape(groups, 2 * rows, half), got.reshape(groups, 2 * rows, half)),
        smem=range(1),
        vmem=48 << 20,
        name="split",
        cost=(groups * rows * width, 2 << 20),
    )
    terms = [own, swap(x_part, "tensor", 2), swap(y_part, "expert", 1), swap_both(xy_part, 1, 2)]
    for stage in stages[::-1]:
        count = len(stage) + 1
        groups //= count
        piece = (groups, rows, quarter)
        pieces = call(
            functools.partial(pass_body, len(terms)),
            [shape(piece, F32)] + [shape(piece, BF16)] * len(stage),
            terms,
            vmem=48 << 20,
            name="pass_on",
            cost=(groups * rows * width, 1 << 20),
        )
        terms = [pieces[0]] + [swap(p, "expert", b) for p, b in zip(pieces[1:], stage)]
    combined, squares = call(
        functools.partial(combine_body, len(terms)),
        [shape((rows, quarter), F32), shape((rows, LANES), F32)],
        (*terms, residual),
        name="combine",
        cost=(rows * width, 1 << 18),
    )
    return call(
        functools.partial(finish_body, width),
        shape((rows, quarter), BF16),
        (combined, final_gain[None, :], squares, *[swap(squares, "tensor", b) for b in (1, 2, 3)]),
        name="finish",
        cost=(rows * width, 1 << 18),
    )


def solution(mesh):
    in_specs = (
        P("expert", None),
        P(),
        P(None, "tensor"),
        P("tensor", None, None),
        P("expert", "tensor", None, None),
        P("expert", None),
        P("expert"),
        P("expert"),
        P("tensor"),
        P("tensor", None),
        P(),
        P("expert", None),
        P("expert", None),
        P(),
        P("expert", None, "tensor"),
        P("expert", None, "tensor"),
        P("expert", "tensor", None),
        P("tensor"),
    )
    out_specs = P("expert", "tensor")
    return jax.shard_map(
        on_device, mesh=mesh, in_specs=in_specs, out_specs=out_specs, check_vma=False
    )
```

time: 150 us -> 79.7 us (0.53)
  waiting for transfers between devices: 63.7 us -> 24.8 us
  blocking collectives: 30.6 us -> 0 us
  starting transfers between devices: 6.14 us -> 20.4 us
  between operations: 13.7 us -> 0.17 us
  matrix products: 12.2 us -> 0 us
  Pallas kernels: 0 us -> 10.1 us
  local copies, waits for them, and re-layouts: 15.9 us -> 23.5 us
  other arithmetic: 6.95 us -> 0.07 us
    psum x1 -> x0, waiting for transfers between devices: 34 us -> none  [on_device(): lax.psum(attended.astype(jnp.bfloat16), 'tensor').astype(jnp.float32)]
    ppermute x2 -> x23, waiting for transfers between devices: 0.01 us -> 24.8 us  [the longest x21 22.4 us: swap(): return lax.ppermute(block, axis, [(i, i ^ bits) for i in range(count)])]
    all_to_all x1 -> x0, blocking collectives: 24.6 us -> none  [on_device(): lax.all_to_all(outbox.reshape(peers, hosted * capacity, features), 'exper...]
    unnamed x3 -> x0, waiting for transfers between devices: 21.8 us -> none
    ppermute x2 -> x23, starting transfers between devices: 0.54 us -> 20.4 us  [the longest x21 18.1 us: swap(): return lax.ppermute(block, axis, [(i, i ^ bits) for i in range(count)])]
    unnamed x24 -> x40, local copies, waits for them, and re-layouts: 9.35 us -> 22.8 us
    dot_general x7 -> x0, matrix products: 12.2 us -> none  [the longest x1 3.86 us: on_device(): jnp.einsum('hrf,hfd->hrd', hidden, down_weight, preferred_element_type=jn...]
    pallas_call x0 -> x11, Pallas kernels: none -> 10.1 us  [the longest x9 5.31 us: call(): pl.pallas_call(body, out_shape=listed, in_specs=in_specs, out_specs=out_s...]
  transfers between devices with their start and end apart: 5 -> 23, of which waited for: 3 -> 13; matrix products, arithmetic and copies ran while one was open for 3% -> 12% of each run, Pallas kernels for 0% -> 4%
where the time goes in v1:
time: 79.7 us; the launch traced here: 79 us
  waiting for transfers between devices  24.8 us (31%)
  local copies, waits for them, and re-layouts  23.5 us (29%)
  starting transfers between devices  20.4 us (26%)
  Pallas kernels  10.1 us (13%)
    unnamed x40, local copies, waits for them, and re-layouts  22.8 us
    ppermute x21, waiting for transfers between devices, swap(): return lax.ppermute(block, axis, [(i, i ^ bits) for i in range(count)])  22.4 us
    ppermute x21, starting transfers between devices, swap(): return lax.ppermute(block, axis, [(i, i ^ bits) for i in range(count)])  18.1 us
    pallas_call x9, Pallas kernels, call(): pl.pallas_call(body, out_shape=listed, in_specs=in_specs, out_specs=out_s...  5.31 us
    pallas_call x1, Pallas kernels, expert_calls(): pl.pallas_call(functools.partial(expert_body, copies, blocks), grid=grid,...  3.52 us
    ppermute x2, waiting for transfers between devices, swap_both(): lax.ppermute(block, ('expert', 'tensor'), [(i, i ^ bits) for i in range(c...  2.42 us
    ppermute x2, starting transfers between devices, swap_both(): lax.ppermute(block, ('expert', 'tensor'), [(i, i ^ bits) for i in range(c...  2.32 us
  transfers between devices with their start and end apart: 23, of which 13 were waited for; matrix products, arithmetic and copies ran while one was open for 12% of the time, Pallas kernels for 4%

profile of v1, /device:TPU:0, one launch (start us, length us, event | category | flops | bytes accessed | tf_op | source)
XLA Modules:
  0.0 79.0 jit_solution(2798667311322455638)
XLA Ops:
  1.2 1.3 %copy-done.2 = bf16[1536,384]{1,0:T(8,128)(2,1)S(1)} copy-done((bf16[1536,384]{1,0:T(8,128)(2,1)S(1)}, bf16[1536,384]{1,0:T(8,128)(2,1)}, u32[]{:S(2)}) %copy-start.2) | copy-done | bytes 1179672
  17.7 2.9 %collective-permute-start.3 = (bf16[32,896]{1,0:T(8,128)(2,1)S(1)}, bf16[32,896]{1,0:T(8,128)(2,1)S(1)}, u32[]{:S(2)}, u32[]{:S(2)}) collective-permute-start(bf16[32,896]{1,0:T(8,128)(2,1)S(1)} %chip_sum.1.own_ref), channel_id=1, source_target_pairs={{0,2},{1,3},{2,0},{3,1},{4,6},{5,7},{6,4},{7,5},{8,10},{9,11},{10,... | collective-permute-start | bytes 172040 | tf_op jit(solution)/shard_map/ppermute | solution.py:25
  20.6 1.5 %collective-permute-start.4 = (bf16[32,896]{1,0:T(8,128)(2,1)S(1)}, bf16[32,896]{1,0:T(8,128)(2,1)S(1)}, u32[]{:S(2)}, u32[]{:S(2)}) collective-permute-start(bf16[32,896]{1,0:T(8,128)(2,1)S(1)} %chip_sum.1.own_ref), channel_id=1, source_target_pairs={{0,4},{4,0},{8,12},{12,8},{16,20},{20,16},{24,28},{28,24},{1,5},{5... | collective-permute-start | bytes 172040 | tf_op jit(solution)/shard_map/ppermute | solution.py:25
  22.9 1.9 %collective-permute-done.4.y_ref = bf16[32,896]{1,0:T(8,128)(2,1)S(1)} collective-permute-done((bf16[32,896]{1,0:T(8,128)(2,1)S(1)}, bf16[32,896]{1,0:T(8,128)(2,1)S(1)}, u32[]{:S(2)}, u32[]{:S(2)}) %collective-permute-start.4) | collective-permute-done | bytes 57376 | tf_op jit(solution)/shard_map/ppermute | solution.py:25
  24.8 2.4 %collective-permute-done.5.xy_ref = bf16[32,896]{1,0:T(8,128)(2,1)S(1)} collective-permute-done((bf16[32,896]{1,0:T(8,128)(2,1)S(1)}, bf16[32,896]{1,0:T(8,128)(2,1)S(1)}, u32[]{:S(2)}, u32[]{:S(2)}) %collective-permute-start.5) | collective-permute-done | bytes 57376 | tf_op jit(solution)/shard_map/ppermute | solution.py:32
  27.9 1.6 %collective-permute-start.6 = (bf16[64,896]{1,0:T(8,128)(2,1)S(1)}, bf16[64,896]{1,0:T(8,128)(2,1)S(1)}, u32[]{:S(2)}, u32[]{:S(2)}) collective-permute-start(bf16[64,896]{1,0:T(8,128)(2,1)S(1)} %get-tuple-element.35.refs_0_), channel_id=1, source_target_pairs={{0,8},{4,12},{8,0},{12,4},{16,24},{20,28},{24,16},{28,20},{1,9},{5... | collective-permute-start | bytes 344072 | tf_op jit(solution)/shard_map/ppermute | solution.py:25
  29.5 2.6 %collective-permute-start.7 = (bf16[64,896]{1,0:T(8,128)(2,1)S(1)}, bf16[64,896]{1,0:T(8,128)(2,1)S(1)}, u32[]{:S(2)}, u32[]{:S(2)}) collective-permute-start(bf16[64,896]{1,0:T(8,128)(2,1)S(1)} %get-tuple-element.35.refs_0_), channel_id=1, source_target_pairs={{0,16},{4,20},{8,24},{12,28},{16,0},{20,4},{24,8},{28,12},{1,17},{... | collective-permute-start | bytes 344072 | tf_op jit(solution)/shard_map/ppermute | solution.py:25
  33.6 6.2 %collective-permute-done.7.refs_2_ = bf16[64,896]{1,0:T(8,128)(2,1)S(1)} collective-permute-done((bf16[64,896]{1,0:T(8,128)(2,1)S(1)}, bf16[64,896]{1,0:T(8,128)(2,1)S(1)}, u32[]{:S(2)}, u32[]{:S(2)}) %collective-permute-start.7) | collective-permute-done | bytes 114720 | tf_op jit(solution)/shard_map/ppermute | solution.py:25
  40.3 3.0 %copy.21.refs_8_ = bf16[4,1536,192]{2,1,0:T(8,128)(2,1)S(1)} copy(bf16[4,1536,192]{1,2,0:T(8,128)(2,1)} %param.32) | data formatting | bytes 4718592 | tf_op args[14]
  43.3 4.5 %copy.22.refs_9_ = bf16[4,1536,192]{2,1,0:T(8,128)(2,1)} copy(bf16[4,1536,192]{1,2,0:T(8,128)(2,1)} %param.33) | data formatting | bytes 4718592 | tf_op args[15]
  47.9 1.9 %copy-done = bf16[4,1536,192]{2,1,0:T(8,128)(2,1)S(1)} copy-done((bf16[4,1536,192]{2,1,0:T(8,128)(2,1)S(1)}, bf16[4,1536,192]{2,1,0:T(8,128)(2,1)}, u32[]{:S(2)}) %copy-start) | copy-done | bytes 2359320
  49.8 1.7 %copy-done.1 = bf16[4,192,1536]{2,1,0:T(8,128)(2,1)S(1)} copy-done((bf16[4,192,1536]{2,1,0:T(8,128)(2,1)S(1)}, bf16[4,192,1536]{2,1,0:T(8,128)(2,1)}, u32[]{:S(2)}) %copy-start.1) | copy-done | bytes 2359320
  51.4 3.5 %experts.1 = (bf16[4,4,64,192]{3,2,1,0:T(8,128)(2,1)S(1)}, bf16[4,64,768]{2,1,0:T(8,128)(2,1)S(1)}) custom-call(s32[2]{0:T(128)S(1)} %pad_add_fusion.member_ref, bf16[64,896]{1,0:T(8,128)(2,1)S(1)} %get-tuple-element.35.refs_0_, bf16[64,896]{1,0:T(8,128)(2,1)S(1)} %collective-permute-done.6.refs_1_, bf16[64,896]{1,0:T(8,128)(2,1)S(1)} %collective-permute-done.7.refs_2_, ...), custom_call_target="tpu_custom_call" | custom-call | flops 1509949440 | bytes 8388608 | tf_op jit(solution)/shard_map/experts/pallas_call | solution.py:339
  55.0 1.2 %experts_own_half.1.keep_ref = f32[4,64,768]{2,1,0:T(8,128)S(1)} custom-call(s32[2]{0:T(128)S(1)} %pad_add_fusion.member_ref, bf16[4,4,64,192]{3,2,1,0:T(8,128)(2,1)S(1)} %get-tuple-element.36.hidden_ref, bf16[4,192,1536]{2,1,0:T(8,128)(2,1)S(1)} %copy-done.1), custom_call_target="tpu_custom_call" | custom-call | flops 301989888 | bytes 4194304 | tf_op jit(solution)/shard_map/experts_own_half/pallas_call | solution.py:350
  58.6 2.3 %collective-permute-start.16 = (bf16[4,32,384]{2,1,0:T(8,128)(2,1)S(1)}, bf16[4,32,384]{2,1,0:T(8,128)(2,1)S(1)}, u32[]{:S(2)}, u32[]{:S(2)}) collective-permute-start(bf16[4,32,384]{2,1,0:T(8,128)(2,1)S(1)} %get-tuple-element.41), channel_id=1, source_target_pairs={{0,6},{1,7},{2,4},{3,5},{4,2},{5,3},{6,0},{7,1},{8,14},{9,15},{10,... | collective-permute-start | bytes 294920 | tf_op jit(solution)/shard_map/ppermute | solution.py:32
  60.9 2.1 %collective-permute-done.14.refs_1_ = bf16[4,32,384]{2,1,0:T(8,128)(2,1)S(1)} collective-permute-done((bf16[4,32,384]{2,1,0:T(8,128)(2,1)S(1)}, bf16[4,32,384]{2,1,0:T(8,128)(2,1)S(1)}, u32[]{:S(2)}, u32[]{:S(2)}) %collective-permute-start.14) | collective-permute-done | bytes 98336 | tf_op jit(solution)/shard_map/ppermute | solution.py:25
  63.0 1.7 %collective-permute-done.15.refs_2_ = bf16[4,32,384]{2,1,0:T(8,128)(2,1)S(1)} collective-permute-done((bf16[4,32,384]{2,1,0:T(8,128)(2,1)S(1)}, bf16[4,32,384]{2,1,0:T(8,128)(2,1)S(1)}, u32[]{:S(2)}, u32[]{:S(2)}) %collective-permute-start.15) | collective-permute-done | bytes 98336 | tf_op jit(solution)/shard_map/ppermute | solution.py:25
  64.7 1.7 %collective-permute-start.17 = (bf16[1,32,384]{2,1,0:T(8,128)(2,1)S(1)}, bf16[1,32,384]{2,1,0:T(8,128)(2,1)S(1)}, u32[]{:S(2)}, u32[]{:S(2)}) collective-permute-start(bf16[1,32,384]{2,1,0:T(8,128)(2,1)S(1)} %get-tuple-element.43), channel_id=1, source_target_pairs={{0,8},{4,12},{8,0},{12,4},{16,24},{20,28},{24,16},{28,20},{1,9},{5... | collective-permute-start | bytes 73736 | tf_op jit(solution)/shard_map/ppermute | solution.py:25
  66.5 1.4 %collective-permute-start.18 = (bf16[1,32,384]{2,1,0:T(8,128)(2,1)S(1)}, bf16[1,32,384]{2,1,0:T(8,128)(2,1)S(1)}, u32[]{:S(2)}, u32[]{:S(2)}) collective-permute-start(bf16[1,32,384]{2,1,0:T(8,128)(2,1)S(1)} %get-tuple-element.44), channel_id=1, source_target_pairs={{0,16},{4,20},{8,24},{12,28},{16,0},{20,4},{24,8},{28,12},{1,17},{... | collective-permute-start | bytes 73736 | tf_op jit(solution)/shard_map/ppermute | solution.py:25
  67.9 1.3 %collective-permute-start.19 = (bf16[1,32,384]{2,1,0:T(8,128)(2,1)S(1)}, bf16[1,32,384]{2,1,0:T(8,128)(2,1)S(1)}, u32[]{:S(2)}, u32[]{:S(2)}) collective-permute-start(bf16[1,32,384]{2,1,0:T(8,128)(2,1)S(1)} %get-tuple-element.45), channel_id=1, source_target_pairs={{0,24},{4,28},{8,16},{12,20},{16,8},{20,12},{24,0},{28,4},{1,25},{... | collective-permute-start | bytes 73736 | tf_op jit(solution)/shard_map/ppermute | solution.py:25
  69.2 2.4 %collective-permute-done.18.refs_2_ = bf16[1,32,384]{2,1,0:T(8,128)(2,1)S(1)} collective-permute-done((bf16[1,32,384]{2,1,0:T(8,128)(2,1)S(1)}, bf16[1,32,384]{2,1,0:T(8,128)(2,1)S(1)}, u32[]{:S(2)}, u32[]{:S(2)}) %collective-permute-start.18) | collective-permute-done | bytes 24608 | tf_op jit(solution)/shard_map/ppermute | solution.py:25
  71.6 1.9 %collective-permute-done.19.refs_3_ = bf16[1,32,384]{2,1,0:T(8,128)(2,1)S(1)} collective-permute-done((bf16[1,32,384]{2,1,0:T(8,128)(2,1)S(1)}, bf16[1,32,384]{2,1,0:T(8,128)(2,1)S(1)}, u32[]{:S(2)}, u32[]{:S(2)}) %collective-permute-start.19) | collective-permute-done | bytes 24608 | tf_op jit(solution)/shard_map/ppermute | solution.py:25
  73.6 1.6 %collective-permute-start.21 = (f32[32,128]{1,0:T(8,128)S(1)}, f32[32,128]{1,0:T(8,128)S(1)}, u32[]{:S(2)}, u32[]{:S(2)}) collective-permute-start(f32[32,128]{1,0:T(8,128)S(1)} %get-tuple-element.48.a_ref), channel_id=1, source_target_pairs={{0,2},{1,3},{2,0},{3,1},{4,6},{5,7},{6,4},{7,5},{8,10},{9,11},{10,... | collective-permute-start | bytes 49160 | tf_op jit(solution)/shard_map/ppermute | solution.py:25
  75.5 1.9 %collective-permute-done.21.c_ref = f32[32,128]{1,0:T(8,128)S(1)} collective-permute-done((f32[32,128]{1,0:T(8,128)S(1)}, f32[32,128]{1,0:T(8,128)S(1)}, u32[]{:S(2)}, u32[]{:S(2)}) %collective-permute-start.21) | collective-permute-done | bytes 16416 | tf_op jit(solution)/shard_map/ppermute | solution.py:25
  (77 shorter events, 24.2 us)
Async XLA Ops:
  0.0 22.2 %copy-start.16 = (bf16[1536]{0:T(1024)(128)(2,1)S(1)}, bf16[1536]{0:T(1024)(128)(2,1)}, u32[]{:S(2)}) copy-start(bf16[1536]{0:T(1024)(128)(2,1)} %param.28) | copy-start | bytes 9220
  0.0 9.1 %collective-permute-start.1 = (bf16[768,128]{1,0:T(8,128)(2,1)}, bf16[768,128]{1,0:T(8,128)(2,1)S(1)}, u32[]{:S(2)}, u32[]{:S(2)}) collective-permute-start(bf16[768,128]{1,0:T(8,128)(2,1)} %bitcast.4), channel_id=1, source_target_pairs={{0,1},{1,0},{2,3},{3,2},{4,5},{5,4},{6,7},{7,6},{8,9},{9,8},{10,11... | collective-permute-start | bytes 589832 | tf_op jit(solution)/shard_map/ppermute | solution.py:25
  7.4 7.0 %collective-permute-start = (bf16[32,128]{1,0:T(8,128)(2,1)S(1)}, bf16[32,128]{1,0:T(8,128)(2,1)S(1)}, u32[]{:S(2)}, u32[]{:S(2)}) collective-permute-start(bf16[32,128]{1,0:T(8,128)(2,1)S(1)} %get-tuple-element.28.mine_ref), channel_id=1, source_target_pairs={{0,1},{1,0},{2,3},{3,2},{4,5},{5,4},{6,7},{7,6},{8,9},{9,8},{10,11... | collective-permute-start | bytes 24584 | tf_op jit(solution)/shard_map/ppermute | solution.py:25
  16.3 1.4 %collective-permute-start.2 = (bf16[32,768]{1,0:T(8,128)(2,1)S(1)}, bf16[32,768]{1,0:T(8,128)(2,1)S(1)}, u32[]{:S(2)}, u32[]{:S(2)}) collective-permute-start(bf16[32,768]{1,0:T(8,128)(2,1)S(1)} %get-tuple-element.34), channel_id=1, source_target_pairs={{0,1},{1,0},{2,3},{3,2},{4,5},{5,4},{6,7},{7,6},{8,9},{9,8},{10,11... | collective-permute-start | bytes 147464 | tf_op jit(solution)/shard_map/ppermute | solution.py:25
  17.7 5.1 %collective-permute-start.3 = (bf16[32,896]{1,0:T(8,128)(2,1)S(1)}, bf16[32,896]{1,0:T(8,128)(2,1)S(1)}, u32[]{:S(2)}, u32[]{:S(2)}) collective-permute-start(bf16[32,896]{1,0:T(8,128)(2,1)S(1)} %chip_sum.1.own_ref), channel_id=1, source_target_pairs={{0,2},{1,3},{2,0},{3,1},{4,6},{5,7},{6,4},{7,5},{8,10},{9,11},{10,... | collective-permute-start | bytes 172040 | tf_op jit(solution)/shard_map/ppermute | solution.py:25
  20.6 4.2 %collective-permute-start.4 = (bf16[32,896]{1,0:T(8,128)(2,1)S(1)}, bf16[32,896]{1,0:T(8,128)(2,1)S(1)}, u32[]{:S(2)}, u32[]{:S(2)}) collective-permute-start(bf16[32,896]{1,0:T(8,128)(2,1)S(1)} %chip_sum.1.own_ref), channel_id=1, source_target_pairs={{0,4},{4,0},{8,12},{12,8},{16,20},{20,16},{24,28},{28,24},{1,5},{5... | collective-permute-start | bytes 172040 | tf_op jit(solution)/shard_map/ppermute | solution.py:25
  22.1 5.1 %collective-permute-start.5 = (bf16[32,896]{1,0:T(8,128)(2,1)S(1)}, bf16[32,896]{1,0:T(8,128)(2,1)S(1)}, u32[]{:S(2)}, u32[]{:S(2)}) collective-permute-start(bf16[32,896]{1,0:T(8,128)(2,1)S(1)} %chip_sum.1.own_ref), channel_id=1, source_target_pairs={{0,6},{1,7},{2,4},{3,5},{4,2},{5,3},{6,0},{7,1},{8,14},{9,15},{10,... | collective-permute-start | bytes 172040 | tf_op jit(solution)/shard_map/ppermute | solution.py:32
  27.9 5.7 %collective-permute-start.6 = (bf16[64,896]{1,0:T(8,128)(2,1)S(1)}, bf16[64,896]{1,0:T(8,128)(2,1)S(1)}, u32[]{:S(2)}, u32[]{:S(2)}) collective-permute-start(bf16[64,896]{1,0:T(8,128)(2,1)S(1)} %get-tuple-element.35.refs_0_), channel_id=1, source_target_pairs={{0,8},{4,12},{8,0},{12,4},{16,24},{20,28},{24,16},{28,20},{1,9},{5... | collective-permute-start | bytes 344072 | tf_op jit(solution)/shard_map/ppermute | solution.py:25
  29.5 10.3 %collective-permute-start.7 = (bf16[64,896]{1,0:T(8,128)(2,1)S(1)}, bf16[64,896]{1,0:T(8,128)(2,1)S(1)}, u32[]{:S(2)}, u32[]{:S(2)}) collective-permute-start(bf16[64,896]{1,0:T(8,128)(2,1)S(1)} %get-tuple-element.35.refs_0_), channel_id=1, source_target_pairs={{0,16},{4,20},{8,24},{12,28},{16,0},{20,4},{24,8},{28,12},{1,17},{... | collective-permute-start | bytes 344072 | tf_op jit(solution)/shard_map/ppermute | solution.py:25
  32.1 7.7 %collective-permute-start.8 = (bf16[64,896]{1,0:T(8,128)(2,1)S(1)}, bf16[64,896]{1,0:T(8,128)(2,1)}, u32[]{:S(2)}, u32[]{:S(2)}) collective-permute-start(bf16[64,896]{1,0:T(8,128)(2,1)S(1)} %get-tuple-element.35.refs_0_), channel_id=1, source_target_pairs={{0,24},{4,28},{8,16},{12,20},{16,8},{20,12},{24,0},{28,4},{1,25},{... | collective-permute-start | bytes 344072 | tf_op jit(solution)/shard_map/ppermute | solution.py:25
  32.3 15.5 %collective-permute-start.9 = (bf16[64,896]{1,0:T(8,128)(2,1)S(1)}, bf16[64,896]{1,0:T(8,128)(2,1)}, u32[]{:S(2)}, u32[]{:S(2)}) collective-permute-start(bf16[64,896]{1,0:T(8,128)(2,1)S(1)} %get-tuple-element.35.refs_0_), channel_id=1, source_target_pairs={{0,1},{1,0},{2,3},{3,2},{4,5},{5,4},{6,7},{7,6},{8,9},{9,8},{10,11... | collective-permute-start | bytes 344072 | tf_op jit(solution)/shard_map/ppermute | solution.py:25
  33.6 14.3 %collective-permute-start.10 = (bf16[64,896]{1,0:T(8,128)(2,1)S(1)}, bf16[64,896]{1,0:T(8,128)(2,1)}, u32[]{:S(2)}, u32[]{:S(2)}) collective-permute-start(bf16[64,896]{1,0:T(8,128)(2,1)S(1)} %collective-permute-done.6.refs_1_), channel_id=1, source_target_pairs={{0,1},{1,0},{2,3},{3,2},{4,5},{5,4},{6,7},{7,6},{8,9},{9,8},{10,11... | collective-permute-start | bytes 344072 | tf_op jit(solution)/shard_map/ppermute | solution.py:25
  39.8 8.0 %collective-permute-start.11 = (bf16[64,896]{1,0:T(8,128)(2,1)S(1)}, bf16[64,896]{1,0:T(8,128)(2,1)}, u32[]{:S(2)}, u32[]{:S(2)}) collective-permute-start(bf16[64,896]{1,0:T(8,128)(2,1)S(1)} %collective-permute-done.7.refs_2_), channel_id=1, source_target_pairs={{0,1},{1,0},{2,3},{3,2},{4,5},{5,4},{6,7},{7,6},{8,9},{9,8},{10,11... | collective-permute-start | bytes 344072 | tf_op jit(solution)/shard_map/ppermute | solution.py:25
  39.8 8.0 %collective-permute-start.12 = (bf16[64,896]{1,0:T(8,128)(2,1)}, bf16[64,896]{1,0:T(8,128)(2,1)}, u32[]{:S(2)}, u32[]{:S(2)}) collective-permute-start(bf16[64,896]{1,0:T(8,128)(2,1)} %collective-permute-done.8.refs_3_), channel_id=1, source_target_pairs={{0,1},{1,0},{2,3},{3,2},{4,5},{5,4},{6,7},{7,6},{8,9},{9,8},{10,11... | collective-permute-start | bytes 344072 | tf_op jit(solution)/shard_map/ppermute | solution.py:25
  54.9 1.8 %collective-permute-start.13 = (bf16[4,64,768]{2,1,0:T(8,128)(2,1)S(1)}, bf16[4,64,768]{2,1,0:T(8,128)(2,1)S(1)}, u32[]{:S(2)}, u32[]{:S(2)}) collective-permute-start(bf16[4,64,768]{2,1,0:T(8,128)(2,1)S(1)} %get-tuple-element.37), channel_id=1, source_target_pairs={{0,1},{1,0},{2,3},{3,2},{4,5},{5,4},{6,7},{7,6},{8,9},{9,8},{10,11... | collective-permute-start | bytes 1179656 | tf_op jit(solution)/shard_map/ppermute | solution.py:25
  57.4 5.6 %collective-permute-start.14 = (bf16[4,32,384]{2,1,0:T(8,128)(2,1)S(1)}, bf16[4,32,384]{2,1,0:T(8,128)(2,1)S(1)}, u32[]{:S(2)}, u32[]{:S(2)}) collective-permute-start(bf16[4,32,384]{2,1,0:T(8,128)(2,1)S(1)} %get-tuple-element.39), channel_id=1, source_target_pairs={{0,2},{1,3},{2,0},{3,1},{4,6},{5,7},{6,4},{7,5},{8,10},{9,11},{10,... | collective-permute-start | bytes 294920 | tf_op jit(solution)/shard_map/ppermute | solution.py:25
  58.0 6.7 %collective-permute-start.15 = (bf16[4,32,384]{2,1,0:T(8,128)(2,1)S(1)}, bf16[4,32,384]{2,1,0:T(8,128)(2,1)S(1)}, u32[]{:S(2)}, u32[]{:S(2)}) collective-permute-start(bf16[4,32,384]{2,1,0:T(8,128)(2,1)S(1)} %get-tuple-element.40), channel_id=1, source_target_pairs={{0,4},{4,0},{8,12},{12,8},{16,20},{20,16},{24,28},{28,24},{1,5},{5... | collective-permute-start | bytes 294920 | tf_op jit(solution)/shard_map/ppermute | solution.py:25
  58.6 6.1 %collective-permute-start.16 = (bf16[4,32,384]{2,1,0:T(8,128)(2,1)S(1)}, bf16[4,32,384]{2,1,0:T(8,128)(2,1)S(1)}, u32[]{:S(2)}, u32[]{:S(2)}) collective-permute-start(bf16[4,32,384]{2,1,0:T(8,128)(2,1)S(1)} %get-tuple-element.41), channel_id=1, source_target_pairs={{0,6},{1,7},{2,4},{3,5},{4,2},{5,3},{6,0},{7,1},{8,14},{9,15},{10,... | collective-permute-start | bytes 294920 | tf_op jit(solution)/shard_map/ppermute | solution.py:32
  64.7 4.5 %collective-permute-start.17 = (bf16[1,32,384]{2,1,0:T(8,128)(2,1)S(1)}, bf16[1,32,384]{2,1,0:T(8,128)(2,1)S(1)}, u32[]{:S(2)}, u32[]{:S(2)}) collective-permute-start(bf16[1,32,384]{2,1,0:T(8,128)(2,1)S(1)} %get-tuple-element.43), channel_id=1, source_target_pairs={{0,8},{4,12},{8,0},{12,4},{16,24},{20,28},{24,16},{28,20},{1,9},{5... | collective-permute-start | bytes 73736 | tf_op jit(solution)/shard_map/ppermute | solution.py:25
  66.5 5.1 %collective-permute-start.18 = (bf16[1,32,384]{2,1,0:T(8,128)(2,1)S(1)}, bf16[1,32,384]{2,1,0:T(8,128)(2,1)S(1)}, u32[]{:S(2)}, u32[]{:S(2)}) collective-permute-start(bf16[1,32,384]{2,1,0:T(8,128)(2,1)S(1)} %get-tuple-element.44), channel_id=1, source_target_pairs={{0,16},{4,20},{8,24},{12,28},{16,0},{20,4},{24,8},{28,12},{1,17},{... | collective-permute-start | bytes 73736 | tf_op jit(solution)/shard_map/ppermute | solution.py:25
  67.9 5.6 %collective-permute-start.19 = (bf16[1,32,384]{2,1,0:T(8,128)(2,1)S(1)}, bf16[1,32,384]{2,1,0:T(8,128)(2,1)S(1)}, u32[]{:S(2)}, u32[]{:S(2)}) collective-permute-start(bf16[1,32,384]{2,1,0:T(8,128)(2,1)S(1)} %get-tuple-element.45), channel_id=1, source_target_pairs={{0,24},{4,28},{8,16},{12,20},{16,8},{20,12},{24,0},{28,4},{1,25},{... | collective-permute-start | bytes 73736 | tf_op jit(solution)/shard_map/ppermute | solution.py:25
  73.6 1.9 %collective-permute-start.20 = (f32[32,128]{1,0:T(8,128)S(1)}, f32[32,128]{1,0:T(8,128)S(1)}, u32[]{:S(2)}, u32[]{:S(2)}) collective-permute-start(f32[32,128]{1,0:T(8,128)S(1)} %get-tuple-element.48.a_ref), channel_id=1, source_target_pairs={{0,1},{1,0},{2,3},{3,2},{4,5},{5,4},{6,7},{7,6},{8,9},{9,8},{10,11... | collective-permute-start | bytes 49160 | tf_op jit(solution)/shard_map/ppermute | solution.py:25
  73.6 3.8 %collective-permute-start.21 = (f32[32,128]{1,0:T(8,128)S(1)}, f32[32,128]{1,0:T(8,128)S(1)}, u32[]{:S(2)}, u32[]{:S(2)}) collective-permute-start(f32[32,128]{1,0:T(8,128)S(1)} %get-tuple-element.48.a_ref), channel_id=1, source_target_pairs={{0,2},{1,3},{2,0},{3,1},{4,6},{5,7},{6,4},{7,5},{8,10},{9,11},{10,... | collective-permute-start | bytes 49160 | tf_op jit(solution)/shard_map/ppermute | solution.py:25
  75.2 3.2 %collective-permute-start.22 = (f32[32,128]{1,0:T(8,128)S(1)}, f32[32,128]{1,0:T(8,128)S(1)}, u32[]{:S(2)}, u32[]{:S(2)}) collective-permute-start(f32[32,128]{1,0:T(8,128)S(1)} %get-tuple-element.48.a_ref), channel_id=1, source_target_pairs={{0,3},{1,2},{2,1},{3,0},{4,7},{5,6},{6,5},{7,4},{8,11},{9,10},{10,... | collective-permute-start | bytes 49160 | tf_op jit(solution)/shard_map/ppermute | solution.py:25
  (17 other events, 42.3 us)

commit v2 on v1

v2 whole, which is shorter than its diff:
```python
import functools
import math

import jax
import jax.numpy as jnp
from jax import lax
from jax.experimental import pallas as pl
from jax.experimental.pallas import tpu as pltpu
from jax.sharding import PartitionSpec as P

EXPERTS = 32
TOP = 4
PROMPT_CAP = 256
WINDOW = 192
EPSILON = 1e-06
LANES = 128
HIDE = -1e30
F32 = jnp.float32
BF16 = jnp.bfloat16
I32 = jnp.int32


def swap(block, axis, bits):
    count = lax.axis_size(axis)
    return lax.ppermute(block, axis, [(i, i ^ bits) for i in range(count)])


def swap_both(block, expert_bits, tensor_bits):
    lanes = lax.axis_size("tensor")
    count = lax.axis_size("expert") * lanes
    bits = expert_bits * lanes + tensor_bits
    return lax.ppermute(block, ("expert", "tensor"), [(i, i ^ bits) for i in range(count)])


def iota(shape, dim):
    return lax.broadcasted_iota(I32, shape, dim)


def dot(a, b):
    return jnp.dot(a, b, preferred_element_type=F32)


def dot_t(a, b):
    return lax.dot_general(a, b, (((1,), (1,)), ((), ())), preferred_element_type=F32)


def call(body, outs, args, hbm=(), scratch=(), vmem=None, cost=None, name=None):
    in_specs = [
        pl.BlockSpec(memory_space=pltpu.HBM) if i in hbm else pl.BlockSpec(memory_space=pltpu.VMEM)
        for i in range(len(args))
    ]
    single = not isinstance(outs, (list, tuple))
    listed = [outs] if single else list(outs)
    out_specs = [pl.BlockSpec(memory_space=pltpu.VMEM) for _ in listed]
    flops, nbytes = cost or (0, 0)
    result = pl.pallas_call(
        body,
        out_shape=listed,
        in_specs=in_specs,
        out_specs=out_specs,
        scratch_shapes=list(scratch),
        compiler_params=pltpu.CompilerParams(vmem_limit_bytes=vmem or 16 << 20),
        cost_estimate=pl.CostEstimate(flops=flops, bytes_accessed=nbytes, transcendentals=0),
        name=name,
    )(*args)
    return result[0] if single else result


def shape(dims, dtype):
    return jax.ShapeDtypeStruct(tuple(dims), dtype)


def spread(rows, values):
    index = iota((rows, LANES), 0)
    total = jnp.full((rows, LANES), values[0], I32)
    for i in range(1, rows):
        total = jnp.where(index == i, values[i], total)
    return total


def is_key():
    return lax.axis_index("tensor") % 2 == 0


def is_first():
    return lax.axis_index("tensor") < 2


def project_body(
    length_hbm, group_hbm, offset_hbm, tok_hbm, gain_hbm, kvw_hbm, qw_hbm, cache_hbm,
    q_ref, own_ref, cache_ref, token_ref, group_out, length_out, position_out,
    length_ref, group_ref, offset_ref, tok_ref, gain_ref, kvw_ref, qw_ref, sems,
):
    pairs = [
        (length_hbm, length_ref), (group_hbm, group_ref), (offset_hbm, offset_ref), (tok_hbm, tok_ref),
        (gain_hbm, gain_ref), (kvw_hbm.at[0], kvw_ref), (qw_hbm, qw_ref), (cache_hbm.at[0, 0], cache_ref),
    ]
    loads = [pltpu.make_async_copy(src, dst, sems.at[i]) for i, (src, dst) in enumerate(pairs)]
    for load in loads:
        load.start()
    rows, width = tok_ref.shape
    dim = kvw_ref.shape[1]
    heads = qw_ref.shape[1] // dim
    half = dim // 2
    quarter = width // 4
    for load in loads[:3]:
        load.wait()
    groups = [group_ref[i] for i in range(rows)]
    lengths = [length_ref[0, g] for g in groups]
    group_out[...] = spread(rows, groups)
    length_out[...] = spread(rows, lengths)
    position = spread(rows, [lengths[i] + offset_ref[i] for i in range(rows)])
    position_out[...] = position
    lane = iota((rows, dim), 1)
    step = jnp.where(lane >= half, lane - half, lane).astype(F32)
    angle = position.astype(F32) * jnp.exp(step * (-math.log(10000.0) / half))
    cosine = jnp.cos(angle)
    sine = jnp.sin(angle)
    sine = jnp.where(lane < half, -sine, sine)
    loads[3].wait()
    loads[4].wait()
    tok = tok_ref[...].astype(F32)
    mean = jnp.sum(tok * tok, axis=1, keepdims=True) / width
    normed = (tok * lax.rsqrt(mean + EPSILON) * gain_ref[...].astype(F32)).astype(BF16)
    for i in range(2):
        low, high = (tok[:, (2 * i + k) * quarter : (2 * i + k + 1) * quarter] for k in range(2))
        token_ref[:, i * quarter : (i + 1) * quarter] = jnp.where(
            is_first(), jnp.where(is_key(), low, high), 0.0
        )
    loads[5].wait()
    own = dot(normed, kvw_ref[...])
    turned = own * cosine + pltpu.roll(own, half, 1) * sine
    own_ref[...] = jnp.where(is_key(), turned, own).astype(BF16)
    loads[6].wait()
    q = dot(normed, qw_ref[...])
    for h in range(heads):
        part = q[:, h * dim : (h + 1) * dim]
        q_ref[h * rows : (h + 1) * rows, :] = (part * cosine + pltpu.roll(part, half, 1) * sine).astype(BF16)
    loads[7].wait()


def cached_body(
    q_ref, mine_ref, theirs_ref, group_ref, length_ref, position_ref, sink_hbm, routes_hbm, weight_hbm, slot_hbm,
    sums_ref, tops_ref, parts_ref, extra_ref, sink_ref, routes_ref, weight_ref, slot_ref, sems,
):
    pairs = [(sink_hbm, sink_ref), (routes_hbm, routes_ref), (weight_hbm, weight_ref), (slot_hbm, slot_ref)]
    loads = [pltpu.make_async_copy(src, dst, sems.at[i]) for i, (src, dst) in enumerate(pairs)]
    for load in loads:
        load.start()
    rows = group_ref.shape[0]
    dim = q_ref.shape[1]
    heads = q_ref.shape[0] // rows
    slots = mine_ref.shape[0]
    scale = 1.0 / dim**0.5
    mine, theirs = mine_ref[...], theirs_ref[...]
    keys = jnp.where(is_key(), mine, theirs)
    values = jnp.where(is_key(), theirs, mine)
    scores = dot_t(q_ref[...], keys)
    group, row_length, position = group_ref[...], length_ref[...], position_ref[...]
    lane = iota((rows, LANES), 1)
    seen = []
    for start in range(0, slots, LANES):
        place = lane + start % PROMPT_CAP
        seen.append((group == start // PROMPT_CAP) & (place < row_length) & (place > position - WINDOW))
    for load in loads:
        load.wait()
    probs = []
    for h in range(heads):
        span = slice(h * rows, (h + 1) * rows)
        masked = [
            jnp.where(seen[k], scores[span, k * LANES : (k + 1) * LANES] * scale, HIDE) for k in range(len(seen))
        ]
        top = functools.reduce(jnp.maximum, masked)
        top = jnp.maximum(jnp.max(top, axis=1, keepdims=True), sink_ref[h])
        part = [jnp.exp(m - top) for m in masked]
        total = jnp.sum(functools.reduce(jnp.add, part), axis=1, keepdims=True) + jnp.exp(sink_ref[h] - top)
        probs.append(jnp.concatenate([p.astype(BF16) for p in part], axis=1))
        tops_ref[span, :] = jnp.broadcast_to(top, (rows, LANES))
        parts_ref[span, :] = jnp.broadcast_to(total, (rows, LANES))
    sums_ref[...] = dot(jnp.concatenate(probs, axis=0), values)
    copies = slot_ref.shape[1]
    replicas = copies // EXPERTS
    block = iota((copies, rows), 1) // (rows // replicas)
    place = iota((copies, rows), 0)
    chosen = jnp.zeros((copies, rows), F32)
    for k in range(TOP):
        named = routes_ref[k : k + 1, :] * replicas + block
        chosen = chosen + jnp.where(named == place, weight_ref[k : k + 1, :], 0.0)
    order = (iota((copies, copies), 0) == slot_ref[...]).astype(F32).astype(BF16)
    high = chosen.astype(BF16)
    low = (chosen - high.astype(F32)).astype(BF16)
    extra_ref[...] = jnp.zeros(extra_ref.shape, F32)
    for i, part in enumerate((high, low)):
        moved = lax.dot_general(part, order, (((0,), (1,)), ((), ())), preferred_element_type=F32)
        extra_ref[:, i * copies : (i + 1) * copies] = jnp.where(is_first(), moved, 0.0)


def attend_body(
    q_ref, mine_ref, theirs_ref, sums_ref, tops_ref, parts_ref, out_ref, token_ref, extra_ref, send_ref, keep_ref
):
    rows, dim = mine_ref.shape
    heads = q_ref.shape[0] // rows
    quarter = send_ref.shape[1] // 2
    scale = 1.0 / dim**0.5
    mine, theirs = mine_ref[...].astype(F32), theirs_ref[...].astype(F32)
    key = jnp.where(is_key(), mine, theirs)
    value = jnp.where(is_key(), theirs, mine)
    context = []
    for h in range(heads):
        span = slice(h * rows, (h + 1) * rows)
        score = jnp.sum(q_ref[span, :].astype(F32) * key, axis=1, keepdims=True) * scale
        top = jnp.maximum(tops_ref[span, :], score)
        old = jnp.exp(tops_ref[span, :] - top)
        own = jnp.exp(score - top)
        inverse = 1.0 / (parts_ref[span, :] * old + own)
        context.append(((sums_ref[span, :] * old + own * value) * inverse).astype(BF16))
    attended = dot(jnp.concatenate(context, axis=1), out_ref[...])
    part = [attended[:, i * quarter : (i + 1) * quarter] for i in range(4)]
    for i in range(2):
        span = slice(i * quarter, (i + 1) * quarter)
        send_ref[:, span] = jnp.where(is_key(), part[2 * i + 1], part[2 * i]).astype(BF16)
        keep_ref[:, span] = jnp.where(is_key(), part[2 * i], part[2 * i + 1]) + token_ref[:, span]
    keep_ref[:, 2 * quarter :] = extra_ref[...]


def chip_body(keep_ref, got_ref, out_ref):
    width = got_ref.shape[1]
    out_ref[:, :width] = (keep_ref[:, :width] + got_ref[...].astype(F32)).astype(BF16)
    out_ref[:, width:] = keep_ref[:, width:].astype(BF16)


def residual_body(copies, gain_ref, own_ref, x_ref, y_ref, xy_ref, rows_ref, keep_ref):
    rows, total = own_ref.shape
    width = keep_ref.shape[1]
    quarter = width // 2
    gain = [gain_ref[:, i * quarter : (i + 1) * quarter] for i in range(4)]
    gain = [jnp.where(is_key(), gain[2 * i].astype(F32), gain[2 * i + 1].astype(F32)) for i in range(2)]
    lane = iota((rows, total - width), 1)
    for i, (a_ref, b_ref) in enumerate(((own_ref, x_ref), (y_ref, xy_ref))):
        span = slice(i * rows, (i + 1) * rows)
        squares = jnp.zeros((rows, 1), F32)
        for k in range(2):
            cols = slice(k * quarter, (k + 1) * quarter)
            part = (a_ref[:, cols].astype(F32) + b_ref[:, cols].astype(F32)).astype(BF16)
            wide = part.astype(F32)
            squares = squares + jnp.sum(wide * wide, axis=1, keepdims=True)
            rows_ref[span, cols] = (wide * gain[k]).astype(BF16)
            if i == 0:
                keep_ref[:, cols] = part
        extra = a_ref[:, width:].astype(F32) + b_ref[:, width:].astype(F32)
        high = squares.astype(BF16).astype(F32)
        extra = jnp.where(lane == 2 * copies, high, extra)
        extra = jnp.where(lane == 2 * copies + 1, squares - high, extra)
        rows_ref[span, width:] = extra.astype(BF16)


def expert_body(copies, blocks, *refs):
    own_refs, other_refs = refs[:blocks], refs[blocks : 2 * blocks]
    gate_ref, up_ref, down_ref, hidden_ref, send_ref = refs[2 * blocks :]
    hosted, units, width = gate_ref.shape
    quarter = width // 4
    own = jnp.concatenate([r[...] for r in own_refs], axis=0)
    other = jnp.concatenate([r[...] for r in other_refs], axis=0)
    parts = []
    for i in range(4):
        span = slice(i // 2 * quarter, (i // 2 + 1) * quarter)
        mine = is_key() if i % 2 == 0 else jnp.logical_not(is_key())
        parts.append(jnp.where(mine, own[:, span], other[:, span]))
    rows = jnp.concatenate(parts, axis=1)
    extra = own[:, 2 * quarter :].astype(F32)
    lane = iota(extra.shape, 1)
    squares = jnp.where((lane == 2 * copies) | (lane == 2 * copies + 1), extra + other[:, 2 * quarter :].astype(F32), 0.0)
    scale = lax.rsqrt(jnp.sum(squares, axis=1, keepdims=True) / width + EPSILON)
    tall = rows.shape[0] // blocks
    hiddens = []
    for j in range(hosted):
        slot = lax.axis_index("expert") * hosted + j
        weight = jnp.where((lane == slot) | (lane == slot + copies), extra, 0.0)
        weight = jnp.sum(weight, axis=1, keepdims=True)
        gate = dot_t(rows, gate_ref[j]) * scale
        up = dot_t(rows, up_ref[j]) * scale
        hidden = (jnp.maximum(gate, 0.0) * up * weight).astype(BF16)
        hiddens.append(hidden)
        for b in range(blocks):
            hidden_ref[j, b] = hidden[b * tall : (b + 1) * tall]
    for k in range(2):
        start = pl.multiple_of((2 * k + 1 - lax.axis_index("tensor") % 2) * quarter, LANES)
        total = None
        for j in range(hosted):
            part = dot(hiddens[j], down_ref[j, :, pl.ds(start, quarter)])
            total = part if total is None else total + part
        total = total.astype(BF16)
        for b in range(blocks):
            send_ref[b, :, k * quarter : (k + 1) * quarter] = total[b * tall : (b + 1) * tall]


def keep_body(blocks, hidden_ref, down_ref, out_ref):
    hosted = down_ref.shape[0]
    quarter = down_ref.shape[2] // 4
    tall = hidden_ref.shape[2]
    hiddens = [jnp.concatenate([hidden_ref[j, b] for b in range(blocks)], axis=0) for j in range(hosted)]
    for k in range(2):
        start = pl.multiple_of((2 * k + lax.axis_index("tensor") % 2) * quarter, LANES)
        total = None
        for j in range(hosted):
            part = dot(hiddens[j], down_ref[j, :, pl.ds(start, quarter)])
            total = part if total is None else total + part
        for b in range(blocks):
            out_ref[b, :, k * quarter : (k + 1) * quarter] = total[b * tall : (b + 1) * tall]


def chips_body(keep_ref, got_ref, *out_refs):
    for b, out_ref in enumerate(out_refs):
        out_ref[...] = (keep_ref[b] + got_ref[b].astype(F32)).astype(out_ref.dtype)


def pass_body(terms, *refs):
    total = refs[0][...]
    for r in refs[1:terms]:
        total = total + r[...].astype(F32)
    outs = refs[terms:]
    tall = total.shape[0] // len(outs)
    for i, r in enumerate(outs):
        r[...] = total[i * tall : (i + 1) * tall].astype(r.dtype)


def pair_body(terms, *refs):
    total = refs[0][...]
    for r in refs[1:terms]:
        total = total + r[...].astype(F32)
    own_ref, x_ref, y_ref = refs[terms:]
    rows = own_ref.shape[0]
    own_ref[...] = total[:rows]
    x_ref[...] = total[:rows].astype(BF16)
    y_ref[...] = total[rows:].astype(BF16)


def combine_body(own_ref, x_ref, y_ref, xy_ref, residual_ref, combined_ref, square_ref):
    quarter = combined_ref.shape[1]
    total = (own_ref[...] + x_ref[...].astype(F32)) + (y_ref[...].astype(F32) + xy_ref[...].astype(F32))
    total = residual_ref[...].astype(F32) + total
    combined_ref[...] = jnp.where(is_first(), total[:, :quarter], total[:, quarter:])
    square_ref[...] = jnp.broadcast_to(jnp.sum(total * total, axis=1, keepdims=True), square_ref.shape)


def finish_body(width, combined_ref, gain_ref, a_ref, b_ref, out_ref):
    mean = (a_ref[...] + b_ref[...])[:, :1] / width
    out_ref[...] = (combined_ref[...] * lax.rsqrt(mean + EPSILON) * gain_ref[...].astype(F32)).astype(BF16)


def run_experts(own, other, gate_weight, up_weight, down_weight, copies, first):
    blocks = len(own)
    tall, total = own[0].shape
    hosted, units, width = gate_weight.shape
    step = min(tall, 64)
    grid = (tall // step,) if tall > step else ()

    def spec(dims, place):
        if not grid:
            return pl.BlockSpec(memory_space=pltpu.VMEM)
        return pl.BlockSpec(dims, place)

    row_spec = spec((step, total), lambda i: (i, 0))
    half_spec = spec((blocks, step, width // 2), lambda i: (0, i, 0))
    hidden_spec = spec((hosted, blocks, step, units), lambda i: (0, 0, i, 0))
    whole = pl.BlockSpec(memory_space=pltpu.VMEM)
    params = pltpu.CompilerParams(vmem_limit_bytes=32 << 20)
    flops = 2 * blocks * tall * hosted * width * units
    hidden, send = pl.pallas_call(
        functools.partial(expert_body, copies, blocks),
        grid=grid,
        out_shape=[shape((hosted, blocks, tall, units), BF16), shape((blocks, tall, width // 2), BF16)],
        in_specs=[row_spec] * (2 * blocks) + [whole] * 3,
        out_specs=[hidden_spec, half_spec],
        compiler_params=params,
        cost_estimate=pl.CostEstimate(flops=5 * flops // 2, bytes_accessed=8 << 20, transcendentals=0),
        name="experts",
    )(*own, *other, gate_weight, up_weight, down_weight)
    got = swap(send, "tensor", 1)
    keep = pl.pallas_call(
        functools.partial(keep_body, blocks),
        grid=grid,
        out_shape=shape((blocks, tall, width // 2), F32),
        in_specs=[hidden_spec, whole],
        out_specs=half_spec,
        compiler_params=params,
        cost_estimate=pl.CostEstimate(flops=flops // 2, bytes_accessed=3 << 20, transcendentals=0),
        name="experts_own_half",
    )(hidden, down_weight)
    sums = call(
        chips_body,
        [shape((tall, width // 2), F32 if first and b == 0 else BF16) for b in range(blocks)],
        (keep, got),
        vmem=48 << 20,
        name="chip_sums",
        cost=(blocks * tall * width, 1 << 20),
    )
    return list(sums)


def on_device(
    tokens, attn_gain, query_weight, key_value_weight, paired_cache, prompt_length, group_index, offsets,
    sink_logit, out_weight, mixer_gain, routes, route_weight, copy_slot, gate_weight, up_weight, down_weight,
    final_gain,
):
    rows, width = tokens.shape
    dim = key_value_weight.shape[2]
    heads = query_weight.shape[1] // dim
    half, quarter = width // 2, width // 4
    slots = paired_cache.shape[2]
    copies = copy_slot.shape[0]
    peers = lax.axis_size("expert")
    extra_width = -(-(2 * copies + 2) // LANES) * LANES
    gate_weight = jnp.swapaxes(gate_weight, 1, 2)
    up_weight = jnp.swapaxes(up_weight, 1, 2)

    other_cache = swap(paired_cache[0, 0], "tensor", 1)
    place = shape((rows, LANES), I32)
    queries, own_new, own_cache, token_half, *places = call(
        project_body,
        [
            shape((heads * rows, dim), BF16), shape((rows, dim), BF16), shape((slots, dim), BF16),
            shape((rows, half), F32), place, place, place,
        ],
        (
            prompt_length, group_index, offsets, tokens, attn_gain[None, :], key_value_weight, query_weight,
            paired_cache,
        ),
        hbm=range(8),
        scratch=[
            pltpu.SMEM(prompt_length.shape, I32),
            pltpu.SMEM(group_index.shape, I32),
            pltpu.SMEM(offsets.shape, I32),
            pltpu.VMEM(tokens.shape, BF16),
            pltpu.VMEM((1, width), BF16),
            pltpu.VMEM(key_value_weight.shape[1:], BF16),
            pltpu.VMEM(query_weight.shape, BF16),
            pltpu.SemaphoreType.DMA((8,)),
        ],
        name="project",
        cost=(2 * rows * width * (heads + 1) * dim, 2 << 20),
    )
    other_new = swap(own_new, "tensor", 1)
    sums, tops, parts, extra = call(
        cached_body,
        [shape((heads * rows, dim), F32)] + [shape((heads * rows, LANES), F32)] * 2 + [shape((rows, extra_width), F32)],
        (
            queries, own_cache, other_cache, *places, sink_logit, routes.T, route_weight.T, copy_slot[None, :],
        ),
        hbm=range(6, 10),
        scratch=[
            pltpu.SMEM(sink_logit.shape, F32),
            pltpu.VMEM((TOP, rows), I32),
            pltpu.VMEM((TOP, rows), F32),
            pltpu.VMEM((1, copies), I32),
            pltpu.SemaphoreType.DMA((4,)),
        ],
        name="cached_attention",
        cost=(4 * heads * rows * dim * slots, 1 << 20),
    )
    send, keep = call(
        attend_body,
        [shape((rows, half), BF16), shape((rows, half + extra_width), F32)],
        (queries, own_new, other_new, sums, tops, parts, out_weight, token_half, extra),
        name="attention_out",
        cost=(2 * rows * heads * dim * width, 2 << 20),
    )
    own = call(
        chip_body, shape((rows, half + extra_width), BF16), (keep, swap(send, "tensor", 1)), name="chip_sum",
        cost=(rows * width, 1 << 18),
    )
    block, residual = call(
        functools.partial(residual_body, copies),
        [shape((2 * rows, half + extra_width), BF16), shape((rows, half), BF16)],
        (mixer_gain[None, :], own, swap(own, "tensor", 2), swap(own, "expert", 1), swap_both(own, 1, 2)),
        name="residual",
        cost=(rows * width, 1 << 18),
    )

    bit, stages = 2, []
    while bit < peers:
        stages.append([bit] if 2 * bit >= peers else [bit, 2 * bit, 3 * bit])
        bit *= 4
    blocks = [block]
    for stage in stages:
        whole = blocks[0] if len(blocks) == 1 else jnp.concatenate(blocks, axis=0)
        blocks = [whole] + [swap(whole, "expert", b) for b in stage]
    others = [swap(b, "tensor", 1) for b in blocks]
    pieces = []
    for i in range(0, len(blocks), 2):
        pieces += run_experts(
            blocks[i : i + 2], others[i : i + 2], gate_weight, up_weight, down_weight, copies, i == 0
        )
    terms = [pieces[0]] + [swap(p, "expert", b) for p, b in zip(pieces[1:], stages[-1])]
    for stage in stages[-2::-1]:
        tall = terms[0].shape[0] // (len(stage) + 1)
        pieces = call(
            functools.partial(pass_body, len(terms)),
            [shape((tall, half), F32)] + [shape((tall, half), BF16)] * len(stage),
            terms,
            vmem=48 << 20,
            name="pass_on",
            cost=(tall * width, 1 << 20),
        )
        terms = [pieces[0]] + [swap(p, "expert", b) for p, b in zip(pieces[1:], stage)]
    own, x_part, y_part = call(
        functools.partial(pair_body, len(terms)),
        [shape((rows, half), F32), shape((rows, half), BF16), shape((rows, half), BF16)],
        terms,
        name="z_sums",
        cost=(rows * width, 1 << 18),
    )
    combined, squares = call(
        combine_body,
        [shape((rows, quarter), F32), shape((rows, LANES), F32)],
        (own, swap(x_part, "tensor", 2), swap(y_part, "expert", 1), swap_both(y_part, 1, 2), residual),
        name="combine",
        cost=(rows * width, 1 << 18),
    )
    return call(
        functools.partial(finish_body, width),
        shape((rows, quarter), BF16),
        (combined, final_gain[None, :], squares, swap(squares, "tensor", 1)),
        name="finish",
        cost=(rows * width, 1 << 18),
    )


def solution(mesh):
    in_specs = (
        P("expert", None),
        P(),
        P(None, "tensor"),
        P("tensor", None, None),
        P("expert", "tensor", None, None),
        P("expert", None),
        P("expert"),
        P("expert"),
        P("tensor"),
        P("tensor", None),
        P(),
        P("expert", None),
        P("expert", None),
        P(),
        P("expert", None, "tensor"),
        P("expert", None, "tensor"),
        P("expert", "tensor", None),
        P("tensor"),
    )
    out_specs = P("expert", "tensor")
    return jax.shard_map(
        on_device, mesh=mesh, in_specs=in_specs, out_specs=out_specs, check_vma=False
    )
```

time: 79.7 us -> 67.7 us (0.85)
  local copies, waits for them, and re-layouts: 23.5 us -> 14.9 us
  starting transfers between devices: 20.4 us -> 19.2 us
  Pallas kernels: 10.1 us -> 8.94 us
  waiting for transfers between devices: 24.8 us -> 24 us
    unnamed x40 -> x34, local copies, waits for them, and re-layouts: 22.8 us -> 13.3 us
    ppermute x21 -> x20, waiting for transfers between devices: 22.4 us -> 20.2 us  [swap(): return lax.ppermute(block, axis, [(i, i ^ bits) for i in range(count)])]
    ppermute x2, waiting for transfers between devices: 2.42 us -> 3.84 us  [swap_both(): lax.ppermute(block, ('expert', 'tensor'), [(i, i ^ bits) for i in range(c...]
    ppermute x21 -> x20, starting transfers between devices: 18.1 us -> 16.8 us  [swap(): return lax.ppermute(block, axis, [(i, i ^ bits) for i in range(count)])]
    pallas_call x9 -> x10, Pallas kernels: 5.31 us -> 4.19 us  [call(): pl.pallas_call(body, out_shape=listed, in_specs=in_specs, out_specs=out_s...]
    pallas_call x2 -> x4, Pallas kernels: 4.76 us -> 4.75 us  [the longest x2 3.89 us: run_experts(): pl.pallas_call(functools.partial(expert_body, copies, blocks), grid=grid,...]
  transfers between devices with their start and end apart: 23 -> 22, of which waited for: 13 -> 12; matrix products, arithmetic and copies ran while one was open for 12% -> 2% of each run, Pallas kernels for 4% -> 11%
where the time goes in v2:
time: 67.7 us; the launch traced here: 67.3 us
  waiting for transfers between devices  24 us (35%)
  starting transfers between devices  19.2 us (28%)
  local copies, waits for them, and re-layouts  14.9 us (22%)
  Pallas kernels  8.94 us (13%)
    ppermute x20, waiting for transfers between devices, swap(): return lax.ppermute(block, axis, [(i, i ^ bits) for i in range(count)])  20.2 us
    ppermute x20, starting transfers between devices, swap(): return lax.ppermute(block, axis, [(i, i ^ bits) for i in range(count)])  16.8 us
    unnamed x34, local copies, waits for them, and re-layouts  13.3 us
    pallas_call x10, Pallas kernels, call(): pl.pallas_call(body, out_shape=listed, in_specs=in_specs, out_specs=out_s...  4.19 us
    pallas_call x2, Pallas kernels, run_experts(): pl.pallas_call(functools.partial(expert_body, copies, blocks), grid=grid,...  3.89 us
    ppermute x2, waiting for transfers between devices, swap_both(): lax.ppermute(block, ('expert', 'tensor'), [(i, i ^ bits) for i in range(c...  3.84 us
    ppermute x2, starting transfers between devices, swap_both(): lax.ppermute(block, ('expert', 'tensor'), [(i, i ^ bits) for i in range(c...  2.34 us
  transfers between devices with their start and end apart: 22, of which 12 were waited for; matrix products, arithmetic and copies ran while one was open for 2% of the time, Pallas kernels for 11%

profile of v2, /device:TPU:0, one launch (start us, length us, event | category | flops | bytes accessed | tf_op | source)
XLA Modules:
  0.0 67.3 jit_solution(17768627054132763689)
XLA Ops:
  0.5 0.9 %broadcast_in_dim.13.gain_hbm = bf16[1,1536]{1,0:T(2,128)(2,1)S(1)} reshape(bf16[1536]{0:T(1024)(128)(2,1)} %param.19) | data formatting | bytes 6144 | tf_op jit(solution)/shard_map/broadcast_in_dim | solution.py:426
  1.4 1.3 %copy-done.4 = bf16[1536,384]{1,0:T(8,128)(2,1)S(1)} copy-done((bf16[1536,384]{1,0:T(8,128)(2,1)S(1)}, bf16[1536,384]{1,0:T(8,128)(2,1)}, u32[]{:S(2)}) %copy-start.4) | copy-done | bytes 1179672
  2.6 1.0 %copy-done.6 = bf16[1,1536,128]{2,1,0:T(8,128)(2,1)S(1)} copy-done((bf16[1,1536,128]{2,1,0:T(8,128)(2,1)S(1)}, bf16[1,1536,128]{2,1,0:T(8,128)(2,1)}, u32[]{:S(2)}) %copy-start.6) | copy-done | bytes 393240
  3.6 0.9 %copy-done.7 = bf16[1,1,768,128]{3,2,1,0:T(8,128)(2,1)S(1)} copy-done((bf16[1,1,768,128]{3,2,1,0:T(8,128)(2,1)S(1)}, bf16[1,1,768,128]{3,2,1,0:T(8,128)(2,1)}, u32[]{:S(2)}) %copy-start.7) | copy-done | bytes 196632
  7.4 1.8 %project.1 = (bf16[96,128]{1,0:T(8,128)(2,1)S(1)}, bf16[32,128]{1,0:T(8,128)(2,1)S(1)}, bf16[768,128]{1,0:T(8,128)(2,1)S(1)}, f32[32,768]{1,0:T(8,128)S(1)}, s32...) custom-call(s32[1,3]{1,0:T(1,128)S(1)} %copy-done.11, s32[32]{0:T(128)S(1)} %copy-done.12, ...), custom_call_target="tpu_custom_call" | custom-call | flops 50331648 | bytes 2097152 | tf_op jit(solution)/shard_map/project/pallas_call | solution.py:56
  12.0 0.9 %cached_attention.1 = (f32[96,128]{1,0:T(8,128)S(1)}, f32[96,128]{1,0:T(8,128)S(1)}, f32[96,128]{1,0:T(8,128)S(1)}, f32[32,128]{1,0:T(8,128)S(1)}) custom-call(bf16[96,128]{1,0:T(8,128)(2,1)S(1)} %get-tuple-element.33.q_ref, bf16[768,128]{1,0:T(8,128)(2,1)S(1)} %get-tuple-element.35.mine_ref, bf16[768,128]{1,0:T(8,128)(2,1)S(1)} %collective-permute-done.1.theirs_ref, ...), custom_call_target="tpu_custom_call" | custom-call | flops 37748736 | bytes 1048576 | tf_op jit(solution)/shard_map/cached_attention/pallas_call | solution.py:56
  13.0 1.3 %copy-done.5 = bf16[384,1536]{1,0:T(8,128)(2,1)S(1)} copy-done((bf16[384,1536]{1,0:T(8,128)(2,1)S(1)}, bf16[384,1536]{1,0:T(8,128)(2,1)}, u32[]{:S(2)}) %copy-start.5) | copy-done | bytes 1179672
  16.1 2.7 %collective-permute-start.3 = (bf16[32,896]{1,0:T(8,128)(2,1)S(1)}, bf16[32,896]{1,0:T(8,128)(2,1)S(1)}, u32[]{:S(2)}, u32[]{:S(2)}) collective-permute-start(bf16[32,896]{1,0:T(8,128)(2,1)S(1)} %chip_sum.1.own_ref), channel_id=1, source_target_pairs={{0,2},{1,3},{2,0},{3,1},{4,6},{5,7},{6,4},{7,5},{8,10},{9,11},{10,... | collective-permute-start | bytes 172040 | tf_op jit(solution)/shard_map/ppermute | solution.py:25
  18.8 1.5 %collective-permute-start.4 = (bf16[32,896]{1,0:T(8,128)(2,1)S(1)}, bf16[32,896]{1,0:T(8,128)(2,1)S(1)}, u32[]{:S(2)}, u32[]{:S(2)}) collective-permute-start(bf16[32,896]{1,0:T(8,128)(2,1)S(1)} %chip_sum.1.own_ref), channel_id=1, source_target_pairs={{0,4},{4,0},{8,12},{12,8},{16,20},{20,16},{24,28},{28,24},{1,5},{5... | collective-permute-start | bytes 172040 | tf_op jit(solution)/shard_map/ppermute | solution.py:25
  21.0 1.9 %collective-permute-done.4.y_ref = bf16[32,896]{1,0:T(8,128)(2,1)S(1)} collective-permute-done((bf16[32,896]{1,0:T(8,128)(2,1)S(1)}, bf16[32,896]{1,0:T(8,128)(2,1)S(1)}, u32[]{:S(2)}, u32[]{:S(2)}) %collective-permute-start.4) | collective-permute-done | bytes 57376 | tf_op jit(solution)/shard_map/ppermute | solution.py:25
  23.0 2.4 %collective-permute-done.5.xy_ref = bf16[32,896]{1,0:T(8,128)(2,1)S(1)} collective-permute-done((bf16[32,896]{1,0:T(8,128)(2,1)S(1)}, bf16[32,896]{1,0:T(8,128)(2,1)S(1)}, u32[]{:S(2)}, u32[]{:S(2)}) %collective-permute-start.5) | collective-permute-done | bytes 57376 | tf_op jit(solution)/shard_map/ppermute | solution.py:32
  25.5 2.7 %collective-permute-start.11 = (bf16[64,896]{1,0:T(8,128)(2,1)S(1)}, bf16[64,896]{1,0:T(8,128)(2,1)S(1)}, u32[]{:S(2)}, u32[]{:S(2)}) collective-permute-start(bf16[64,896]{1,0:T(8,128)(2,1)S(1)} %get-tuple-element.46.refs_0_), channel_id=1, source_target_pairs={{0,16},{4,20},{8,24},{12,28},{16,0},{20,4},{24,8},{28,12},{1,17},{... | collective-permute-start | bytes 344072 | tf_op jit(solution)/shard_map/ppermute | solution.py:25
  28.2 1.4 %collective-permute-start.12 = (bf16[64,896]{1,0:T(8,128)(2,1)S(1)}, bf16[64,896]{1,0:T(8,128)(2,1)S(1)}, u32[]{:S(2)}, u32[]{:S(2)}) collective-permute-start(bf16[64,896]{1,0:T(8,128)(2,1)S(1)} %get-tuple-element.46.refs_0_), channel_id=1, source_target_pairs={{0,24},{4,28},{8,16},{12,20},{16,8},{20,12},{24,0},{28,4},{1,25},{... | collective-permute-start | bytes 344072 | tf_op jit(solution)/shard_map/ppermute | solution.py:25
  29.8 6.4 %collective-permute-done.11.refs_0_ = bf16[64,896]{1,0:T(8,128)(2,1)S(1)} collective-permute-done((bf16[64,896]{1,0:T(8,128)(2,1)S(1)}, bf16[64,896]{1,0:T(8,128)(2,1)S(1)}, u32[]{:S(2)}, u32[]{:S(2)}) %collective-permute-start.11) | collective-permute-done | bytes 114720 | tf_op jit(solution)/shard_map/ppermute | solution.py:25
  37.6 1.7 %copy-done.1 = bf16[4,1536,192]{1,2,0:T(8,128)(2,1)S(1)} copy-done((bf16[4,1536,192]{1,2,0:T(8,128)(2,1)S(1)}, bf16[4,1536,192]{1,2,0:T(8,128)(2,1)}, u32[]{:S(2)}) %copy-start.1) | copy-done | bytes 2359320
  39.3 1.7 %copy-done.3 = bf16[4,1536,192]{1,2,0:T(8,128)(2,1)S(1)} copy-done((bf16[4,1536,192]{1,2,0:T(8,128)(2,1)S(1)}, bf16[4,1536,192]{1,2,0:T(8,128)(2,1)}, u32[]{:S(2)}) %copy-start.3) | copy-done | bytes 2359320
  41.0 1.9 %experts.3 = (bf16[4,2,64,192]{3,2,1,0:T(8,128)(2,1)S(1)}, bf16[2,64,768]{2,1,0:T(8,128)(2,1)S(1)}) custom-call(bf16[64,896]{1,0:T(8,128)(2,1)S(1)} %collective-permute-done.11.refs_0_, bf16[64,896]{1,0:T(8,128)(2,1)S(1)} %collective-permute-done.12.refs_1_, bf16[64,896]{1,0:T(8,128)(2,1)S(1)} %collective-permute-done.13.refs_2_, ...), custom_call_target="tpu_custom_call" | custom-call | flops 754974720 | bytes 8388608 | tf_op jit(solution)/shard_map/experts/pallas_call | solution.py:369
  43.3 2.0 %experts.2 = (bf16[4,2,64,192]{3,2,1,0:T(8,128)(2,1)S(1)}, bf16[2,64,768]{2,1,0:T(8,128)(2,1)S(1)}) custom-call(bf16[64,896]{1,0:T(8,128)(2,1)S(1)} %get-tuple-element.46.refs_0_, bf16[64,896]{1,0:T(8,128)(2,1)S(1)} %collective-permute-done.6.refs_1_, bf16[64,896]{1,0:T(8,128)(2,1)S(1)} %collective-permute-done.7.refs_2_, ...), custom_call_target="tpu_custom_call" | custom-call | flops 754974720 | bytes 8388608 | tf_op jit(solution)/shard_map/experts/pallas_call | solution.py:369
  46.5 3.7 %collective-permute-start.16 = (bf16[64,768]{1,0:T(8,128)(2,1)S(1)}, bf16[64,768]{1,0:T(8,128)(2,1)S(1)}, u32[]{:S(2)}, u32[]{:S(2)}) collective-permute-start(bf16[64,768]{1,0:T(8,128)(2,1)S(1)} %get-tuple-element.53), channel_id=1, source_target_pairs={{0,16},{4,20},{8,24},{12,28},{16,0},{20,4},{24,8},{28,12},{1,17},{... | collective-permute-start | bytes 294920 | tf_op jit(solution)/shard_map/ppermute | solution.py:25
  50.9 6.9 %collective-permute-done.16.refs_2_ = bf16[64,768]{1,0:T(8,128)(2,1)S(1)} collective-permute-done((bf16[64,768]{1,0:T(8,128)(2,1)S(1)}, bf16[64,768]{1,0:T(8,128)(2,1)S(1)}, u32[]{:S(2)}, u32[]{:S(2)}) %collective-permute-start.16) | collective-permute-done | bytes 98336 | tf_op jit(solution)/shard_map/ppermute | solution.py:25
  57.8 1.2 %collective-permute-done.10.refs_1_ = bf16[64,768]{1,0:T(8,128)(2,1)S(1)} collective-permute-done((bf16[64,768]{1,0:T(8,128)(2,1)S(1)}, bf16[64,768]{1,0:T(8,128)(2,1)S(1)}, u32[]{:S(2)}, u32[]{:S(2)}) %collective-permute-start.10) | collective-permute-done | bytes 98336 | tf_op jit(solution)/shard_map/ppermute | solution.py:25
  60.3 2.3 %collective-permute-start.20 = (bf16[32,768]{1,0:T(8,128)(2,1)S(1)}, bf16[32,768]{1,0:T(8,128)(2,1)S(1)}, u32[]{:S(2)}, u32[]{:S(2)}) collective-permute-start(bf16[32,768]{1,0:T(8,128)(2,1)S(1)} %get-tuple-element.57), channel_id=1, source_target_pairs={{0,6},{1,7},{2,4},{3,5},{4,2},{5,3},{6,0},{7,1},{8,14},{9,15},{10,... | collective-permute-start | bytes 147464 | tf_op jit(solution)/shard_map/ppermute | solution.py:32
  63.8 1.4 %collective-permute-done.20.xy_ref = bf16[32,768]{1,0:T(8,128)(2,1)S(1)} collective-permute-done((bf16[32,768]{1,0:T(8,128)(2,1)S(1)}, bf16[32,768]{1,0:T(8,128)(2,1)S(1)}, u32[]{:S(2)}, u32[]{:S(2)}) %collective-permute-start.20) | collective-permute-done | bytes 49184 | tf_op jit(solution)/shard_map/ppermute | solution.py:32
  65.4 1.2 %collective-permute-done.21.b_ref = f32[32,128]{1,0:T(8,128)S(1)} collective-permute-done((f32[32,128]{1,0:T(8,128)S(1)}, f32[32,128]{1,0:T(8,128)S(1)}, u32[]{:S(2)}, u32[]{:S(2)}) %collective-permute-start.21) | collective-permute-done | bytes 16416 | tf_op jit(solution)/shard_map/ppermute | solution.py:25
  (71 shorter events, 16.1 us)
Async XLA Ops:
  0.0 37.6 %copy-start = (bf16[4,192,1536]{2,1,0:T(8,128)(2,1)S(1)}, bf16[4,192,1536]{2,1,0:T(8,128)(2,1)}, u32[]{:S(2)}) copy-start(bf16[4,192,1536]{2,1,0:T(8,128)(2,1)} %down_ref.3) | copy-start | bytes 7077892
  0.0 9.3 %collective-permute-start.1 = (bf16[768,128]{1,0:T(8,128)(2,1)}, bf16[768,128]{1,0:T(8,128)(2,1)S(1)}, u32[]{:S(2)}, u32[]{:S(2)}) collective-permute-start(bf16[768,128]{1,0:T(8,128)(2,1)} %bitcast.10), channel_id=1, source_target_pairs={{0,1},{1,0},{2,3},{3,2},{4,5},{5,4},{6,7},{7,6},{8,9},{9,8},{10,11... | collective-permute-start | bytes 589832 | tf_op jit(solution)/shard_map/ppermute | solution.py:25
  9.2 3.7 %collective-permute-start = (bf16[32,128]{1,0:T(8,128)(2,1)S(1)}, bf16[32,128]{1,0:T(8,128)(2,1)S(1)}, u32[]{:S(2)}, u32[]{:S(2)}) collective-permute-start(bf16[32,128]{1,0:T(8,128)(2,1)S(1)} %get-tuple-element.34.mine_ref), channel_id=1, source_target_pairs={{0,1},{1,0},{2,3},{3,2},{4,5},{5,4},{6,7},{7,6},{8,9},{9,8},{10,11... | collective-permute-start | bytes 24584 | tf_op jit(solution)/shard_map/ppermute | solution.py:25
  14.6 1.4 %collective-permute-start.2 = (bf16[32,768]{1,0:T(8,128)(2,1)S(1)}, bf16[32,768]{1,0:T(8,128)(2,1)S(1)}, u32[]{:S(2)}, u32[]{:S(2)}) collective-permute-start(bf16[32,768]{1,0:T(8,128)(2,1)S(1)} %get-tuple-element.45), channel_id=1, source_target_pairs={{0,1},{1,0},{2,3},{3,2},{4,5},{5,4},{6,7},{7,6},{8,9},{9,8},{10,11... | collective-permute-start | bytes 147464 | tf_op jit(solution)/shard_map/ppermute | solution.py:25
  16.1 5.0 %collective-permute-start.3 = (bf16[32,896]{1,0:T(8,128)(2,1)S(1)}, bf16[32,896]{1,0:T(8,128)(2,1)S(1)}, u32[]{:S(2)}, u32[]{:S(2)}) collective-permute-start(bf16[32,896]{1,0:T(8,128)(2,1)S(1)} %chip_sum.1.own_ref), channel_id=1, source_target_pairs={{0,2},{1,3},{2,0},{3,1},{4,6},{5,7},{6,4},{7,5},{8,10},{9,11},{10,... | collective-permute-start | bytes 172040 | tf_op jit(solution)/shard_map/ppermute | solution.py:25
  18.8 4.2 %collective-permute-start.4 = (bf16[32,896]{1,0:T(8,128)(2,1)S(1)}, bf16[32,896]{1,0:T(8,128)(2,1)S(1)}, u32[]{:S(2)}, u32[]{:S(2)}) collective-permute-start(bf16[32,896]{1,0:T(8,128)(2,1)S(1)} %chip_sum.1.own_ref), channel_id=1, source_target_pairs={{0,4},{4,0},{8,12},{12,8},{16,20},{20,16},{24,28},{28,24},{1,5},{5... | collective-permute-start | bytes 172040 | tf_op jit(solution)/shard_map/ppermute | solution.py:25
  20.3 5.1 %collective-permute-start.5 = (bf16[32,896]{1,0:T(8,128)(2,1)S(1)}, bf16[32,896]{1,0:T(8,128)(2,1)S(1)}, u32[]{:S(2)}, u32[]{:S(2)}) collective-permute-start(bf16[32,896]{1,0:T(8,128)(2,1)S(1)} %chip_sum.1.own_ref), channel_id=1, source_target_pairs={{0,6},{1,7},{2,4},{3,5},{4,2},{5,3},{6,0},{7,1},{8,14},{9,15},{10,... | collective-permute-start | bytes 172040 | tf_op jit(solution)/shard_map/ppermute | solution.py:32
  25.5 10.6 %collective-permute-start.11 = (bf16[64,896]{1,0:T(8,128)(2,1)S(1)}, bf16[64,896]{1,0:T(8,128)(2,1)S(1)}, u32[]{:S(2)}, u32[]{:S(2)}) collective-permute-start(bf16[64,896]{1,0:T(8,128)(2,1)S(1)} %get-tuple-element.46.refs_0_), channel_id=1, source_target_pairs={{0,16},{4,20},{8,24},{12,28},{16,0},{20,4},{24,8},{28,12},{1,17},{... | collective-permute-start | bytes 344072 | tf_op jit(solution)/shard_map/ppermute | solution.py:25
  28.2 8.0 %collective-permute-start.12 = (bf16[64,896]{1,0:T(8,128)(2,1)S(1)}, bf16[64,896]{1,0:T(8,128)(2,1)S(1)}, u32[]{:S(2)}, u32[]{:S(2)}) collective-permute-start(bf16[64,896]{1,0:T(8,128)(2,1)S(1)} %get-tuple-element.46.refs_0_), channel_id=1, source_target_pairs={{0,24},{4,28},{8,16},{12,20},{16,8},{20,12},{24,0},{28,4},{1,25},{... | collective-permute-start | bytes 344072 | tf_op jit(solution)/shard_map/ppermute | solution.py:25
  29.5 7.1 %collective-permute-start.6 = (bf16[64,896]{1,0:T(8,128)(2,1)S(1)}, bf16[64,896]{1,0:T(8,128)(2,1)S(1)}, u32[]{:S(2)}, u32[]{:S(2)}) collective-permute-start(bf16[64,896]{1,0:T(8,128)(2,1)S(1)} %get-tuple-element.46.refs_0_), channel_id=1, source_target_pairs={{0,8},{4,12},{8,0},{12,4},{16,24},{20,28},{24,16},{28,20},{1,9},{5... | collective-permute-start | bytes 344072 | tf_op jit(solution)/shard_map/ppermute | solution.py:25
  36.1 1.3 %collective-permute-start.13 = (bf16[64,896]{1,0:T(8,128)(2,1)S(1)}, bf16[64,896]{1,0:T(8,128)(2,1)S(1)}, u32[]{:S(2)}, u32[]{:S(2)}) collective-permute-start(bf16[64,896]{1,0:T(8,128)(2,1)S(1)} %collective-permute-done.11.refs_0_), channel_id=1, source_target_pairs={{0,1},{1,0},{2,3},{3,2},{4,5},{5,4},{6,7},{7,6},{8,9},{9,8},{10,11... | collective-permute-start | bytes 344072 | tf_op jit(solution)/shard_map/ppermute | solution.py:25
  36.1 1.5 %collective-permute-start.14 = (bf16[64,896]{1,0:T(8,128)(2,1)S(1)}, bf16[64,896]{1,0:T(8,128)(2,1)S(1)}, u32[]{:S(2)}, u32[]{:S(2)}) collective-permute-start(bf16[64,896]{1,0:T(8,128)(2,1)S(1)} %collective-permute-done.12.refs_1_), channel_id=1, source_target_pairs={{0,1},{1,0},{2,3},{3,2},{4,5},{5,4},{6,7},{7,6},{8,9},{9,8},{10,11... | collective-permute-start | bytes 344072 | tf_op jit(solution)/shard_map/ppermute | solution.py:25
  36.7 6.7 %collective-permute-start.7 = (bf16[64,896]{1,0:T(8,128)(2,1)S(1)}, bf16[64,896]{1,0:T(8,128)(2,1)S(1)}, u32[]{:S(2)}, u32[]{:S(2)}) collective-permute-start(bf16[64,896]{1,0:T(8,128)(2,1)S(1)} %get-tuple-element.46.refs_0_), channel_id=1, source_target_pairs={{0,1},{1,0},{2,3},{3,2},{4,5},{5,4},{6,7},{7,6},{8,9},{9,8},{10,11... | collective-permute-start | bytes 344072 | tf_op jit(solution)/shard_map/ppermute | solution.py:25
  36.7 6.7 %collective-permute-start.8 = (bf16[64,896]{1,0:T(8,128)(2,1)S(1)}, bf16[64,896]{1,0:T(8,128)(2,1)S(1)}, u32[]{:S(2)}, u32[]{:S(2)}) collective-permute-start(bf16[64,896]{1,0:T(8,128)(2,1)S(1)} %collective-permute-done.6.refs_1_), channel_id=1, source_target_pairs={{0,1},{1,0},{2,3},{3,2},{4,5},{5,4},{6,7},{7,6},{8,9},{9,8},{10,11... | collective-permute-start | bytes 344072 | tf_op jit(solution)/shard_map/ppermute | solution.py:25
  42.9 3.5 %collective-permute-start.15 = (bf16[2,64,768]{2,1,0:T(8,128)(2,1)S(1)}, bf16[2,64,768]{2,1,0:T(8,128)(2,1)S(1)}, u32[]{:S(2)}, u32[]{:S(2)}) collective-permute-start(bf16[2,64,768]{2,1,0:T(8,128)(2,1)S(1)} %get-tuple-element.52), channel_id=1, source_target_pairs={{0,1},{1,0},{2,3},{3,2},{4,5},{5,4},{6,7},{7,6},{8,9},{9,8},{10,11... | collective-permute-start | bytes 589832 | tf_op jit(solution)/shard_map/ppermute | solution.py:25
  45.3 5.3 %collective-permute-start.9 = (bf16[2,64,768]{2,1,0:T(8,128)(2,1)S(1)}, bf16[2,64,768]{2,1,0:T(8,128)(2,1)S(1)}, u32[]{:S(2)}, u32[]{:S(2)}) collective-permute-start(bf16[2,64,768]{2,1,0:T(8,128)(2,1)S(1)} %get-tuple-element.48), channel_id=1, source_target_pairs={{0,1},{1,0},{2,3},{3,2},{4,5},{5,4},{6,7},{7,6},{8,9},{9,8},{10,11... | collective-permute-start | bytes 589832 | tf_op jit(solution)/shard_map/ppermute | solution.py:25
  45.9 19.5 %copy-start.16 = (bf16[384]{0:T(512)(128)(2,1)S(1)}, bf16[384]{0:T(512)(128)(2,1)}, u32[]{:S(2)}) copy-start(bf16[384]{0:T(512)(128)(2,1)} %param.35) | copy-start | bytes 2308
  46.5 11.4 %collective-permute-start.16 = (bf16[64,768]{1,0:T(8,128)(2,1)S(1)}, bf16[64,768]{1,0:T(8,128)(2,1)S(1)}, u32[]{:S(2)}, u32[]{:S(2)}) collective-permute-start(bf16[64,768]{1,0:T(8,128)(2,1)S(1)} %get-tuple-element.53), channel_id=1, source_target_pairs={{0,16},{4,20},{8,24},{12,28},{16,0},{20,4},{24,8},{28,12},{1,17},{... | collective-permute-start | bytes 294920 | tf_op jit(solution)/shard_map/ppermute | solution.py:25
  50.2 7.7 %collective-permute-start.17 = (bf16[64,768]{1,0:T(8,128)(2,1)S(1)}, bf16[64,768]{1,0:T(8,128)(2,1)S(1)}, u32[]{:S(2)}, u32[]{:S(2)}) collective-permute-start(bf16[64,768]{1,0:T(8,128)(2,1)S(1)} %get-tuple-element.54), channel_id=1, source_target_pairs={{0,24},{4,28},{8,16},{12,20},{16,8},{20,12},{24,0},{28,4},{1,25},{... | collective-permute-start | bytes 294920 | tf_op jit(solution)/shard_map/ppermute | solution.py:25
  50.7 8.3 %collective-permute-start.10 = (bf16[64,768]{1,0:T(8,128)(2,1)S(1)}, bf16[64,768]{1,0:T(8,128)(2,1)S(1)}, u32[]{:S(2)}, u32[]{:S(2)}) collective-permute-start(bf16[64,768]{1,0:T(8,128)(2,1)S(1)} %get-tuple-element.50), channel_id=1, source_target_pairs={{0,8},{4,12},{8,0},{12,4},{16,24},{20,28},{24,16},{28,20},{1,9},{5... | collective-permute-start | bytes 294920 | tf_op jit(solution)/shard_map/ppermute | solution.py:25
  59.1 4.5 %collective-permute-start.18 = (bf16[32,768]{1,0:T(8,128)(2,1)S(1)}, bf16[32,768]{1,0:T(8,128)(2,1)S(1)}, u32[]{:S(2)}, u32[]{:S(2)}) collective-permute-start(bf16[32,768]{1,0:T(8,128)(2,1)S(1)} %get-tuple-element.56), channel_id=1, source_target_pairs={{0,2},{1,3},{2,0},{3,1},{4,6},{5,7},{6,4},{7,5},{8,10},{9,11},{10,... | collective-permute-start | bytes 147464 | tf_op jit(solution)/shard_map/ppermute | solution.py:25
  59.6 4.2 %collective-permute-start.19 = (bf16[32,768]{1,0:T(8,128)(2,1)S(1)}, bf16[32,768]{1,0:T(8,128)(2,1)S(1)}, u32[]{:S(2)}, u32[]{:S(2)}) collective-permute-start(bf16[32,768]{1,0:T(8,128)(2,1)S(1)} %get-tuple-element.57), channel_id=1, source_target_pairs={{0,4},{4,0},{8,12},{12,8},{16,20},{20,16},{24,28},{28,24},{1,5},{5... | collective-permute-start | bytes 147464 | tf_op jit(solution)/shard_map/ppermute | solution.py:25
  60.3 5.0 %collective-permute-start.20 = (bf16[32,768]{1,0:T(8,128)(2,1)S(1)}, bf16[32,768]{1,0:T(8,128)(2,1)S(1)}, u32[]{:S(2)}, u32[]{:S(2)}) collective-permute-start(bf16[32,768]{1,0:T(8,128)(2,1)S(1)} %get-tuple-element.57), channel_id=1, source_target_pairs={{0,6},{1,7},{2,4},{3,5},{4,2},{5,3},{6,0},{7,1},{8,14},{9,15},{10,... | collective-permute-start | bytes 147464 | tf_op jit(solution)/shard_map/ppermute | solution.py:32
  65.4 1.2 %collective-permute-start.21 = (f32[32,128]{1,0:T(8,128)S(1)}, f32[32,128]{1,0:T(8,128)S(1)}, u32[]{:S(2)}, u32[]{:S(2)}) collective-permute-start(f32[32,128]{1,0:T(8,128)S(1)} %get-tuple-element.60.a_ref), channel_id=1, source_target_pairs={{0,1},{1,0},{2,3},{3,2},{4,5},{5,4},{6,7},{7,6},{8,9},{9,8},{10,11... | collective-permute-start | bytes 49160 | tf_op jit(solution)/shard_map/ppermute | solution.py:25
  (15 other events, 15.7 us)

commit v3 on v2

--- a/solution.py
+++ b/solution.py
@@ -14,6 +14,7 @@
 WINDOW = 192
 EPSILON = 1e-06
 LANES = 128
+CHUNKS = 4
 HIDE = -1e30
 F32 = jnp.float32
 BF16 = jnp.bfloat16
@@ -44,11 +45,12 @@
     return lax.dot_general(a, b, (((1,), (1,)), ((), ())), preferred_element_type=F32)
 
 
-def call(body, outs, args, hbm=(), scratch=(), vmem=None, cost=None, name=None):
+def call(body, outs, args, hbm=(), free=(), scratch=(), vmem=None, cost=None, name=None):
     in_specs = [
-        pl.BlockSpec(memory_space=pltpu.HBM) if i in hbm else pl.BlockSpec(memory_space=pltpu.VMEM)
+        pl.BlockSpec(memory_space=pltpu.HBM if i in hbm else pl.ANY if i in free else pltpu.VMEM)
         for i in range(len(args))
     ]
+    args = [pltpu.with_memory_space_constraint(a, pltpu.HBM) if i in hbm else a for i, a in enumerate(args)]
     single = not isinstance(outs, (list, tuple))
     listed = [outs] if single else list(outs)
     out_specs = [pl.BlockSpec(memory_space=pltpu.VMEM) for _ in listed]
@@ -91,14 +93,17 @@
     q_ref, own_ref, cache_ref, token_ref, group_out, length_out, position_out,
     length_ref, group_ref, offset_ref, tok_ref, gain_ref, kvw_ref, qw_ref, sems,
 ):
+    rows, width = tok_ref.shape
+    part = width // CHUNKS
     pairs = [
         (length_hbm, length_ref), (group_hbm, group_ref), (offset_hbm, offset_ref), (tok_hbm, tok_ref),
-        (gain_hbm, gain_ref), (kvw_hbm.at[0], kvw_ref), (qw_hbm, qw_ref), (cache_hbm.at[0, 0], cache_ref),
+        (gain_hbm, gain_ref), (kvw_hbm.at[0], kvw_ref),
     ]
+    pairs += [(qw_hbm.at[pl.ds(i * part, part)], qw_ref.at[pl.ds(i * part, part)]) for i in range(CHUNKS)]
+    pairs += [(cache_hbm.at[0, 0], cache_ref)]
     loads = [pltpu.make_async_copy(src, dst, sems.at[i]) for i, (src, dst) in enumerate(pairs)]
     for load in loads:
         load.start()
-    rows, width = tok_ref.shape
     dim = kvw_ref.shape[1]
     heads = qw_ref.shape[1] // dim
     half = dim // 2
@@ -121,7 +126,7 @@
     loads[4].wait()
     tok = tok_ref[...].astype(F32)
     mean = jnp.sum(tok * tok, axis=1, keepdims=True) / width
-    normed = (tok * lax.rsqrt(mean + EPSILON) * gain_ref[...].astype(F32)).astype(BF16)
+    normed = (tok * lax.rsqrt(mean + EPSILON) * gain_ref[...].astype(F32).reshape(1, width)).astype(BF16)
     for i in range(2):
         low, high = (tok[:, (2 * i + k) * quarter : (2 * i + k + 1) * quarter] for k in range(2))
         token_ref[:, i * quarter : (i + 1) * quarter] = jnp.where(
@@ -131,12 +136,15 @@
     own = dot(normed, kvw_ref[...])
     turned = own * cosine + pltpu.roll(own, half, 1) * sine
     own_ref[...] = jnp.where(is_key(), turned, own).astype(BF16)
-    loads[6].wait()
-    q = dot(normed, qw_ref[...])
+    q = None
+    for i in range(CHUNKS):
+        loads[6 + i].wait()
+        part_sum = dot(normed[:, i * part : (i + 1) * part], qw_ref[i * part : (i + 1) * part, :])
+        q = part_sum if q is None else q + part_sum
     for h in range(heads):
-        part = q[:, h * dim : (h + 1) * dim]
-        q_ref[h * rows : (h + 1) * rows, :] = (part * cosine + pltpu.roll(part, half, 1) * sine).astype(BF16)
-    loads[7].wait()
+        head = q[:, h * dim : (h + 1) * dim]
+        q_ref[h * rows : (h + 1) * rows, :] = (head * cosine + pltpu.roll(head, half, 1) * sine).astype(BF16)
+    loads[-1].wait()
 
 
 def cached_body(
@@ -229,7 +237,25 @@
     out_ref[:, width:] = keep_ref[:, width:].astype(BF16)
 
 
-def residual_body(copies, gain_ref, own_ref, x_ref, y_ref, xy_ref, rows_ref, keep_ref):
+def relay_body(count, *refs):
+    for src, dst in zip(refs[:count], refs[-count:]):
+        dst[...] = src[...]
+
+
+def after_all(blocks, earlier):
+    tall, total = blocks[0].shape
+    return call(
+        functools.partial(relay_body, len(blocks)),
+        [shape(b.shape, b.dtype) for b in blocks],
+        (*blocks, *earlier),
+        free=range(len(blocks), len(blocks) + len(earlier)),
+        vmem=16 << 20,
+        name="relay",
+        cost=(len(blocks) * tall * total, 1 << 18),
+    )
+
+
+def residual_body(copies, gain_ref, own_ref, x_ref, y_ref, xy_ref, loaded_ref, rows_ref, keep_ref):
     rows, total = own_ref.shape
     width = keep_ref.shape[1]
     quarter = width // 2
@@ -254,9 +280,23 @@
         rows_ref[span, width:] = extra.astype(BF16)
 
 
+def load_body(*refs):
+    sems = refs[-1]
+    count = (len(refs) - 2) // 2
+    loads = []
+    for src, dst in zip(refs[1 : 1 + count], refs[1 + count : -1]):
+        for j in range(src.shape[0]):
+            loads.append(pltpu.make_async_copy(src.at[j], dst.at[j], sems.at[len(loads)]))
+    for load in loads:
+        load.start()
+    for load in loads:
+        load.wait()
+
+
 def expert_body(copies, blocks, *refs):
     own_refs, other_refs = refs[:blocks], refs[blocks : 2 * blocks]
-    gate_ref, up_ref, down_ref, hidden_ref, send_ref = refs[2 * blocks :]
+    gate_ref, up_ref, down_ref = refs[2 * blocks : 2 * blocks + 3]
+    hidden_ref, send_ref = refs[-2:]
     hosted, units, width = gate_ref.shape
     quarter = width // 4
     own = jnp.concatenate([r[...] for r in own_refs], axis=0)
@@ -373,7 +413,7 @@
         in_specs=[row_spec] * (2 * blocks) + [whole] * 3,
         out_specs=[hidden_spec, half_spec],
         compiler_params=params,
-        cost_estimate=pl.CostEstimate(flops=5 * flops // 2, bytes_accessed=8 << 20, transcendentals=0),
+        cost_estimate=pl.CostEstimate(flops=1, bytes_accessed=1, transcendentals=0),
         name="experts",
     )(*own, *other, gate_weight, up_weight, down_weight)
     got = swap(send, "tensor", 1)
@@ -384,7 +424,7 @@
         in_specs=[hidden_spec, whole],
         out_specs=half_spec,
         compiler_params=params,
-        cost_estimate=pl.CostEstimate(flops=flops // 2, bytes_accessed=3 << 20, transcendentals=0),
+        cost_estimate=pl.CostEstimate(flops=1, bytes_accessed=1, transcendentals=0),
         name="experts_own_half",
     )(hidden, down_weight)
     sums = call(
@@ -393,9 +433,9 @@
         (keep, got),
         vmem=48 << 20,
         name="chip_sums",
-        cost=(blocks * tall * width, 1 << 20),
-    )
-    return list(sums)
+        cost=(1, 1),
+    )
+    return list(sums), send
 
 
 def on_device(
@@ -409,7 +449,7 @@
     half, quarter = width // 2, width // 4
     slots = paired_cache.shape[2]
     copies = copy_slot.shape[0]
-    peers = lax.axis_size("expert")
+    far = lax.axis_size("expert") // 2
     extra_width = -(-(2 * copies + 2) // LANES) * LANES
     gate_weight = jnp.swapaxes(gate_weight, 1, 2)
     up_weight = jnp.swapaxes(up_weight, 1, 2)
@@ -423,7 +463,7 @@
             shape((rows, half), F32), place, place, place,
         ],
         (
-            prompt_length, group_index, offsets, tokens, attn_gain[None, :], key_value_weight, query_weight,
+            prompt_length, group_index, offsets, tokens, attn_gain, key_value_weight, query_weight,
             paired_cache,
         ),
         hbm=range(8),
@@ -432,10 +472,10 @@
             pltpu.SMEM(group_index.shape, I32),
             pltpu.SMEM(offsets.shape, I32),
             pltpu.VMEM(tokens.shape, BF16),
-            pltpu.VMEM((1, width), BF16),
+            pltpu.VMEM((width,), BF16),
             pltpu.VMEM(key_value_weight.shape[1:], BF16),
             pltpu.VMEM(query_weight.shape, BF16),
-            pltpu.SemaphoreType.DMA((8,)),
+            pltpu.SemaphoreType.DMA((7 + CHUNKS,)),
         ],
         name="project",
         cost=(2 * rows * width * (heads + 1) * dim, 2 << 20),
@@ -469,28 +509,40 @@
         chip_body, shape((rows, half + extra_width), BF16), (keep, swap(send, "tensor", 1)), name="chip_sum",
         cost=(rows * width, 1 << 18),
     )
+    weights = (gate_weight, up_weight, down_weight)
+    weights = call(
+        load_body,
+        [shape(w.shape, BF16) for w in weights],
+        (own, *weights),
+        hbm=range(1, 4),
+        scratch=[pltpu.SemaphoreType.DMA((sum(w.shape[0] for w in weights),))],
+        name="load_experts",
+        cost=(0, 8 << 20),
+    )
     block, residual = call(
         functools.partial(residual_body, copies),
         [shape((2 * rows, half + extra_width), BF16), shape((rows, half), BF16)],
-        (mixer_gain[None, :], own, swap(own, "tensor", 2), swap(own, "expert", 1), swap_both(own, 1, 2)),
+        (mixer_gain[None, :], own, swap(own, "tensor", 2), swap(own, "expert", far), swap_both(own, far, 2), weights[0]),
+        free=[5],
         name="residual",
         cost=(rows * width, 1 << 18),
     )
 
-    bit, stages = 2, []
-    while bit < peers:
-        stages.append([bit] if 2 * bit >= peers else [bit, 2 * bit, 3 * bit])
+    bit, stages = 1, []
+    while bit < far:
+        stages.append([bit] if 2 * bit >= far else [bit, 2 * bit, 3 * bit])
         bit *= 4
     blocks = [block]
     for stage in stages:
         whole = blocks[0] if len(blocks) == 1 else jnp.concatenate(blocks, axis=0)
         blocks = [whole] + [swap(whole, "expert", b) for b in stage]
-    others = [swap(b, "tensor", 1) for b in blocks]
     pieces = []
-    for i in range(0, len(blocks), 2):
-        pieces += run_experts(
-            blocks[i : i + 2], others[i : i + 2], gate_weight, up_weight, down_weight, copies, i == 0
-        )
+    for group in (blocks[:1], blocks[1:]):
+        if pieces:
+            group = after_all(group, [send])
+        others = [swap(b, "tensor", 1) for b in group]
+        sums, send = run_experts(group, others, *weights, copies, not pieces)
+        pieces += sums
     terms = [pieces[0]] + [swap(p, "expert", b) for p, b in zip(pieces[1:], stages[-1])]
     for stage in stages[-2::-1]:
         tall = terms[0].shape[0] // (len(stage) + 1)
@@ -503,7 +555,7 @@
             cost=(tall * width, 1 << 20),
         )
         terms = [pieces[0]] + [swap(p, "expert", b) for p, b in zip(pieces[1:], stage)]
-    own, x_part, y_part = call(
+    own, x_part, far_part = call(
         functools.partial(pair_body, len(terms)),
         [shape((rows, half), F32), shape((rows, half), BF16), shape((rows, half), BF16)],
         terms,
@@ -513,7 +565,7 @@
     combined, squares = call(
         combine_body,
         [shape((rows, quarter), F32), shape((rows, LANES), F32)],
-        (own, swap(x_part, "tensor", 2), swap(y_part, "expert", 1), swap_both(y_part, 1, 2), residual),
+        (own, swap(x_part, "tensor", 2), swap(far_part, "expert", far), swap_both(far_part, far, 2), residual),
         name="combine",
         cost=(rows * width, 1 << 18),
     )

time: 67.7 us -> 52.5 us (0.78)
  local copies, waits for them, and re-layouts: 14.9 us -> 0.02 us
  waiting for transfers between devices: 24 us -> 20.2 us
  Pallas kernels: 8.94 us -> 12.4 us
    unnamed x34 -> x6, local copies, waits for them, and re-layouts: 13.3 us -> 0.01 us
    ppermute x20, waiting for transfers between devices: 20.2 us -> 15.3 us  [swap(): return lax.ppermute(block, axis, [(i, i ^ bits) for i in range(count)])]
    pallas_call x10 -> x12, Pallas kernels: 4.19 us -> 7.79 us  [call(): pl.pallas_call(body, out_shape=listed, in_specs=in_specs, out_specs=out_s...]
    ppermute x20, starting transfers between devices: 16.8 us -> 18.7 us  [swap(): return lax.ppermute(block, axis, [(i, i ^ bits) for i in range(count)])]
    ppermute x2, starting transfers between devices: 2.34 us -> 0.73 us  [swap_both(): lax.ppermute(block, ('expert', 'tensor'), [(i, i ^ bits) for i in range(c...]
    ppermute x2, waiting for transfers between devices: 3.84 us -> 4.91 us  [swap_both(): lax.ppermute(block, ('expert', 'tensor'), [(i, i ^ bits) for i in range(c...]
    broadcast_in_dim x1 -> x0, local copies, waits for them, and re-layouts: 0.92 us -> none  [on_device(): attn_gain[None, :]]
    broadcast_in_dim x1, local copies, waits for them, and re-layouts: 0.69 us -> 0.01 us  [on_device(): mixer_gain[None, :]]
  transfers between devices with their start and end apart: 22 -> 22, of which waited for: 12 -> 16; matrix products, arithmetic and copies ran while one was open for 2% -> 0% of each run, Pallas kernels for 11% -> 18%
where the time goes in v3:
time: 52.5 us; the launch traced here: 52.3 us
  waiting for transfers between devices  20.2 us (38%)
  starting transfers between devices  19.4 us (37%)
  Pallas kernels  12.4 us (24%)
    ppermute x20, starting transfers between devices, swap(): return lax.ppermute(block, axis, [(i, i ^ bits) for i in range(count)])  18.7 us
    ppermute x20, waiting for transfers between devices, swap(): return lax.ppermute(block, axis, [(i, i ^ bits) for i in range(count)])  15.3 us
    pallas_call x12, Pallas kernels, call(): pl.pallas_call(body, out_shape=listed, in_specs=in_specs, out_specs=out_s...  7.79 us
    ppermute x2, waiting for transfers between devices, swap_both(): lax.ppermute(block, ('expert', 'tensor'), [(i, i ^ bits) for i in range(c...  4.91 us
    pallas_call x2, Pallas kernels, run_experts(): pl.pallas_call(functools.partial(expert_body, copies, blocks), grid=grid,...  3.69 us
  transfers between devices with their start and end apart: 22, of which 16 were waited for; matrix products, arithmetic and copies ran while one was open for 0% of the time, Pallas kernels for 18%

profile of v3, /device:TPU:0, one launch (start us, length us, event | category | flops | bytes accessed | tf_op | source)
XLA Modules:
  0.0 52.3 jit_solution(14718797264246393059)
XLA Ops:
  0.5 2.0 %project.1 = (bf16[96,128]{1,0:T(8,128)(2,1)S(1)}, bf16[32,128]{1,0:T(8,128)(2,1)S(1)}, bf16[768,128]{1,0:T(8,128)(2,1)S(1)}, f32[32,768]{1,0:T(8,128)S(1)}, s32...) custom-call(s32[1,3]{1,0:T(1,128)} %length_hbm.1, s32[32]{0:T(128)} %group_hbm.1, s32[32]{0:T(128)} %offset_hbm.1, ...), custom_call_target="tpu_custom_call" | custom-call | flops 50331648 | bytes 2097152 | tf_op jit(solution)/shard_map/project/pallas_call | solution.py:58
  2.7 1.1 %cached_attention.1 = (f32[96,128]{1,0:T(8,128)S(1)}, f32[96,128]{1,0:T(8,128)S(1)}, f32[96,128]{1,0:T(8,128)S(1)}, f32[32,128]{1,0:T(8,128)S(1)}) custom-call(bf16[96,128]{1,0:T(8,128)(2,1)S(1)} %get-tuple-element.38.q_ref, bf16[768,128]{1,0:T(8,128)(2,1)S(1)} %get-tuple-element.40.mine_ref, bf16[768,128]{1,0:T(8,128)(2,1)S(1)} %collective-permute-done.1.theirs_ref, ...), custom_call_target="tpu_custom_call" | custom-call | flops 37748736 | bytes 1048576 | tf_op jit(solution)/shard_map/cached_attention/pallas_call | solution.py:58
  4.7 0.9 %collective-permute-done.2.got_ref = bf16[32,768]{1,0:T(8,128)(2,1)S(1)} collective-permute-done((bf16[32,768]{1,0:T(8,128)(2,1)S(1)}, bf16[32,768]{1,0:T(8,128)(2,1)S(1)}, u32[]{:S(2)}, u32[]{:S(2)}) %collective-permute-start.2) | collective-permute-done | bytes 49184 | tf_op jit(solution)/shard_map/ppermute | solution.py:26
  5.6 2.9 %collective-permute-start.3 = (bf16[32,896]{1,0:T(8,128)(2,1)S(1)}, bf16[32,896]{1,0:T(8,128)(2,1)S(1)}, u32[]{:S(2)}, u32[]{:S(2)}) collective-permute-start(bf16[32,896]{1,0:T(8,128)(2,1)S(1)} %chip_sum.1.refs_0_.own_ref), channel_id=1, source_target_pairs={{0,2},{1,3},{2,0},{3,1},{4,6},{5,7},{6,4},{7,5},{8,10},{9,11},{10,... | collective-permute-start | bytes 172040 | tf_op jit(solution)/shard_map/ppermute | solution.py:26
  8.5 2.6 %collective-permute-start.4 = (bf16[32,896]{1,0:T(8,128)(2,1)S(1)}, bf16[32,896]{1,0:T(8,128)(2,1)S(1)}, u32[]{:S(2)}, u32[]{:S(2)}) collective-permute-start(bf16[32,896]{1,0:T(8,128)(2,1)S(1)} %chip_sum.1.refs_0_.own_ref), channel_id=1, source_target_pairs={{0,16},{4,20},{8,24},{12,28},{16,0},{20,4},{24,8},{28,12},{1,17},{... | collective-permute-start | bytes 172040 | tf_op jit(solution)/shard_map/ppermute | solution.py:26
  11.1 3.1 %load_experts.1 = (bf16[4,192,1536]{2,1,0:T(8,128)(2,1)S(1)}, bf16[4,192,1536]{2,1,0:T(8,128)(2,1)S(1)}, bf16[4,192,1536]{2,1,0:T(8,128)(2,1)S(1)}) custom-call(bf16[32,896]{1,0:T(8,128)(2,1)S(1)} %chip_sum.1.refs_0_.own_ref, bf16[4,192,1536]{2,1,0:T(8,128)(2,1)} %bitcast.6, bf16[4,192,1536]{2,1,0:T(8,128)(2,1)} %bitcast.7, bf16[4,192,1536]{2,1,0:T(8,128)(2,1)} %refs_3_.1), custom_call_target="tpu_custom_call" | custom-call | bytes 8388608 | tf_op jit(solution)/shard_map/load_experts/pallas_call | solution.py:58
  14.9 2.5 %collective-permute-done.5.xy_ref = bf16[32,896]{1,0:T(8,128)(2,1)S(1)} collective-permute-done((bf16[32,896]{1,0:T(8,128)(2,1)S(1)}, bf16[32,896]{1,0:T(8,128)(2,1)S(1)}, u32[]{:S(2)}, u32[]{:S(2)}) %collective-permute-start.5) | collective-permute-done | bytes 57376 | tf_op jit(solution)/shard_map/ppermute | solution.py:33
  17.6 1.6 %collective-permute-start.8 = (bf16[64,896]{1,0:T(8,128)(2,1)S(1)}, bf16[64,896]{1,0:T(8,128)(2,1)S(1)}, u32[]{:S(2)}, u32[]{:S(2)}) collective-permute-start(bf16[64,896]{1,0:T(8,128)(2,1)S(1)} %get-tuple-element.52.refs_0_), channel_id=1, source_target_pairs={{0,4},{4,0},{8,12},{12,8},{16,20},{20,16},{24,28},{28,24},{1,5},{5... | collective-permute-start | bytes 344072 | tf_op jit(solution)/shard_map/ppermute | solution.py:26
  19.1 1.3 %collective-permute-start.9 = (bf16[64,896]{1,0:T(8,128)(2,1)S(1)}, bf16[64,896]{1,0:T(8,128)(2,1)S(1)}, u32[]{:S(2)}, u32[]{:S(2)}) collective-permute-start(bf16[64,896]{1,0:T(8,128)(2,1)S(1)} %get-tuple-element.52.refs_0_), channel_id=1, source_target_pairs={{0,8},{4,12},{8,0},{12,4},{16,24},{20,28},{24,16},{28,20},{1,9},{5... | collective-permute-start | bytes 344072 | tf_op jit(solution)/shard_map/ppermute | solution.py:26
  21.1 1.9 %experts.2 = (bf16[4,1,64,192]{3,2,1,0:T(8,128)(2,1)S(1)}, bf16[1,64,768]{2,1,0:T(8,128)(2,1)S(1)}) custom-call(bf16[64,896]{1,0:T(8,128)(2,1)S(1)} %get-tuple-element.52.refs_0_, bf16[64,896]{1,0:T(8,128)(2,1)S(1)} %collective-permute-done.6.refs_1_, bf16[4,192,1536]{2,1,0:T(8,128)(2,1)S(1)} %get-tuple-element.51.loaded_ref.refs_2_.refs_6_, ...), custom_call_target="tpu_custom_call" | custom-call | flops 1 | bytes 1 | tf_op jit(solution)/shard_map/experts/pallas_call | solution.py:409
  23.1 2.0 %collective-permute-done.9.refs_1_ = bf16[64,896]{1,0:T(8,128)(2,1)S(1)} collective-permute-done((bf16[64,896]{1,0:T(8,128)(2,1)S(1)}, bf16[64,896]{1,0:T(8,128)(2,1)S(1)}, u32[]{:S(2)}, u32[]{:S(2)}) %collective-permute-start.9) | collective-permute-done | bytes 114720 | tf_op jit(solution)/shard_map/ppermute | solution.py:26
  25.1 1.6 %collective-permute-done.10.refs_2_ = bf16[64,896]{1,0:T(8,128)(2,1)S(1)} collective-permute-done((bf16[64,896]{1,0:T(8,128)(2,1)S(1)}, bf16[64,896]{1,0:T(8,128)(2,1)S(1)}, u32[]{:S(2)}, u32[]{:S(2)}) %collective-permute-start.10) | collective-permute-done | bytes 114720 | tf_op jit(solution)/shard_map/ppermute | solution.py:26
  27.5 0.7 %collective-permute-done.11.refs_3_ = bf16[64,896]{1,0:T(8,128)(2,1)S(1)} collective-permute-done((bf16[64,896]{1,0:T(8,128)(2,1)S(1)}, bf16[64,896]{1,0:T(8,128)(2,1)S(1)}, u32[]{:S(2)}, u32[]{:S(2)}) %collective-permute-start.11) | collective-permute-done | bytes 114720 | tf_op jit(solution)/shard_map/ppermute | solution.py:26
  28.7 1.8 %experts.3 = (bf16[4,3,64,192]{3,2,1,0:T(8,128)(2,1)S(1)}, bf16[3,64,768]{2,1,0:T(8,128)(2,1)S(1)}) custom-call(bf16[64,896]{1,0:T(8,128)(2,1)S(1)} %get-tuple-element.57.refs_0_, bf16[64,896]{1,0:T(8,128)(2,1)S(1)} %get-tuple-element.58.refs_1_, bf16[64,896]{1,0:T(8,128)(2,1)S(1)} %get-tuple-element.59.refs_2_, ...), custom_call_target="tpu_custom_call" | custom-call | flops 1 | bytes 1 | tf_op jit(solution)/shard_map/experts/pallas_call | solution.py:409
  32.2 1.6 %collective-permute-start.15 = (bf16[64,768]{1,0:T(8,128)(2,1)S(1)}, bf16[64,768]{1,0:T(8,128)(2,1)S(1)}, u32[]{:S(2)}, u32[]{:S(2)}) collective-permute-start(bf16[64,768]{1,0:T(8,128)(2,1)S(1)} %get-tuple-element.62), channel_id=1, source_target_pairs={{0,4},{4,0},{8,12},{12,8},{16,20},{20,16},{24,28},{28,24},{1,5},{5... | collective-permute-start | bytes 294920 | tf_op jit(solution)/shard_map/ppermute | solution.py:26
  33.8 1.3 %collective-permute-start.16 = (bf16[64,768]{1,0:T(8,128)(2,1)S(1)}, bf16[64,768]{1,0:T(8,128)(2,1)S(1)}, u32[]{:S(2)}, u32[]{:S(2)}) collective-permute-start(bf16[64,768]{1,0:T(8,128)(2,1)S(1)} %get-tuple-element.63), channel_id=1, source_target_pairs={{0,8},{4,12},{8,0},{12,4},{16,24},{20,28},{24,16},{28,20},{1,9},{5... | collective-permute-start | bytes 294920 | tf_op jit(solution)/shard_map/ppermute | solution.py:26
  36.2 0.9 %collective-permute-done.15.refs_1_ = bf16[64,768]{1,0:T(8,128)(2,1)S(1)} collective-permute-done((bf16[64,768]{1,0:T(8,128)(2,1)S(1)}, bf16[64,768]{1,0:T(8,128)(2,1)S(1)}, u32[]{:S(2)}, u32[]{:S(2)}) %collective-permute-start.15) | collective-permute-done | bytes 98336 | tf_op jit(solution)/shard_map/ppermute | solution.py:26
  37.1 2.3 %collective-permute-done.16.refs_2_ = bf16[64,768]{1,0:T(8,128)(2,1)S(1)} collective-permute-done((bf16[64,768]{1,0:T(8,128)(2,1)S(1)}, bf16[64,768]{1,0:T(8,128)(2,1)S(1)}, u32[]{:S(2)}, u32[]{:S(2)}) %collective-permute-start.16) | collective-permute-done | bytes 98336 | tf_op jit(solution)/shard_map/ppermute | solution.py:26
  39.4 1.2 %collective-permute-done.17.refs_3_ = bf16[64,768]{1,0:T(8,128)(2,1)S(1)} collective-permute-done((bf16[64,768]{1,0:T(8,128)(2,1)S(1)}, bf16[64,768]{1,0:T(8,128)(2,1)S(1)}, u32[]{:S(2)}, u32[]{:S(2)}) %collective-permute-start.17) | collective-permute-done | bytes 98336 | tf_op jit(solution)/shard_map/ppermute | solution.py:26
  41.3 3.1 %collective-permute-start.19 = (bf16[32,768]{1,0:T(8,128)(2,1)S(1)}, bf16[32,768]{1,0:T(8,128)(2,1)S(1)}, u32[]{:S(2)}, u32[]{:S(2)}) collective-permute-start(bf16[32,768]{1,0:T(8,128)(2,1)S(1)} %get-tuple-element.67), channel_id=1, source_target_pairs={{0,16},{4,20},{8,24},{12,28},{16,0},{20,4},{24,8},{28,12},{1,17},{... | collective-permute-start | bytes 147464 | tf_op jit(solution)/shard_map/ppermute | solution.py:26
  44.4 0.7 %collective-permute-start.20 = (bf16[32,768]{1,0:T(8,128)(2,1)S(1)}, bf16[32,768]{1,0:T(8,128)(2,1)S(1)}, u32[]{:S(2)}, u32[]{:S(2)}) collective-permute-start(bf16[32,768]{1,0:T(8,128)(2,1)S(1)} %get-tuple-element.67), channel_id=1, source_target_pairs={{0,18},{1,19},{2,16},{3,17},{4,22},{5,23},{6,20},{7,21},{8,26},{9,... | collective-permute-start | bytes 147464 | tf_op jit(solution)/shard_map/ppermute | solution.py:33
  45.1 2.7 %collective-permute-done.19.y_ref = bf16[32,768]{1,0:T(8,128)(2,1)S(1)} collective-permute-done((bf16[32,768]{1,0:T(8,128)(2,1)S(1)}, bf16[32,768]{1,0:T(8,128)(2,1)S(1)}, u32[]{:S(2)}, u32[]{:S(2)}) %collective-permute-start.19) | collective-permute-done | bytes 49184 | tf_op jit(solution)/shard_map/ppermute | solution.py:26
  47.9 2.4 %collective-permute-done.20.xy_ref = bf16[32,768]{1,0:T(8,128)(2,1)S(1)} collective-permute-done((bf16[32,768]{1,0:T(8,128)(2,1)S(1)}, bf16[32,768]{1,0:T(8,128)(2,1)S(1)}, u32[]{:S(2)}, u32[]{:S(2)}) %collective-permute-start.20) | collective-permute-done | bytes 49184 | tf_op jit(solution)/shard_map/ppermute | solution.py:33
  50.4 1.2 %collective-permute-done.21.b_ref = f32[32,128]{1,0:T(8,128)S(1)} collective-permute-done((f32[32,128]{1,0:T(8,128)S(1)}, f32[32,128]{1,0:T(8,128)S(1)}, u32[]{:S(2)}, u32[]{:S(2)}) %collective-permute-start.21) | collective-permute-done | bytes 16416 | tf_op jit(solution)/shard_map/ppermute | solution.py:26
  (44 shorter events, 8.5 us)
Async XLA Ops:
  0.0 11.1 %copy-start.1 = (bf16[1536]{0:T(1024)(128)(2,1)S(1)}, bf16[1536]{0:T(1024)(128)(2,1)}, u32[]{:S(2)}) copy-start(bf16[1536]{0:T(1024)(128)(2,1)} %param.28) | copy-start | bytes 9220
  0.0 2.7 %collective-permute-start.1 = (bf16[768,128]{1,0:T(8,128)(2,1)}, bf16[768,128]{1,0:T(8,128)(2,1)S(1)}, u32[]{:S(2)}, u32[]{:S(2)}) collective-permute-start(bf16[768,128]{1,0:T(8,128)(2,1)} %bitcast.8), channel_id=1, source_target_pairs={{0,1},{1,0},{2,3},{3,2},{4,5},{5,4},{6,7},{7,6},{8,9},{9,8},{10,11... | collective-permute-start | bytes 589832 | tf_op jit(solution)/shard_map/ppermute | solution.py:26
  2.5 1.4 %collective-permute-start = (bf16[32,128]{1,0:T(8,128)(2,1)S(1)}, bf16[32,128]{1,0:T(8,128)(2,1)S(1)}, u32[]{:S(2)}, u32[]{:S(2)}) collective-permute-start(bf16[32,128]{1,0:T(8,128)(2,1)S(1)} %get-tuple-element.39.mine_ref), channel_id=1, source_target_pairs={{0,1},{1,0},{2,3},{3,2},{4,5},{5,4},{6,7},{7,6},{8,9},{9,8},{10,11... | collective-permute-start | bytes 24584 | tf_op jit(solution)/shard_map/ppermute | solution.py:26
  4.3 1.3 %collective-permute-start.2 = (bf16[32,768]{1,0:T(8,128)(2,1)S(1)}, bf16[32,768]{1,0:T(8,128)(2,1)S(1)}, u32[]{:S(2)}, u32[]{:S(2)}) collective-permute-start(bf16[32,768]{1,0:T(8,128)(2,1)S(1)} %get-tuple-element.50), channel_id=1, source_target_pairs={{0,1},{1,0},{2,3},{3,2},{4,5},{5,4},{6,7},{7,6},{8,9},{9,8},{10,11... | collective-permute-start | bytes 147464 | tf_op jit(solution)/shard_map/ppermute | solution.py:26
  5.6 8.6 %collective-permute-start.3 = (bf16[32,896]{1,0:T(8,128)(2,1)S(1)}, bf16[32,896]{1,0:T(8,128)(2,1)S(1)}, u32[]{:S(2)}, u32[]{:S(2)}) collective-permute-start(bf16[32,896]{1,0:T(8,128)(2,1)S(1)} %chip_sum.1.refs_0_.own_ref), channel_id=1, source_target_pairs={{0,2},{1,3},{2,0},{3,1},{4,6},{5,7},{6,4},{7,5},{8,10},{9,11},{10,... | collective-permute-start | bytes 172040 | tf_op jit(solution)/shard_map/ppermute | solution.py:26
  8.5 6.3 %collective-permute-start.4 = (bf16[32,896]{1,0:T(8,128)(2,1)S(1)}, bf16[32,896]{1,0:T(8,128)(2,1)S(1)}, u32[]{:S(2)}, u32[]{:S(2)}) collective-permute-start(bf16[32,896]{1,0:T(8,128)(2,1)S(1)} %chip_sum.1.refs_0_.own_ref), channel_id=1, source_target_pairs={{0,16},{4,20},{8,24},{12,28},{16,0},{20,4},{24,8},{28,12},{1,17},{... | collective-permute-start | bytes 172040 | tf_op jit(solution)/shard_map/ppermute | solution.py:26
  11.1 6.2 %collective-permute-start.5 = (bf16[32,896]{1,0:T(8,128)(2,1)S(1)}, bf16[32,896]{1,0:T(8,128)(2,1)S(1)}, u32[]{:S(2)}, u32[]{:S(2)}) collective-permute-start(bf16[32,896]{1,0:T(8,128)(2,1)S(1)} %chip_sum.1.refs_0_.own_ref), channel_id=1, source_target_pairs={{0,18},{1,19},{2,16},{3,17},{4,22},{5,23},{6,20},{7,21},{8,26},{9,... | collective-permute-start | bytes 172040 | tf_op jit(solution)/shard_map/ppermute | solution.py:33
  17.5 3.6 %collective-permute-start.6 = (bf16[64,896]{1,0:T(8,128)(2,1)S(1)}, bf16[64,896]{1,0:T(8,128)(2,1)S(1)}, u32[]{:S(2)}, u32[]{:S(2)}) collective-permute-start(bf16[64,896]{1,0:T(8,128)(2,1)S(1)} %get-tuple-element.52.refs_0_), channel_id=1, source_target_pairs={{0,1},{1,0},{2,3},{3,2},{4,5},{5,4},{6,7},{7,6},{8,9},{9,8},{10,11... | collective-permute-start | bytes 344072 | tf_op jit(solution)/shard_map/ppermute | solution.py:26
  17.6 5.6 %collective-permute-start.8 = (bf16[64,896]{1,0:T(8,128)(2,1)S(1)}, bf16[64,896]{1,0:T(8,128)(2,1)S(1)}, u32[]{:S(2)}, u32[]{:S(2)}) collective-permute-start(bf16[64,896]{1,0:T(8,128)(2,1)S(1)} %get-tuple-element.52.refs_0_), channel_id=1, source_target_pairs={{0,4},{4,0},{8,12},{12,8},{16,20},{20,16},{24,28},{28,24},{1,5},{5... | collective-permute-start | bytes 344072 | tf_op jit(solution)/shard_map/ppermute | solution.py:26
  19.1 6.0 %collective-permute-start.9 = (bf16[64,896]{1,0:T(8,128)(2,1)S(1)}, bf16[64,896]{1,0:T(8,128)(2,1)S(1)}, u32[]{:S(2)}, u32[]{:S(2)}) collective-permute-start(bf16[64,896]{1,0:T(8,128)(2,1)S(1)} %get-tuple-element.52.refs_0_), channel_id=1, source_target_pairs={{0,8},{4,12},{8,0},{12,4},{16,24},{20,28},{24,16},{28,20},{1,9},{5... | collective-permute-start | bytes 344072 | tf_op jit(solution)/shard_map/ppermute | solution.py:26
  20.5 6.3 %collective-permute-start.10 = (bf16[64,896]{1,0:T(8,128)(2,1)S(1)}, bf16[64,896]{1,0:T(8,128)(2,1)S(1)}, u32[]{:S(2)}, u32[]{:S(2)}) collective-permute-start(bf16[64,896]{1,0:T(8,128)(2,1)S(1)} %get-tuple-element.52.refs_0_), channel_id=1, source_target_pairs={{0,12},{4,8},{8,4},{12,0},{16,28},{20,24},{24,20},{28,16},{1,13},{... | collective-permute-start | bytes 344072 | tf_op jit(solution)/shard_map/ppermute | solution.py:26
  26.8 1.4 %collective-permute-start.11 = (bf16[64,896]{1,0:T(8,128)(2,1)S(1)}, bf16[64,896]{1,0:T(8,128)(2,1)S(1)}, u32[]{:S(2)}, u32[]{:S(2)}) collective-permute-start(bf16[64,896]{1,0:T(8,128)(2,1)S(1)} %get-tuple-element.57.refs_0_), channel_id=1, source_target_pairs={{0,1},{1,0},{2,3},{3,2},{4,5},{5,4},{6,7},{7,6},{8,9},{9,8},{10,11... | collective-permute-start | bytes 344072 | tf_op jit(solution)/shard_map/ppermute | solution.py:26
  26.9 1.5 %collective-permute-start.12 = (bf16[64,896]{1,0:T(8,128)(2,1)S(1)}, bf16[64,896]{1,0:T(8,128)(2,1)S(1)}, u32[]{:S(2)}, u32[]{:S(2)}) collective-permute-start(bf16[64,896]{1,0:T(8,128)(2,1)S(1)} %get-tuple-element.58.refs_1_), channel_id=1, source_target_pairs={{0,1},{1,0},{2,3},{3,2},{4,5},{5,4},{6,7},{7,6},{8,9},{9,8},{10,11... | collective-permute-start | bytes 344072 | tf_op jit(solution)/shard_map/ppermute | solution.py:26
  27.4 1.3 %collective-permute-start.13 = (bf16[64,896]{1,0:T(8,128)(2,1)S(1)}, bf16[64,896]{1,0:T(8,128)(2,1)S(1)}, u32[]{:S(2)}, u32[]{:S(2)}) collective-permute-start(bf16[64,896]{1,0:T(8,128)(2,1)S(1)} %get-tuple-element.59.refs_2_), channel_id=1, source_target_pairs={{0,1},{1,0},{2,3},{3,2},{4,5},{5,4},{6,7},{7,6},{8,9},{9,8},{10,11... | collective-permute-start | bytes 344072 | tf_op jit(solution)/shard_map/ppermute | solution.py:26
  30.5 1.6 %collective-permute-start.14 = (bf16[3,64,768]{2,1,0:T(8,128)(2,1)S(1)}, bf16[3,64,768]{2,1,0:T(8,128)(2,1)S(1)}, u32[]{:S(2)}, u32[]{:S(2)}) collective-permute-start(bf16[3,64,768]{2,1,0:T(8,128)(2,1)S(1)} %get-tuple-element.61), channel_id=1, source_target_pairs={{0,1},{1,0},{2,3},{3,2},{4,5},{5,4},{6,7},{7,6},{8,9},{9,8},{10,11... | collective-permute-start | bytes 884744 | tf_op jit(solution)/shard_map/ppermute | solution.py:26
  30.7 5.4 %collective-permute-start.7 = (bf16[1,64,768]{2,1,0:T(8,128)(2,1)S(1)}, bf16[1,64,768]{2,1,0:T(8,128)(2,1)S(1)}, u32[]{:S(2)}, u32[]{:S(2)}) collective-permute-start(bf16[1,64,768]{2,1,0:T(8,128)(2,1)S(1)} %get-tuple-element.56.refs_3_), channel_id=1, source_target_pairs={{0,1},{1,0},{2,3},{3,2},{4,5},{5,4},{6,7},{7,6},{8,9},{9,8},{10,11... | collective-permute-start | bytes 294920 | tf_op jit(solution)/shard_map/ppermute | solution.py:26
  31.7 18.8 %copy-start.2 = (bf16[384]{0:T(512)(128)(2,1)S(1)}, bf16[384]{0:T(512)(128)(2,1)}, u32[]{:S(2)}) copy-start(bf16[384]{0:T(512)(128)(2,1)} %param.35) | copy-start | bytes 2308
  32.2 4.9 %collective-permute-start.15 = (bf16[64,768]{1,0:T(8,128)(2,1)S(1)}, bf16[64,768]{1,0:T(8,128)(2,1)S(1)}, u32[]{:S(2)}, u32[]{:S(2)}) collective-permute-start(bf16[64,768]{1,0:T(8,128)(2,1)S(1)} %get-tuple-element.62), channel_id=1, source_target_pairs={{0,4},{4,0},{8,12},{12,8},{16,20},{20,16},{24,28},{28,24},{1,5},{5... | collective-permute-start | bytes 294920 | tf_op jit(solution)/shard_map/ppermute | solution.py:26
  33.8 5.6 %collective-permute-start.16 = (bf16[64,768]{1,0:T(8,128)(2,1)S(1)}, bf16[64,768]{1,0:T(8,128)(2,1)S(1)}, u32[]{:S(2)}, u32[]{:S(2)}) collective-permute-start(bf16[64,768]{1,0:T(8,128)(2,1)S(1)} %get-tuple-element.63), channel_id=1, source_target_pairs={{0,8},{4,12},{8,0},{12,4},{16,24},{20,28},{24,16},{28,20},{1,9},{5... | collective-permute-start | bytes 294920 | tf_op jit(solution)/shard_map/ppermute | solution.py:26
  35.1 5.5 %collective-permute-start.17 = (bf16[64,768]{1,0:T(8,128)(2,1)S(1)}, bf16[64,768]{1,0:T(8,128)(2,1)S(1)}, u32[]{:S(2)}, u32[]{:S(2)}) collective-permute-start(bf16[64,768]{1,0:T(8,128)(2,1)S(1)} %get-tuple-element.64), channel_id=1, source_target_pairs={{0,12},{4,8},{8,4},{12,0},{16,28},{20,24},{24,20},{28,16},{1,13},{... | collective-permute-start | bytes 294920 | tf_op jit(solution)/shard_map/ppermute | solution.py:26
  40.7 4.5 %collective-permute-start.18 = (bf16[32,768]{1,0:T(8,128)(2,1)S(1)}, bf16[32,768]{1,0:T(8,128)(2,1)S(1)}, u32[]{:S(2)}, u32[]{:S(2)}) collective-permute-start(bf16[32,768]{1,0:T(8,128)(2,1)S(1)} %get-tuple-element.66), channel_id=1, source_target_pairs={{0,2},{1,3},{2,0},{3,1},{4,6},{5,7},{6,4},{7,5},{8,10},{9,11},{10,... | collective-permute-start | bytes 147464 | tf_op jit(solution)/shard_map/ppermute | solution.py:26
  41.3 6.6 %collective-permute-start.19 = (bf16[32,768]{1,0:T(8,128)(2,1)S(1)}, bf16[32,768]{1,0:T(8,128)(2,1)S(1)}, u32[]{:S(2)}, u32[]{:S(2)}) collective-permute-start(bf16[32,768]{1,0:T(8,128)(2,1)S(1)} %get-tuple-element.67), channel_id=1, source_target_pairs={{0,16},{4,20},{8,24},{12,28},{16,0},{20,4},{24,8},{28,12},{1,17},{... | collective-permute-start | bytes 147464 | tf_op jit(solution)/shard_map/ppermute | solution.py:26
  44.4 5.9 %collective-permute-start.20 = (bf16[32,768]{1,0:T(8,128)(2,1)S(1)}, bf16[32,768]{1,0:T(8,128)(2,1)S(1)}, u32[]{:S(2)}, u32[]{:S(2)}) collective-permute-start(bf16[32,768]{1,0:T(8,128)(2,1)S(1)} %get-tuple-element.67), channel_id=1, source_target_pairs={{0,18},{1,19},{2,16},{3,17},{4,22},{5,23},{6,20},{7,21},{8,26},{9,... | collective-permute-start | bytes 147464 | tf_op jit(solution)/shard_map/ppermute | solution.py:33
  50.4 1.2 %collective-permute-start.21 = (f32[32,128]{1,0:T(8,128)S(1)}, f32[32,128]{1,0:T(8,128)S(1)}, u32[]{:S(2)}, u32[]{:S(2)}) collective-permute-start(f32[32,128]{1,0:T(8,128)S(1)} %get-tuple-element.70.a_ref), channel_id=1, source_target_pairs={{0,1},{1,0},{2,3},{3,2},{4,5},{5,4},{6,7},{7,6},{8,9},{9,8},{10,11... | collective-permute-start | bytes 49160 | tf_op jit(solution)/shard_map/ppermute | solution.py:26
  (1 other events, 3.9 us)

commit v4 on v3

--- a/solution.py
+++ b/solution.py
@@ -74,8 +74,8 @@
 
 def spread(rows, values):
     index = iota((rows, LANES), 0)
-    total = jnp.full((rows, LANES), values[0], I32)
-    for i in range(1, rows):
+    total = jnp.full((rows, LANES), values[0])
+    for i in range(1, len(values)):
         total = jnp.where(index == i, values[i], total)
     return total
 
@@ -89,18 +89,19 @@
 
 
 def project_body(
-    length_hbm, group_hbm, offset_hbm, tok_hbm, gain_hbm, kvw_hbm, qw_hbm, cache_hbm,
-    q_ref, own_ref, cache_ref, token_ref, group_out, length_out, position_out,
-    length_ref, group_ref, offset_ref, tok_ref, gain_ref, kvw_ref, qw_ref, sems,
+    length_hbm, group_hbm, offset_hbm, tok_hbm, gain_hbm, kvw_hbm, qw_hbm, cache_hbm, routes_hbm, weight_hbm,
+    slot_hbm, sink_hbm,
+    q_ref, own_ref, normed_ref, cosine_ref, sine_ref, cache_ref, token_ref, group_out, length_out, position_out,
+    sink_out, routes_ref, weight_ref, slot_ref,
+    length_ref, group_ref, offset_ref, sink_ref, tok_ref, gain_ref, kvw_ref, qw_ref, sems,
 ):
     rows, width = tok_ref.shape
-    part = width // CHUNKS
     pairs = [
         (length_hbm, length_ref), (group_hbm, group_ref), (offset_hbm, offset_ref), (tok_hbm, tok_ref),
-        (gain_hbm, gain_ref), (kvw_hbm.at[0], kvw_ref),
+        (gain_hbm, gain_ref), (kvw_hbm.at[0], kvw_ref), (routes_hbm, routes_ref), (weight_hbm, weight_ref),
+        (slot_hbm, slot_ref), (sink_hbm, sink_ref),
     ]
-    pairs += [(qw_hbm.at[pl.ds(i * part, part)], qw_ref.at[pl.ds(i * part, part)]) for i in range(CHUNKS)]
-    pairs += [(cache_hbm.at[0, 0], cache_ref)]
+    pairs += [(qw_hbm, qw_ref), (cache_hbm.at[0, 0], cache_ref)]
     loads = [pltpu.make_async_copy(src, dst, sems.at[i]) for i, (src, dst) in enumerate(pairs)]
     for load in loads:
         load.start()
@@ -122,6 +123,8 @@
     cosine = jnp.cos(angle)
     sine = jnp.sin(angle)
     sine = jnp.where(lane < half, -sine, sine)
+    cosine_ref[...] = cosine
+    sine_ref[...] = sine
     loads[3].wait()
     loads[4].wait()
     tok = tok_ref[...].astype(F32)
@@ -132,60 +135,24 @@
         token_ref[:, i * quarter : (i + 1) * quarter] = jnp.where(
             is_first(), jnp.where(is_key(), low, high), 0.0
         )
+    normed_ref[...] = normed
+    loads[9].wait()
+    sink_out[...] = spread(sink_out.shape[0], [sink_ref[i] for i in range(heads)])
     loads[5].wait()
     own = dot(normed, kvw_ref[...])
     turned = own * cosine + pltpu.roll(own, half, 1) * sine
     own_ref[...] = jnp.where(is_key(), turned, own).astype(BF16)
-    q = None
-    for i in range(CHUNKS):
-        loads[6 + i].wait()
-        part_sum = dot(normed[:, i * part : (i + 1) * part], qw_ref[i * part : (i + 1) * part, :])
-        q = part_sum if q is None else q + part_sum
+    loads[10].wait()
+    q = dot(normed, qw_ref[...])
     for h in range(heads):
         head = q[:, h * dim : (h + 1) * dim]
         q_ref[h * rows : (h + 1) * rows, :] = (head * cosine + pltpu.roll(head, half, 1) * sine).astype(BF16)
-    loads[-1].wait()
-
-
-def cached_body(
-    q_ref, mine_ref, theirs_ref, group_ref, length_ref, position_ref, sink_hbm, routes_hbm, weight_hbm, slot_hbm,
-    sums_ref, tops_ref, parts_ref, extra_ref, sink_ref, routes_ref, weight_ref, slot_ref, sems,
-):
-    pairs = [(sink_hbm, sink_ref), (routes_hbm, routes_ref), (weight_hbm, weight_ref), (slot_hbm, slot_ref)]
-    loads = [pltpu.make_async_copy(src, dst, sems.at[i]) for i, (src, dst) in enumerate(pairs)]
-    for load in loads:
-        load.start()
-    rows = group_ref.shape[0]
-    dim = q_ref.shape[1]
-    heads = q_ref.shape[0] // rows
-    slots = mine_ref.shape[0]
-    scale = 1.0 / dim**0.5
-    mine, theirs = mine_ref[...], theirs_ref[...]
-    keys = jnp.where(is_key(), mine, theirs)
-    values = jnp.where(is_key(), theirs, mine)
-    scores = dot_t(q_ref[...], keys)
-    group, row_length, position = group_ref[...], length_ref[...], position_ref[...]
-    lane = iota((rows, LANES), 1)
-    seen = []
-    for start in range(0, slots, LANES):
-        place = lane + start % PROMPT_CAP
-        seen.append((group == start // PROMPT_CAP) & (place < row_length) & (place > position - WINDOW))
-    for load in loads:
+    for load in loads[6:9] + loads[11:]:
         load.wait()
-    probs = []
-    for h in range(heads):
-        span = slice(h * rows, (h + 1) * rows)
-        masked = [
-            jnp.where(seen[k], scores[span, k * LANES : (k + 1) * LANES] * scale, HIDE) for k in range(len(seen))
-        ]
-        top = functools.reduce(jnp.maximum, masked)
-        top = jnp.maximum(jnp.max(top, axis=1, keepdims=True), sink_ref[h])
-        part = [jnp.exp(m - top) for m in masked]
-        total = jnp.sum(functools.reduce(jnp.add, part), axis=1, keepdims=True) + jnp.exp(sink_ref[h] - top)
-        probs.append(jnp.concatenate([p.astype(BF16) for p in part], axis=1))
-        tops_ref[span, :] = jnp.broadcast_to(top, (rows, LANES))
-        parts_ref[span, :] = jnp.broadcast_to(total, (rows, LANES))
-    sums_ref[...] = dot(jnp.concatenate(probs, axis=0), values)
+
+
+def extra_body(routes_ref, weight_ref, slot_ref, sent_ref, extra_ref):
+    rows = routes_ref.shape[1]
     copies = slot_ref.shape[1]
     replicas = copies // EXPERTS
     block = iota((copies, rows), 1) // (rows // replicas)
@@ -198,64 +165,86 @@
     high = chosen.astype(BF16)
     low = (chosen - high.astype(F32)).astype(BF16)
     extra_ref[...] = jnp.zeros(extra_ref.shape, F32)
-    for i, part in enumerate((high, low)):
-        moved = lax.dot_general(part, order, (((0,), (1,)), ((), ())), preferred_element_type=F32)
+    for i, term in enumerate((high, low)):
+        moved = lax.dot_general(term, order, (((0,), (1,)), ((), ())), preferred_element_type=F32)
         extra_ref[:, i * copies : (i + 1) * copies] = jnp.where(is_first(), moved, 0.0)
 
 
 def attend_body(
-    q_ref, mine_ref, theirs_ref, sums_ref, tops_ref, parts_ref, out_ref, token_ref, extra_ref, send_ref, keep_ref
+    q_ref, own_ref, normed_ref, other_ref, cosine_ref, sine_ref, mine_ref, theirs_ref, group_ref, length_ref,
+    position_ref, sink_ref, out_ref, token_ref, send_ref, keep_ref,
 ):
-    rows, dim = mine_ref.shape
+    rows, dim = own_ref.shape
     heads = q_ref.shape[0] // rows
+    slots = mine_ref.shape[0]
     quarter = send_ref.shape[1] // 2
     scale = 1.0 / dim**0.5
-    mine, theirs = mine_ref[...].astype(F32), theirs_ref[...].astype(F32)
-    key = jnp.where(is_key(), mine, theirs)
-    value = jnp.where(is_key(), theirs, mine)
-    context = []
+    mine, theirs = mine_ref[...], theirs_ref[...]
+    keys = jnp.where(is_key(), mine, theirs)
+    values = jnp.where(is_key(), theirs, mine)
+    scores = dot_t(q_ref[...], keys)
+    other = dot(normed_ref[...], other_ref[...])
+    turned = other * cosine_ref[...] + pltpu.roll(other, dim // 2, 1) * sine_ref[...]
+    other = jnp.where(is_key(), other, turned).astype(BF16).astype(F32)
+    own = own_ref[...].astype(F32)
+    key = jnp.where(is_key(), own, other)
+    value = jnp.where(is_key(), other, own)
+    group, row_length, position = group_ref[...], length_ref[...], position_ref[...]
+    lane = iota((rows, LANES), 1)
+    seen = []
+    for start in range(0, slots, LANES):
+        place = lane + start % PROMPT_CAP
+        seen.append((group == start // PROMPT_CAP) & (place < row_length) & (place > position - WINDOW))
+    probs, own_probs = [], []
     for h in range(heads):
         span = slice(h * rows, (h + 1) * rows)
+        masked = [
+            jnp.where(seen[k], scores[span, k * LANES : (k + 1) * LANES] * scale, HIDE) for k in range(len(seen))
+        ]
+        sink = sink_ref[h : h + 1, :1]
         score = jnp.sum(q_ref[span, :].astype(F32) * key, axis=1, keepdims=True) * scale
-        top = jnp.maximum(tops_ref[span, :], score)
-        old = jnp.exp(tops_ref[span, :] - top)
-        own = jnp.exp(score - top)
-        inverse = 1.0 / (parts_ref[span, :] * old + own)
-        context.append(((sums_ref[span, :] * old + own * value) * inverse).astype(BF16))
+        top = jnp.max(functools.reduce(jnp.maximum, masked), axis=1, keepdims=True)
+        top = jnp.maximum(jnp.maximum(top, score), sink)
+        part = [jnp.exp(m - top) for m in masked]
+        fresh = jnp.exp(score - top)
+        total = jnp.sum(functools.reduce(jnp.add, part), axis=1, keepdims=True) + fresh + jnp.exp(sink - top)
+        inverse = 1.0 / total
+        probs.append(jnp.concatenate([(p * inverse).astype(BF16) for p in part], axis=1))
+        own_probs.append((fresh * inverse).astype(BF16).astype(F32))
+    cached = dot(jnp.concatenate(probs, axis=0), values)
+    context = [
+        (cached[h * rows : (h + 1) * rows] + own_probs[h] * value).astype(BF16) for h in range(heads)
+    ]
     attended = dot(jnp.concatenate(context, axis=1), out_ref[...])
     part = [attended[:, i * quarter : (i + 1) * quarter] for i in range(4)]
     for i in range(2):
         span = slice(i * quarter, (i + 1) * quarter)
         send_ref[:, span] = jnp.where(is_key(), part[2 * i + 1], part[2 * i]).astype(BF16)
         keep_ref[:, span] = jnp.where(is_key(), part[2 * i], part[2 * i + 1]) + token_ref[:, span]
-    keep_ref[:, 2 * quarter :] = extra_ref[...]
-
-
-def chip_body(keep_ref, got_ref, out_ref):
+
+
+def chip_body(keep_ref, extra_ref, got_ref, out_ref):
     width = got_ref.shape[1]
-    out_ref[:, :width] = (keep_ref[:, :width] + got_ref[...].astype(F32)).astype(BF16)
-    out_ref[:, width:] = keep_ref[:, width:].astype(BF16)
-
-
-def relay_body(count, *refs):
-    for src, dst in zip(refs[:count], refs[-count:]):
-        dst[...] = src[...]
-
-
-def after_all(blocks, earlier):
-    tall, total = blocks[0].shape
+    out_ref[:, :width] = (keep_ref[...] + got_ref[...].astype(F32)).astype(BF16)
+    out_ref[:, width:] = extra_ref[...].astype(BF16)
+
+
+def relay_body(block_ref, *refs):
+    refs[-1][...] = block_ref[...]
+
+
+def after_all(block, earlier):
     return call(
-        functools.partial(relay_body, len(blocks)),
-        [shape(b.shape, b.dtype) for b in blocks],
-        (*blocks, *earlier),
-        free=range(len(blocks), len(blocks) + len(earlier)),
-        vmem=16 << 20,
+        relay_body,
+        shape(block.shape, block.dtype),
+        (block, *earlier),
+        free=range(1, 1 + len(earlier)),
         name="relay",
-        cost=(len(blocks) * tall * total, 1 << 18),
-    )
-
-
-def residual_body(copies, gain_ref, own_ref, x_ref, y_ref, xy_ref, loaded_ref, rows_ref, keep_ref):
+        cost=(block.size, 1 << 17),
+    )
+
+
+def residual_body(copies, gain_ref, own_ref, y_ref, xy_ref, x_ref, loaded_ref, rows_ref, keep_ref):
     rows, total = own_ref.shape
     width = keep_ref.shape[1]
     quarter = width // 2
@@ -285,19 +274,22 @@
     count = (len(refs) - 2) // 2
     loads = []
     for src, dst in zip(refs[1 : 1 + count], refs[1 + count : -1]):
-        for j in range(src.shape[0]):
-            loads.append(pltpu.make_async_copy(src.at[j], dst.at[j], sems.at[len(loads)]))
+        tall = src.shape[0] // CHUNKS
+        for k in range(CHUNKS):
+            part = pl.ds(k * tall, tall)
+            loads.append(pltpu.make_async_copy(src.at[part], dst.at[part], sems.at[len(loads)]))
     for load in loads:
         load.start()
     for load in loads:
         load.wait()
 
 
-def expert_body(copies, blocks, *refs):
+def expert_body(copies, hosted, blocks, *refs):
     own_refs, other_refs = refs[:blocks], refs[blocks : 2 * blocks]
     gate_ref, up_ref, down_ref = refs[2 * blocks : 2 * blocks + 3]
     hidden_ref, send_ref = refs[-2:]
-    hosted, units, width = gate_ref.shape
+    width = gate_ref.shape[1]
+    units = gate_ref.shape[0] // hosted
     quarter = width // 4
     own = jnp.concatenate([r[...] for r in own_refs], axis=0)
     other = jnp.concatenate([r[...] for r in other_refs], axis=0)
@@ -312,39 +304,32 @@
     squares = jnp.where((lane == 2 * copies) | (lane == 2 * copies + 1), extra + other[:, 2 * quarter :].astype(F32), 0.0)
     scale = lax.rsqrt(jnp.sum(squares, axis=1, keepdims=True) / width + EPSILON)
     tall = rows.shape[0] // blocks
-    hiddens = []
+    parts = []
     for j in range(hosted):
         slot = lax.axis_index("expert") * hosted + j
-        weight = jnp.where((lane == slot) | (lane == slot + copies), extra, 0.0)
-        weight = jnp.sum(weight, axis=1, keepdims=True)
-        gate = dot_t(rows, gate_ref[j]) * scale
-        up = dot_t(rows, up_ref[j]) * scale
-        hidden = (jnp.maximum(gate, 0.0) * up * weight).astype(BF16)
-        hiddens.append(hidden)
-        for b in range(blocks):
-            hidden_ref[j, b] = hidden[b * tall : (b + 1) * tall]
+        one = jnp.where((lane == slot) | (lane == slot + copies), extra, 0.0)
+        weight = jnp.sum(one, axis=1, keepdims=True)
+        span = slice(j * units, (j + 1) * units)
+        gate = dot_t(rows, gate_ref[span, :]) * scale
+        up = dot_t(rows, up_ref[span, :]) * scale
+        parts.append((jnp.maximum(gate, 0.0) * up * weight).astype(BF16))
+    hidden = jnp.concatenate(parts, axis=1)
+    for b in range(blocks):
+        hidden_ref[b] = hidden[b * tall : (b + 1) * tall]
     for k in range(2):
         start = pl.multiple_of((2 * k + 1 - lax.axis_index("tensor") % 2) * quarter, LANES)
-        total = None
-        for j in range(hosted):
-            part = dot(hiddens[j], down_ref[j, :, pl.ds(start, quarter)])
-            total = part if total is None else total + part
-        total = total.astype(BF16)
+        total = dot(hidden, down_ref[:, pl.ds(start, quarter)]).astype(BF16)
         for b in range(blocks):
             send_ref[b, :, k * quarter : (k + 1) * quarter] = total[b * tall : (b + 1) * tall]
 
 
 def keep_body(blocks, hidden_ref, down_ref, out_ref):
-    hosted = down_ref.shape[0]
-    quarter = down_ref.shape[2] // 4
-    tall = hidden_ref.shape[2]
-    hiddens = [jnp.concatenate([hidden_ref[j, b] for b in range(blocks)], axis=0) for j in range(hosted)]
+    quarter = down_ref.shape[1] // 4
+    tall = hidden_ref.shape[1]
+    hidden = jnp.concatenate([hidden_ref[b] for b in range(blocks)], axis=0)
     for k in range(2):
         start = pl.multiple_of((2 * k + lax.axis_index("tensor") % 2) * quarter, LANES)
-        total = None
-        for j in range(hosted):
-            part = dot(hiddens[j], down_ref[j, :, pl.ds(start, quarter)])
-            total = part if total is None else total + part
+        total = dot(hidden, down_ref[:, pl.ds(start, quarter)])
         for b in range(blocks):
             out_ref[b, :, k * quarter : (k + 1) * quarter] = total[b * tall : (b + 1) * tall]
 
@@ -388,10 +373,10 @@
     out_ref[...] = (combined_ref[...] * lax.rsqrt(mean + EPSILON) * gain_ref[...].astype(F32)).astype(BF16)
 
 
-def run_experts(own, other, gate_weight, up_weight, down_weight, copies, first):
+def run_experts(own, other, gate_weight, up_weight, down_weight, hosted, copies, first):
     blocks = len(own)
     tall, total = own[0].shape
-    hosted, units, width = gate_weight.shape
+    units, width = gate_weight.shape
     step = min(tall, 64)
     grid = (tall // step,) if tall > step else ()
 
@@ -402,14 +387,13 @@
 
     row_spec = spec((step, total), lambda i: (i, 0))
     half_spec = spec((blocks, step, width // 2), lambda i: (0, i, 0))
-    hidden_spec = spec((hosted, blocks, step, units), lambda i: (0, 0, i, 0))
+    hidden_spec = spec((blocks, step, units), lambda i: (0, i, 0))
     whole = pl.BlockSpec(memory_space=pltpu.VMEM)
     params = pltpu.CompilerParams(vmem_limit_bytes=32 << 20)
-    flops = 2 * blocks * tall * hosted * width * units
     hidden, send = pl.pallas_call(
-        functools.partial(expert_body, copies, blocks),
+        functools.partial(expert_body, copies, hosted, blocks),
         grid=grid,
-        out_shape=[shape((hosted, blocks, tall, units), BF16), shape((blocks, tall, width // 2), BF16)],
+        out_shape=[shape((blocks, tall, units), BF16), shape((blocks, tall, width // 2), BF16)],
         in_specs=[row_spec] * (2 * blocks) + [whole] * 3,
         out_specs=[hidden_spec, half_spec],
         compiler_params=params,
@@ -435,7 +419,7 @@
         name="chip_sums",
         cost=(1, 1),
     )
-    return list(sums), send
+    return list(sums), send, got
 
 
 def on_device(
@@ -451,78 +435,74 @@
     copies = copy_slot.shape[0]
     far = lax.axis_size("expert") // 2
     extra_width = -(-(2 * copies + 2) // LANES) * LANES
-    gate_weight = jnp.swapaxes(gate_weight, 1, 2)
-    up_weight = jnp.swapaxes(up_weight, 1, 2)
+    hosted = gate_weight.shape[0]
+    gate_weight = jnp.swapaxes(gate_weight, 1, 2).reshape(-1, width)
+    up_weight = jnp.swapaxes(up_weight, 1, 2).reshape(-1, width)
+    down_weight = down_weight.reshape(-1, width)
 
     other_cache = swap(paired_cache[0, 0], "tensor", 1)
+    other_weight = swap(key_value_weight[0], "tensor", 1)
     place = shape((rows, LANES), I32)
-    queries, own_new, own_cache, token_half, *places = call(
+    turn = shape((rows, dim), F32)
+    queries, own_new, normed, cosine, sine, own_cache, token_half, *rest, named, named_weight, slot = call(
         project_body,
         [
-            shape((heads * rows, dim), BF16), shape((rows, dim), BF16), shape((slots, dim), BF16),
-            shape((rows, half), F32), place, place, place,
+            shape((heads * rows, dim), BF16), shape((rows, dim), BF16), shape((rows, width), BF16), turn, turn,
+            shape((slots, dim), BF16), shape((rows, half), F32), place, place, place, shape((8, LANES), F32),
+            shape((TOP, rows), I32), shape((TOP, rows), F32), shape((1, copies), I32),
         ],
         (
             prompt_length, group_index, offsets, tokens, attn_gain, key_value_weight, query_weight,
-            paired_cache,
+            paired_cache, routes.T, route_weight.T, copy_slot[None, :], sink_logit,
         ),
-        hbm=range(8),
+        hbm=range(12),
         scratch=[
             pltpu.SMEM(prompt_length.shape, I32),
             pltpu.SMEM(group_index.shape, I32),
             pltpu.SMEM(offsets.shape, I32),
+            pltpu.SMEM(sink_logit.shape, F32),
             pltpu.VMEM(tokens.shape, BF16),
             pltpu.VMEM((width,), BF16),
             pltpu.VMEM(key_value_weight.shape[1:], BF16),
             pltpu.VMEM(query_weight.shape, BF16),
-            pltpu.SemaphoreType.DMA((7 + CHUNKS,)),
+            pltpu.SemaphoreType.DMA((12,)),
         ],
         name="project",
         cost=(2 * rows * width * (heads + 1) * dim, 2 << 20),
     )
-    other_new = swap(own_new, "tensor", 1)
-    sums, tops, parts, extra = call(
-        cached_body,
-        [shape((heads * rows, dim), F32)] + [shape((heads * rows, LANES), F32)] * 2 + [shape((rows, extra_width), F32)],
-        (
-            queries, own_cache, other_cache, *places, sink_logit, routes.T, route_weight.T, copy_slot[None, :],
-        ),
-        hbm=range(6, 10),
-        scratch=[
-            pltpu.SMEM(sink_logit.shape, F32),
-            pltpu.VMEM((TOP, rows), I32),
-            pltpu.VMEM((TOP, rows), F32),
-            pltpu.VMEM((1, copies), I32),
-            pltpu.SemaphoreType.DMA((4,)),
-        ],
-        name="cached_attention",
-        cost=(4 * heads * rows * dim * slots, 1 << 20),
-    )
     send, keep = call(
         attend_body,
-        [shape((rows, half), BF16), shape((rows, half + extra_width), F32)],
-        (queries, own_new, other_new, sums, tops, parts, out_weight, token_half, extra),
-        name="attention_out",
-        cost=(2 * rows * heads * dim * width, 2 << 20),
+        [shape((rows, half), BF16), shape((rows, half), F32)],
+        (queries, own_new, normed, other_weight, cosine, sine, own_cache, other_cache, *rest, out_weight, token_half),
+        name="attention",
+        cost=(4 * heads * rows * dim * slots, 1 << 20),
+    )
+    extra = call(
+        extra_body,
+        shape((rows, extra_width), F32),
+        (named, named_weight, slot, send),
+        free=[3],
+        name="route_columns",
     )
     own = call(
-        chip_body, shape((rows, half + extra_width), BF16), (keep, swap(send, "tensor", 1)), name="chip_sum",
+        chip_body, shape((rows, half + extra_width), BF16), (keep, extra, swap(send, "tensor", 1)), name="chip_sum",
         cost=(rows * width, 1 << 18),
     )
+    far_y, far_xy, near_x = swap(own, "expert", far), swap_both(own, far, 2), swap(own, "tensor", 2)
     weights = (gate_weight, up_weight, down_weight)
     weights = call(
         load_body,
         [shape(w.shape, BF16) for w in weights],
         (own, *weights),
         hbm=range(1, 4),
-        scratch=[pltpu.SemaphoreType.DMA((sum(w.shape[0] for w in weights),))],
+        scratch=[pltpu.SemaphoreType.DMA((len(weights) * CHUNKS,))],
         name="load_experts",
         cost=(0, 8 << 20),
     )
     block, residual = call(
         functools.partial(residual_body, copies),
         [shape((2 * rows, half + extra_width), BF16), shape((rows, half), BF16)],
-        (mixer_gain[None, :], own, swap(own, "tensor", 2), swap(own, "expert", far), swap_both(own, far, 2), weights[0]),
+        (mixer_gain[None, :], own, far_y, far_xy, near_x, weights[0]),
         free=[5],
         name="residual",
         cost=(rows * width, 1 << 18),
@@ -539,9 +519,9 @@
     pieces = []
     for group in (blocks[:1], blocks[1:]):
         if pieces:
-            group = after_all(group, [send])
+            group = [after_all(b, [got if i else send]) for i, b in enumerate(group)]
         others = [swap(b, "tensor", 1) for b in group]
-        sums, send = run_experts(group, others, *weights, copies, not pieces)
+        sums, send, got = run_experts(group, others, *weights, hosted, copies, not pieces)
         pieces += sums
     terms = [pieces[0]] + [swap(p, "expert", b) for p, b in zip(pieces[1:], stages[-1])]
     for stage in stages[-2::-1]:
@@ -562,10 +542,11 @@
         name="z_sums",
         cost=(rows * width, 1 << 18),
     )
+    far_y, far_xy, near_x = swap(far_part, "expert", far), swap_both(far_part, far, 2), swap(x_part, "tensor", 2)
     combined, squares = call(
         combine_body,
         [shape((rows, quarter), F32), shape((rows, LANES), F32)],
-        (own, swap(x_part, "tensor", 2), swap(far_part, "expert", far), swap_both(far_part, far, 2), residual),
+        (own, near_x, far_y, far_xy, residual),
         name="combine",
         cost=(rows * width, 1 << 18),
     )

time: 52.5 us -> 50.3 us (0.958)
  waiting for transfers between devices: 20.2 us -> 18.6 us
    ppermute x20, starting transfers between devices: 18.7 us -> 16.8 us  [swap(): return lax.ppermute(block, axis, [(i, i ^ bits) for i in range(count)])]
    ppermute x2, starting transfers between devices: 0.73 us -> 2.42 us  [swap_both(): lax.ppermute(block, ('expert', 'tensor'), [(i, i ^ bits) for i in range(c...]
    ppermute x2, waiting for transfers between devices: 4.91 us -> 3.92 us  [swap_both(): lax.ppermute(block, ('expert', 'tensor'), [(i, i ^ bits) for i in range(c...]
    ppermute x20, waiting for transfers between devices: 15.3 us -> 14.6 us  [swap(): return lax.ppermute(block, axis, [(i, i ^ bits) for i in range(count)])]
    pallas_call x12 -> x14, Pallas kernels: 7.79 us -> 7.65 us  [call(): pl.pallas_call(body, out_shape=listed, in_specs=in_specs, out_specs=out_s...]
  transfers between devices with their start and end apart: 22 -> 22, of which waited for: 16 -> 12; matrix products, arithmetic and copies ran while one was open for 0% -> 0% of each run, Pallas kernels for 18% -> 16%
where the time goes in v4:
time: 50.3 us; the launch traced here: 50.1 us
  starting transfers between devices  19.2 us (38%)
  waiting for transfers between devices  18.6 us (37%)
  Pallas kernels  12.1 us (24%)
    ppermute x20, starting transfers between devices, swap(): return lax.ppermute(block, axis, [(i, i ^ bits) for i in range(count)])  16.8 us
    ppermute x20, waiting for transfers between devices, swap(): return lax.ppermute(block, axis, [(i, i ^ bits) for i in range(count)])  14.6 us
    pallas_call x14, Pallas kernels, call(): pl.pallas_call(body, out_shape=listed, in_specs=in_specs, out_specs=out_s...  7.65 us
    ppermute x2, waiting for transfers between devices, swap_both(): lax.ppermute(block, ('expert', 'tensor'), [(i, i ^ bits) for i in range(c...  3.92 us
    pallas_call x2, Pallas kernels, run_experts(): pl.pallas_call(functools.partial(expert_body, copies, hosted, blocks), gr...  3.73 us
    ppermute x2, starting transfers between devices, swap_both(): lax.ppermute(block, ('expert', 'tensor'), [(i, i ^ bits) for i in range(c...  2.42 us
  transfers between devices with their start and end apart: 22, of which 12 were waited for; matrix products, arithmetic and copies ran while one was open for 0% of the time, Pallas kernels for 16%

profile of v4, /device:TPU:0, one launch (start us, length us, event | category | flops | bytes accessed | tf_op | source)
XLA Modules:
  0.0 50.1 jit_solution(16928070410859798331)
XLA Ops:
  0.5 2.0 %project.1 = (bf16[96,128]{1,0:T(8,128)(2,1)S(1)}, bf16[32,128]{1,0:T(8,128)(2,1)S(1)}, bf16[32,1536]{1,0:T(8,128)(2,1)S(1)}, f32[32,128]{1,0:T(8,128)S(1)}, f32...) custom-call(s32[1,3]{1,0:T(1,128)} %length_hbm.1, ...), custom_call_target="tpu_custom_call" | custom-call | flops 50331648 | bytes 2097152 | tf_op jit(solution)/shard_map/project/pallas_call | solution.py:58
  2.6 1.2 %attention.1 = (bf16[32,768]{1,0:T(8,128)(2,1)S(1)}, f32[32,768]{1,0:T(8,128)S(1)}) custom-call(bf16[96,128]{1,0:T(8,128)(2,1)S(1)} %get-tuple-element.38.q_ref, bf16[32,128]{1,0:T(8,128)(2,1)S(1)} %get-tuple-element.39.own_ref, bf16[32,1536]{1,0:T(8,128)(2,1)S(1)} %get-tuple-element.40.normed_ref, bf16[1536,128]{1,0:T(8,128)(2,1)S(1)} %collective-permute-done.other_ref, ...), custom_call_target="tpu_custom_call" | custom-call | flops 37748736 | bytes 1048576 | tf_op jit(solution)/shard_map/attention/pallas_call | solution.py:58
  5.2 4.0 %collective-permute-start.3 = (bf16[32,896]{1,0:T(8,128)(2,1)S(1)}, bf16[32,896]{1,0:T(8,128)(2,1)S(1)}, u32[]{:S(2)}, u32[]{:S(2)}) collective-permute-start(bf16[32,896]{1,0:T(8,128)(2,1)S(1)} %chip_sum.1.refs_0_.own_ref), channel_id=1, source_target_pairs={{0,16},{4,20},{8,24},{12,28},{16,0},{20,4},{24,8},{28,12},{1,17},{... | collective-permute-start | bytes 172040 | tf_op jit(solution)/shard_map/ppermute | solution.py:26
  9.2 1.3 %collective-permute-start.4 = (bf16[32,896]{1,0:T(8,128)(2,1)S(1)}, bf16[32,896]{1,0:T(8,128)(2,1)S(1)}, u32[]{:S(2)}, u32[]{:S(2)}) collective-permute-start(bf16[32,896]{1,0:T(8,128)(2,1)S(1)} %chip_sum.1.refs_0_.own_ref), channel_id=1, source_target_pairs={{0,18},{1,19},{2,16},{3,17},{4,22},{5,23},{6,20},{7,21},{8,26},{9,... | collective-permute-start | bytes 172040 | tf_op jit(solution)/shard_map/ppermute | solution.py:33
  10.7 3.1 %load_experts.1 = (bf16[768,1536]{1,0:T(8,128)(2,1)S(1)}, bf16[768,1536]{1,0:T(8,128)(2,1)S(1)}, bf16[768,1536]{1,0:T(8,128)(2,1)S(1)}) custom-call(bf16[32,896]{1,0:T(8,128)(2,1)S(1)} %chip_sum.1.refs_0_.own_ref, bf16[768,1536]{1,0:T(8,128)(2,1)} %bitcast.12, bf16[768,1536]{1,0:T(8,128)(2,1)} %bitcast.13, bf16[768,1536]{1,0:T(8,128)(2,1)} %bitcast.14), custom_call_target="tpu_custom_call" | custom-call | bytes 8388608 | tf_op jit(solution)/shard_map/load_experts/pallas_call | solution.py:58
  13.8 2.4 %collective-permute-done.4.xy_ref = bf16[32,896]{1,0:T(8,128)(2,1)S(1)} collective-permute-done((bf16[32,896]{1,0:T(8,128)(2,1)S(1)}, bf16[32,896]{1,0:T(8,128)(2,1)S(1)}, u32[]{:S(2)}, u32[]{:S(2)}) %collective-permute-start.4) | collective-permute-done | bytes 57376 | tf_op jit(solution)/shard_map/ppermute | solution.py:33
  16.5 1.6 %collective-permute-start.8 = (bf16[64,896]{1,0:T(8,128)(2,1)S(1)}, bf16[64,896]{1,0:T(8,128)(2,1)S(1)}, u32[]{:S(2)}, u32[]{:S(2)}) collective-permute-start(bf16[64,896]{1,0:T(8,128)(2,1)S(1)} %get-tuple-element.55.refs_0_), channel_id=1, source_target_pairs={{0,4},{4,0},{8,12},{12,8},{16,20},{20,16},{24,28},{28,24},{1,5},{5... | collective-permute-start | bytes 344072 | tf_op jit(solution)/shard_map/ppermute | solution.py:26
  18.7 1.4 %collective-permute-start.10 = (bf16[64,896]{1,0:T(8,128)(2,1)S(1)}, bf16[64,896]{1,0:T(8,128)(2,1)S(1)}, u32[]{:S(2)}, u32[]{:S(2)}) collective-permute-start(bf16[64,896]{1,0:T(8,128)(2,1)S(1)} %get-tuple-element.55.refs_0_), channel_id=1, source_target_pairs={{0,12},{4,8},{8,4},{12,0},{16,28},{20,24},{24,20},{28,16},{1,13},{... | collective-permute-start | bytes 344072 | tf_op jit(solution)/shard_map/ppermute | solution.py:26
  20.1 1.9 %experts.2 = (bf16[1,64,768]{2,1,0:T(8,128)(2,1)S(1)}, bf16[1,64,768]{2,1,0:T(8,128)(2,1)S(1)}) custom-call(bf16[64,896]{1,0:T(8,128)(2,1)S(1)} %get-tuple-element.55.refs_0_, bf16[64,896]{1,0:T(8,128)(2,1)S(1)} %collective-permute-done.6.refs_1_, bf16[768,1536]{1,0:T(8,128)(2,1)S(1)} %get-tuple-element.54.loaded_ref.refs_2_.refs_6_, ...), custom_call_target="tpu_custom_call" | custom-call | flops 1 | bytes 1 | tf_op jit(solution)/shard_map/experts/pallas_call | solution.py:393
  22.6 1.5 %collective-permute-done.9.block_ref = bf16[64,896]{1,0:T(8,128)(2,1)S(1)} collective-permute-done((bf16[64,896]{1,0:T(8,128)(2,1)S(1)}, bf16[64,896]{1,0:T(8,128)(2,1)S(1)}, u32[]{:S(2)}, u32[]{:S(2)}) %collective-permute-start.9) | collective-permute-done | bytes 114720 | tf_op jit(solution)/shard_map/ppermute | solution.py:26
  24.2 1.5 %collective-permute-done.10.block_ref = bf16[64,896]{1,0:T(8,128)(2,1)S(1)} collective-permute-done((bf16[64,896]{1,0:T(8,128)(2,1)S(1)}, bf16[64,896]{1,0:T(8,128)(2,1)S(1)}, u32[]{:S(2)}, u32[]{:S(2)}) %collective-permute-start.10) | collective-permute-done | bytes 114720 | tf_op jit(solution)/shard_map/ppermute | solution.py:26
  25.8 1.3 %collective-permute-done.13.refs_5_ = bf16[64,896]{1,0:T(8,128)(2,1)S(1)} collective-permute-done((bf16[64,896]{1,0:T(8,128)(2,1)S(1)}, bf16[64,896]{1,0:T(8,128)(2,1)S(1)}, u32[]{:S(2)}, u32[]{:S(2)}) %collective-permute-start.13) | collective-permute-done | bytes 114720 | tf_op jit(solution)/shard_map/ppermute | solution.py:26
  27.1 1.8 %experts.3 = (bf16[3,64,768]{2,1,0:T(8,128)(2,1)S(1)}, bf16[3,64,768]{2,1,0:T(8,128)(2,1)S(1)}) custom-call(bf16[64,896]{1,0:T(8,128)(2,1)S(1)} %relay.3.refs_0_, bf16[64,896]{1,0:T(8,128)(2,1)S(1)} %relay.4.refs_1_, bf16[64,896]{1,0:T(8,128)(2,1)S(1)} %relay.5.refs_2_, bf16[64,896]{1,0:T(8,128)(2,1)S(1)} %collective-permute-done.11.refs_3_, ...), custom_call_target="tpu_custom_call" | custom-call | flops 1 | bytes 1 | tf_op jit(solution)/shard_map/experts/pallas_call | solution.py:393
  30.6 1.6 %collective-permute-start.15 = (bf16[64,768]{1,0:T(8,128)(2,1)S(1)}, bf16[64,768]{1,0:T(8,128)(2,1)S(1)}, u32[]{:S(2)}, u32[]{:S(2)}) collective-permute-start(bf16[64,768]{1,0:T(8,128)(2,1)S(1)} %get-tuple-element.62), channel_id=1, source_target_pairs={{0,4},{4,0},{8,12},{12,8},{16,20},{20,16},{24,28},{28,24},{1,5},{5... | collective-permute-start | bytes 294920 | tf_op jit(solution)/shard_map/ppermute | solution.py:26
  32.8 1.4 %collective-permute-start.17 = (bf16[64,768]{1,0:T(8,128)(2,1)S(1)}, bf16[64,768]{1,0:T(8,128)(2,1)S(1)}, u32[]{:S(2)}, u32[]{:S(2)}) collective-permute-start(bf16[64,768]{1,0:T(8,128)(2,1)S(1)} %get-tuple-element.64), channel_id=1, source_target_pairs={{0,12},{4,8},{8,4},{12,0},{16,28},{20,24},{24,20},{28,16},{1,13},{... | collective-permute-start | bytes 294920 | tf_op jit(solution)/shard_map/ppermute | solution.py:26
  34.5 1.0 %collective-permute-done.15.refs_1_ = bf16[64,768]{1,0:T(8,128)(2,1)S(1)} collective-permute-done((bf16[64,768]{1,0:T(8,128)(2,1)S(1)}, bf16[64,768]{1,0:T(8,128)(2,1)S(1)}, u32[]{:S(2)}, u32[]{:S(2)}) %collective-permute-start.15) | collective-permute-done | bytes 98336 | tf_op jit(solution)/shard_map/ppermute | solution.py:26
  35.6 2.3 %collective-permute-done.16.refs_2_ = bf16[64,768]{1,0:T(8,128)(2,1)S(1)} collective-permute-done((bf16[64,768]{1,0:T(8,128)(2,1)S(1)}, bf16[64,768]{1,0:T(8,128)(2,1)S(1)}, u32[]{:S(2)}, u32[]{:S(2)}) %collective-permute-start.16) | collective-permute-done | bytes 98336 | tf_op jit(solution)/shard_map/ppermute | solution.py:26
  37.9 1.0 %collective-permute-done.17.refs_3_ = bf16[64,768]{1,0:T(8,128)(2,1)S(1)} collective-permute-done((bf16[64,768]{1,0:T(8,128)(2,1)S(1)}, bf16[64,768]{1,0:T(8,128)(2,1)S(1)}, u32[]{:S(2)}, u32[]{:S(2)}) %collective-permute-start.17) | collective-permute-done | bytes 98336 | tf_op jit(solution)/shard_map/ppermute | solution.py:26
  38.9 1.6 %collective-permute-start.18 = (bf16[32,768]{1,0:T(8,128)(2,1)S(1)}, bf16[32,768]{1,0:T(8,128)(2,1)S(1)}, u32[]{:S(2)}, u32[]{:S(2)}) collective-permute-start(bf16[32,768]{1,0:T(8,128)(2,1)S(1)} %get-tuple-element.66), channel_id=1, source_target_pairs={{0,2},{1,3},{2,0},{3,1},{4,6},{5,7},{6,4},{7,5},{8,10},{9,11},{10,... | collective-permute-start | bytes 147464 | tf_op jit(solution)/shard_map/ppermute | solution.py:26
  40.5 1.7 %collective-permute-start.19 = (bf16[32,768]{1,0:T(8,128)(2,1)S(1)}, bf16[32,768]{1,0:T(8,128)(2,1)S(1)}, u32[]{:S(2)}, u32[]{:S(2)}) collective-permute-start(bf16[32,768]{1,0:T(8,128)(2,1)S(1)} %get-tuple-element.67), channel_id=1, source_target_pairs={{0,16},{4,20},{8,24},{12,28},{16,0},{20,4},{24,8},{28,12},{1,17},{... | collective-permute-start | bytes 147464 | tf_op jit(solution)/shard_map/ppermute | solution.py:26
  42.2 1.2 %collective-permute-start.20 = (bf16[32,768]{1,0:T(8,128)(2,1)S(1)}, bf16[32,768]{1,0:T(8,128)(2,1)S(1)}, u32[]{:S(2)}, u32[]{:S(2)}) collective-permute-start(bf16[32,768]{1,0:T(8,128)(2,1)S(1)} %get-tuple-element.67), channel_id=1, source_target_pairs={{0,18},{1,19},{2,16},{3,17},{4,22},{5,23},{6,20},{7,21},{8,26},{9,... | collective-permute-start | bytes 147464 | tf_op jit(solution)/shard_map/ppermute | solution.py:33
  43.4 3.2 %collective-permute-done.19.y_ref = bf16[32,768]{1,0:T(8,128)(2,1)S(1)} collective-permute-done((bf16[32,768]{1,0:T(8,128)(2,1)S(1)}, bf16[32,768]{1,0:T(8,128)(2,1)S(1)}, u32[]{:S(2)}, u32[]{:S(2)}) %collective-permute-start.19) | collective-permute-done | bytes 49184 | tf_op jit(solution)/shard_map/ppermute | solution.py:26
  46.6 1.5 %collective-permute-done.20.xy_ref = bf16[32,768]{1,0:T(8,128)(2,1)S(1)} collective-permute-done((bf16[32,768]{1,0:T(8,128)(2,1)S(1)}, bf16[32,768]{1,0:T(8,128)(2,1)S(1)}, u32[]{:S(2)}, u32[]{:S(2)}) %collective-permute-start.20) | collective-permute-done | bytes 49184 | tf_op jit(solution)/shard_map/ppermute | solution.py:33
  48.3 1.2 %collective-permute-done.21.b_ref = f32[32,128]{1,0:T(8,128)S(1)} collective-permute-done((f32[32,128]{1,0:T(8,128)S(1)}, f32[32,128]{1,0:T(8,128)S(1)}, u32[]{:S(2)}, u32[]{:S(2)}) %collective-permute-start.21) | collective-permute-done | bytes 16416 | tf_op jit(solution)/shard_map/ppermute | solution.py:26
  (46 shorter events, 7.3 us)
Async XLA Ops:
  0.0 10.7 %copy-start.1 = (bf16[1536]{0:T(1024)(128)(2,1)S(1)}, bf16[1536]{0:T(1024)(128)(2,1)}, u32[]{:S(2)}) copy-start(bf16[1536]{0:T(1024)(128)(2,1)} %param.28) | copy-start | bytes 9220
  0.0 2.5 %collective-permute-start = (bf16[1536,128]{1,0:T(8,128)(2,1)}, bf16[1536,128]{1,0:T(8,128)(2,1)S(1)}, u32[]{:S(2)}, u32[]{:S(2)}) collective-permute-start(bf16[1536,128]{1,0:T(8,128)(2,1)} %bitcast.15), channel_id=1, source_target_pairs={{0,1},{1,0},{2,3},{3,2},{4,5},{5,4},{6,7},{7,6},{8,9},{9,8},{10,11... | collective-permute-start | bytes 1179656 | tf_op jit(solution)/shard_map/ppermute | solution.py:26
  0.5 2.1 %collective-permute-start.1 = (bf16[768,128]{1,0:T(8,128)(2,1)}, bf16[768,128]{1,0:T(8,128)(2,1)S(1)}, u32[]{:S(2)}, u32[]{:S(2)}) collective-permute-start(bf16[768,128]{1,0:T(8,128)(2,1)} %bitcast.16), channel_id=1, source_target_pairs={{0,1},{1,0},{2,3},{3,2},{4,5},{5,4},{6,7},{7,6},{8,9},{9,8},{10,11... | collective-permute-start | bytes 589832 | tf_op jit(solution)/shard_map/ppermute | solution.py:26
  3.8 1.4 %collective-permute-start.2 = (bf16[32,768]{1,0:T(8,128)(2,1)S(1)}, bf16[32,768]{1,0:T(8,128)(2,1)S(1)}, u32[]{:S(2)}, u32[]{:S(2)}) collective-permute-start(bf16[32,768]{1,0:T(8,128)(2,1)S(1)} %get-tuple-element.53.sent_ref), channel_id=1, source_target_pairs={{0,1},{1,0},{2,3},{3,2},{4,5},{5,4},{6,7},{7,6},{8,9},{9,8},{10,11... | collective-permute-start | bytes 147464 | tf_op jit(solution)/shard_map/ppermute | solution.py:26
  5.2 8.7 %collective-permute-start.3 = (bf16[32,896]{1,0:T(8,128)(2,1)S(1)}, bf16[32,896]{1,0:T(8,128)(2,1)S(1)}, u32[]{:S(2)}, u32[]{:S(2)}) collective-permute-start(bf16[32,896]{1,0:T(8,128)(2,1)S(1)} %chip_sum.1.refs_0_.own_ref), channel_id=1, source_target_pairs={{0,16},{4,20},{8,24},{12,28},{16,0},{20,4},{24,8},{28,12},{1,17},{... | collective-permute-start | bytes 172040 | tf_op jit(solution)/shard_map/ppermute | solution.py:26
  9.2 7.1 %collective-permute-start.4 = (bf16[32,896]{1,0:T(8,128)(2,1)S(1)}, bf16[32,896]{1,0:T(8,128)(2,1)S(1)}, u32[]{:S(2)}, u32[]{:S(2)}) collective-permute-start(bf16[32,896]{1,0:T(8,128)(2,1)S(1)} %chip_sum.1.refs_0_.own_ref), channel_id=1, source_target_pairs={{0,18},{1,19},{2,16},{3,17},{4,22},{5,23},{6,20},{7,21},{8,26},{9,... | collective-permute-start | bytes 172040 | tf_op jit(solution)/shard_map/ppermute | solution.py:33
  10.4 5.9 %collective-permute-start.5 = (bf16[32,896]{1,0:T(8,128)(2,1)S(1)}, bf16[32,896]{1,0:T(8,128)(2,1)S(1)}, u32[]{:S(2)}, u32[]{:S(2)}) collective-permute-start(bf16[32,896]{1,0:T(8,128)(2,1)S(1)} %chip_sum.1.refs_0_.own_ref), channel_id=1, source_target_pairs={{0,2},{1,3},{2,0},{3,1},{4,6},{5,7},{6,4},{7,5},{8,10},{9,11},{10,... | collective-permute-start | bytes 172040 | tf_op jit(solution)/shard_map/ppermute | solution.py:26
  16.4 3.6 %collective-permute-start.6 = (bf16[64,896]{1,0:T(8,128)(2,1)S(1)}, bf16[64,896]{1,0:T(8,128)(2,1)S(1)}, u32[]{:S(2)}, u32[]{:S(2)}) collective-permute-start(bf16[64,896]{1,0:T(8,128)(2,1)S(1)} %get-tuple-element.55.refs_0_), channel_id=1, source_target_pairs={{0,1},{1,0},{2,3},{3,2},{4,5},{5,4},{6,7},{7,6},{8,9},{9,8},{10,11... | collective-permute-start | bytes 344072 | tf_op jit(solution)/shard_map/ppermute | solution.py:26
  16.5 5.6 %collective-permute-start.8 = (bf16[64,896]{1,0:T(8,128)(2,1)S(1)}, bf16[64,896]{1,0:T(8,128)(2,1)S(1)}, u32[]{:S(2)}, u32[]{:S(2)}) collective-permute-start(bf16[64,896]{1,0:T(8,128)(2,1)S(1)} %get-tuple-element.55.refs_0_), channel_id=1, source_target_pairs={{0,4},{4,0},{8,12},{12,8},{16,20},{20,16},{24,28},{28,24},{1,5},{5... | collective-permute-start | bytes 344072 | tf_op jit(solution)/shard_map/ppermute | solution.py:26
  18.1 6.0 %collective-permute-start.9 = (bf16[64,896]{1,0:T(8,128)(2,1)S(1)}, bf16[64,896]{1,0:T(8,128)(2,1)S(1)}, u32[]{:S(2)}, u32[]{:S(2)}) collective-permute-start(bf16[64,896]{1,0:T(8,128)(2,1)S(1)} %get-tuple-element.55.refs_0_), channel_id=1, source_target_pairs={{0,8},{4,12},{8,0},{12,4},{16,24},{20,28},{24,16},{28,20},{1,9},{5... | collective-permute-start | bytes 344072 | tf_op jit(solution)/shard_map/ppermute | solution.py:26
  18.7 7.0 %collective-permute-start.10 = (bf16[64,896]{1,0:T(8,128)(2,1)S(1)}, bf16[64,896]{1,0:T(8,128)(2,1)S(1)}, u32[]{:S(2)}, u32[]{:S(2)}) collective-permute-start(bf16[64,896]{1,0:T(8,128)(2,1)S(1)} %get-tuple-element.55.refs_0_), channel_id=1, source_target_pairs={{0,12},{4,8},{8,4},{12,0},{16,28},{20,24},{24,20},{28,16},{1,13},{... | collective-permute-start | bytes 344072 | tf_op jit(solution)/shard_map/ppermute | solution.py:26
  22.0 2.1 %collective-permute-start.7 = (bf16[1,64,768]{2,1,0:T(8,128)(2,1)S(1)}, bf16[1,64,768]{2,1,0:T(8,128)(2,1)S(1)}, u32[]{:S(2)}, u32[]{:S(2)}) collective-permute-start(bf16[1,64,768]{2,1,0:T(8,128)(2,1)S(1)} %get-tuple-element.59.refs_0_), channel_id=1, source_target_pairs={{0,1},{1,0},{2,3},{3,2},{4,5},{5,4},{6,7},{7,6},{8,9},{9,8},{10,11... | collective-permute-start | bytes 294920 | tf_op jit(solution)/shard_map/ppermute | solution.py:26
  22.1 3.7 %collective-permute-start.11 = (bf16[64,896]{1,0:T(8,128)(2,1)S(1)}, bf16[64,896]{1,0:T(8,128)(2,1)S(1)}, u32[]{:S(2)}, u32[]{:S(2)}) collective-permute-start(bf16[64,896]{1,0:T(8,128)(2,1)S(1)} %relay.3.refs_0_), channel_id=1, source_target_pairs={{0,1},{1,0},{2,3},{3,2},{4,5},{5,4},{6,7},{7,6},{8,9},{9,8},{10,11... | collective-permute-start | bytes 344072 | tf_op jit(solution)/shard_map/ppermute | solution.py:26
  24.1 1.7 %collective-permute-start.12 = (bf16[64,896]{1,0:T(8,128)(2,1)S(1)}, bf16[64,896]{1,0:T(8,128)(2,1)S(1)}, u32[]{:S(2)}, u32[]{:S(2)}) collective-permute-start(bf16[64,896]{1,0:T(8,128)(2,1)S(1)} %relay.4.refs_1_), channel_id=1, source_target_pairs={{0,1},{1,0},{2,3},{3,2},{4,5},{5,4},{6,7},{7,6},{8,9},{9,8},{10,11... | collective-permute-start | bytes 344072 | tf_op jit(solution)/shard_map/ppermute | solution.py:26
  25.7 1.4 %collective-permute-start.13 = (bf16[64,896]{1,0:T(8,128)(2,1)S(1)}, bf16[64,896]{1,0:T(8,128)(2,1)S(1)}, u32[]{:S(2)}, u32[]{:S(2)}) collective-permute-start(bf16[64,896]{1,0:T(8,128)(2,1)S(1)} %relay.5.refs_2_), channel_id=1, source_target_pairs={{0,1},{1,0},{2,3},{3,2},{4,5},{5,4},{6,7},{7,6},{8,9},{9,8},{10,11... | collective-permute-start | bytes 344072 | tf_op jit(solution)/shard_map/ppermute | solution.py:26
  28.9 1.6 %collective-permute-start.14 = (bf16[3,64,768]{2,1,0:T(8,128)(2,1)S(1)}, bf16[3,64,768]{2,1,0:T(8,128)(2,1)S(1)}, u32[]{:S(2)}, u32[]{:S(2)}) collective-permute-start(bf16[3,64,768]{2,1,0:T(8,128)(2,1)S(1)} %get-tuple-element.61), channel_id=1, source_target_pairs={{0,1},{1,0},{2,3},{3,2},{4,5},{5,4},{6,7},{7,6},{8,9},{9,8},{10,11... | collective-permute-start | bytes 884744 | tf_op jit(solution)/shard_map/ppermute | solution.py:26
  29.6 18.6 %copy-start.2 = (bf16[384]{0:T(512)(128)(2,1)S(1)}, bf16[384]{0:T(512)(128)(2,1)}, u32[]{:S(2)}) copy-start(bf16[384]{0:T(512)(128)(2,1)} %param.35) | copy-start | bytes 2308
  30.6 4.9 %collective-permute-start.15 = (bf16[64,768]{1,0:T(8,128)(2,1)S(1)}, bf16[64,768]{1,0:T(8,128)(2,1)S(1)}, u32[]{:S(2)}, u32[]{:S(2)}) collective-permute-start(bf16[64,768]{1,0:T(8,128)(2,1)S(1)} %get-tuple-element.62), channel_id=1, source_target_pairs={{0,4},{4,0},{8,12},{12,8},{16,20},{20,16},{24,28},{28,24},{1,5},{5... | collective-permute-start | bytes 294920 | tf_op jit(solution)/shard_map/ppermute | solution.py:26
  32.2 5.6 %collective-permute-start.16 = (bf16[64,768]{1,0:T(8,128)(2,1)S(1)}, bf16[64,768]{1,0:T(8,128)(2,1)S(1)}, u32[]{:S(2)}, u32[]{:S(2)}) collective-permute-start(bf16[64,768]{1,0:T(8,128)(2,1)S(1)} %get-tuple-element.63), channel_id=1, source_target_pairs={{0,8},{4,12},{8,0},{12,4},{16,24},{20,28},{24,16},{28,20},{1,9},{5... | collective-permute-start | bytes 294920 | tf_op jit(solution)/shard_map/ppermute | solution.py:26
  32.8 6.1 %collective-permute-start.17 = (bf16[64,768]{1,0:T(8,128)(2,1)S(1)}, bf16[64,768]{1,0:T(8,128)(2,1)S(1)}, u32[]{:S(2)}, u32[]{:S(2)}) collective-permute-start(bf16[64,768]{1,0:T(8,128)(2,1)S(1)} %get-tuple-element.64), channel_id=1, source_target_pairs={{0,12},{4,8},{8,4},{12,0},{16,28},{20,24},{24,20},{28,16},{1,13},{... | collective-permute-start | bytes 294920 | tf_op jit(solution)/shard_map/ppermute | solution.py:26
  38.9 4.5 %collective-permute-start.18 = (bf16[32,768]{1,0:T(8,128)(2,1)S(1)}, bf16[32,768]{1,0:T(8,128)(2,1)S(1)}, u32[]{:S(2)}, u32[]{:S(2)}) collective-permute-start(bf16[32,768]{1,0:T(8,128)(2,1)S(1)} %get-tuple-element.66), channel_id=1, source_target_pairs={{0,2},{1,3},{2,0},{3,1},{4,6},{5,7},{6,4},{7,5},{8,10},{9,11},{10,... | collective-permute-start | bytes 147464 | tf_op jit(solution)/shard_map/ppermute | solution.py:26
  40.5 6.1 %collective-permute-start.19 = (bf16[32,768]{1,0:T(8,128)(2,1)S(1)}, bf16[32,768]{1,0:T(8,128)(2,1)S(1)}, u32[]{:S(2)}, u32[]{:S(2)}) collective-permute-start(bf16[32,768]{1,0:T(8,128)(2,1)S(1)} %get-tuple-element.67), channel_id=1, source_target_pairs={{0,16},{4,20},{8,24},{12,28},{16,0},{20,4},{24,8},{28,12},{1,17},{... | collective-permute-start | bytes 147464 | tf_op jit(solution)/shard_map/ppermute | solution.py:26
  42.2 5.9 %collective-permute-start.20 = (bf16[32,768]{1,0:T(8,128)(2,1)S(1)}, bf16[32,768]{1,0:T(8,128)(2,1)S(1)}, u32[]{:S(2)}, u32[]{:S(2)}) collective-permute-start(bf16[32,768]{1,0:T(8,128)(2,1)S(1)} %get-tuple-element.67), channel_id=1, source_target_pairs={{0,18},{1,19},{2,16},{3,17},{4,22},{5,23},{6,20},{7,21},{8,26},{9,... | collective-permute-start | bytes 147464 | tf_op jit(solution)/shard_map/ppermute | solution.py:33
  48.2 1.2 %collective-permute-start.21 = (f32[32,128]{1,0:T(8,128)S(1)}, f32[32,128]{1,0:T(8,128)S(1)}, u32[]{:S(2)}, u32[]{:S(2)}) collective-permute-start(f32[32,128]{1,0:T(8,128)S(1)} %get-tuple-element.70.a_ref), channel_id=1, source_target_pairs={{0,1},{1,0},{2,3},{3,2},{4,5},{5,4},{6,7},{7,6},{8,9},{9,8},{10,11... | collective-permute-start | bytes 49160 | tf_op jit(solution)/shard_map/ppermute | solution.py:26
  (1 other events, 2.6 us)

commit v5 on v4

--- a/solution.py
+++ b/solution.py
@@ -286,8 +286,8 @@
 
 def expert_body(copies, hosted, blocks, *refs):
     own_refs, other_refs = refs[:blocks], refs[blocks : 2 * blocks]
-    gate_ref, up_ref, down_ref = refs[2 * blocks : 2 * blocks + 3]
-    hidden_ref, send_ref = refs[-2:]
+    gate_ref, up_ref, down_ref, hidden_ref = refs[2 * blocks : 2 * blocks + 4]
+    send_refs = refs[2 * blocks + 4 :]
     width = gate_ref.shape[1]
     units = gate_ref.shape[0] // hosted
     quarter = width // 4
@@ -316,11 +316,78 @@
     hidden = jnp.concatenate(parts, axis=1)
     for b in range(blocks):
         hidden_ref[b] = hidden[b * tall : (b + 1) * tall]
+    send_half(hidden, down_ref, send_refs)
+
+
+def tiles(units):
+    step = 256 if units % 256 == 0 else units
+    return [slice(i, i + step) for i in range(0, units, step)]
+
+
+def quarters(blocks, quarter, core):
+    rows = jnp.concatenate([r[:, : 2 * quarter] for r in blocks], axis=0)
+    for k in range(2):
+        start = pl.multiple_of((2 * k + core) * quarter, LANES)
+        yield rows[:, k * quarter : (k + 1) * quarter], pl.ds(start, quarter)
+
+
+def half_body(blocks, *refs):
+    own_refs = refs[:blocks]
+    gate_ref, up_ref, gate_out, up_out = refs[blocks:]
+    quarter = gate_ref.shape[1] // 4
+    pairs = list(quarters(own_refs, quarter, lax.axis_index("tensor") % 2))
+    for span in tiles(gate_ref.shape[0]):
+        for weight_ref, out_ref in ((gate_ref, gate_out), (up_ref, up_out)):
+            total = sum(dot_t(part, weight_ref[span, cols]) for part, cols in pairs)
+            out_ref[:, :, span] = total.reshape(blocks, -1, total.shape[1])
+
+
+def rest_body(copies, hosted, blocks, *refs):
+    own_refs, other_refs = refs[:blocks], refs[blocks : 2 * blocks]
+    gate_ref, up_ref, down_ref, gate_half, up_half, hidden_ref = refs[2 * blocks : 2 * blocks + 6]
+    send_refs = refs[2 * blocks + 6 :]
+    total, width = gate_ref.shape
+    units = total // hosted
+    quarter = width // 4
+    extra = jnp.concatenate([r[:, 2 * quarter :] for r in own_refs], axis=0).astype(F32)
+    far_extra = jnp.concatenate([r[:, 2 * quarter :] for r in other_refs], axis=0).astype(F32)
+    lane = iota(extra.shape, 1)
+    squares = jnp.where((lane == 2 * copies) | (lane == 2 * copies + 1), extra + far_extra, 0.0)
+    scale = lax.rsqrt(jnp.sum(squares, axis=1, keepdims=True) / width + EPSILON)
+    weights = []
+    for j in range(hosted):
+        slot = lax.axis_index("expert") * hosted + j
+        one = jnp.where((lane == slot) | (lane == slot + copies), extra, 0.0)
+        weights.append(jnp.sum(one, axis=1, keepdims=True))
+    pairs = list(quarters(other_refs, quarter, 1 - lax.axis_index("tensor") % 2))
+    count = extra.shape[0]
+    parts = []
+    for span in tiles(total):
+        size = span.stop - span.start
+        place = iota((count, size), 1) + span.start
+        weight = weights[span.start // units]
+        for j in range(span.start // units + 1, (span.stop - 1) // units + 1):
+            weight = jnp.where(place >= j * units, weights[j], weight)
+        gate, up = gate_half[:, :, span].reshape(count, size), up_half[:, :, span].reshape(count, size)
+        for part, cols in pairs:
+            gate = gate + dot_t(part, gate_ref[span, cols])
+            up = up + dot_t(part, up_ref[span, cols])
+        parts.append((jnp.maximum(gate * scale, 0.0) * (up * scale) * weight).astype(BF16))
+    hidden = jnp.concatenate(parts, axis=1)
+    tall = count // blocks
+    for b in range(blocks):
+        hidden_ref[b] = hidden[b * tall : (b + 1) * tall]
+    send_half(hidden, down_ref, send_refs)
+
+
+def send_half(hidden, down_ref, send_refs):
+    quarter = down_ref.shape[1] // 4
+    tall = hidden.shape[0] // len(send_refs)
     for k in range(2):
         start = pl.multiple_of((2 * k + 1 - lax.axis_index("tensor") % 2) * quarter, LANES)
         total = dot(hidden, down_ref[:, pl.ds(start, quarter)]).astype(BF16)
-        for b in range(blocks):
-            send_ref[b, :, k * quarter : (k + 1) * quarter] = total[b * tall : (b + 1) * tall]
+        for b, send_ref in enumerate(send_refs):
+            send_ref[:, k * quarter : (k + 1) * quarter] = total[b * tall : (b + 1) * tall]
 
 
 def keep_body(blocks, hidden_ref, down_ref, out_ref):
@@ -334,9 +401,8 @@
             out_ref[b, :, k * quarter : (k + 1) * quarter] = total[b * tall : (b + 1) * tall]
 
 
-def chips_body(keep_ref, got_ref, *out_refs):
-    for b, out_ref in enumerate(out_refs):
-        out_ref[...] = (keep_ref[b] + got_ref[b].astype(F32)).astype(out_ref.dtype)
+def chips_body(b, keep_ref, got_ref, out_ref):
+    out_ref[...] = (keep_ref[b] + got_ref[...].astype(F32)).astype(out_ref.dtype)
 
 
 def pass_body(terms, *refs):
@@ -386,40 +452,57 @@
         return pl.BlockSpec(dims, place)
 
     row_spec = spec((step, total), lambda i: (i, 0))
-    half_spec = spec((blocks, step, width // 2), lambda i: (0, i, 0))
+    half_spec = spec((step, width // 2), lambda i: (i, 0))
+    keep_spec = spec((blocks, step, width // 2), lambda i: (0, i, 0))
     hidden_spec = spec((blocks, step, units), lambda i: (0, i, 0))
     whole = pl.BlockSpec(memory_space=pltpu.VMEM)
     params = pltpu.CompilerParams(vmem_limit_bytes=32 << 20)
-    hidden, send = pl.pallas_call(
-        functools.partial(expert_body, copies, hosted, blocks),
+    tiny = pl.CostEstimate(flops=1, bytes_accessed=1, transcendentals=0)
+    halves = []
+    if not first:
+        halves = pl.pallas_call(
+            functools.partial(half_body, blocks),
+            grid=grid,
+            out_shape=[shape((blocks, tall, units), F32)] * 2,
+            in_specs=[row_spec] * blocks + [whole] * 2,
+            out_specs=[hidden_spec] * 2,
+            compiler_params=params,
+            cost_estimate=tiny,
+            name="experts_half_depth",
+        )(*own, gate_weight, up_weight)
+    hidden, *sends = pl.pallas_call(
+        functools.partial(expert_body if first else rest_body, copies, hosted, blocks),
         grid=grid,
-        out_shape=[shape((blocks, tall, units), BF16), shape((blocks, tall, width // 2), BF16)],
-        in_specs=[row_spec] * (2 * blocks) + [whole] * 3,
-        out_specs=[hidden_spec, half_spec],
+        out_shape=[shape((blocks, tall, units), BF16)] + [shape((tall, width // 2), BF16)] * blocks,
+        in_specs=[row_spec] * (2 * blocks) + [whole] * 3 + [hidden_spec] * len(halves),
+        out_specs=[hidden_spec] + [half_spec] * blocks,
         compiler_params=params,
-        cost_estimate=pl.CostEstimate(flops=1, bytes_accessed=1, transcendentals=0),
+        cost_estimate=tiny,
         name="experts",
-    )(*own, *other, gate_weight, up_weight, down_weight)
-    got = swap(send, "tensor", 1)
+    )(*own, *other, gate_weight, up_weight, down_weight, *halves)
+    got = [swap(send, "tensor", 1) for send in sends]
     keep = pl.pallas_call(
         functools.partial(keep_body, blocks),
         grid=grid,
         out_shape=shape((blocks, tall, width // 2), F32),
         in_specs=[hidden_spec, whole],
-        out_specs=half_spec,
+        out_specs=keep_spec,
         compiler_params=params,
-        cost_estimate=pl.CostEstimate(flops=1, bytes_accessed=1, transcendentals=0),
+        cost_estimate=tiny,
         name="experts_own_half",
     )(hidden, down_weight)
-    sums = call(
-        chips_body,
-        [shape((tall, width // 2), F32 if first and b == 0 else BF16) for b in range(blocks)],
-        (keep, got),
-        vmem=48 << 20,
-        name="chip_sums",
-        cost=(1, 1),
-    )
-    return list(sums), send, got
+    sums = [
+        call(
+            functools.partial(chips_body, b),
+            shape((tall, width // 2), F32 if first else BF16),
+            (keep, got[b]),
+            vmem=48 << 20,
+            name="chip_sums",
+            cost=(1, 1),
+        )
+        for b in range(blocks)
+    ]
+    return sums, sends[0], got[0]
 
 
 def on_device(
@@ -510,7 +593,7 @@
 
     bit, stages = 1, []
     while bit < far:
-        stages.append([bit] if 2 * bit >= far else [bit, 2 * bit, 3 * bit])
+        stages.append([bit] if 2 * bit >= far else [3 * bit, bit, 2 * bit])
         bit *= 4
     blocks = [block]
     for stage in stages:

time: 50.3 us -> 48.8 us (0.970)
  waiting for transfers between devices: 18.6 us -> 15.7 us
  starting transfers between devices: 19.2 us -> 20 us
    ppermute x20 -> x22, waiting for transfers between devices: 14.6 us -> 12.6 us  [swap(): return lax.ppermute(block, axis, [(i, i ^ bits) for i in range(count)])]
    ppermute x2, waiting for transfers between devices: 3.92 us -> 3.07 us  [swap_both(): lax.ppermute(block, ('expert', 'tensor'), [(i, i ^ bits) for i in range(c...]
    ppermute x2, starting transfers between devices: 2.42 us -> 2.97 us  [swap_both(): lax.ppermute(block, ('expert', 'tensor'), [(i, i ^ bits) for i in range(c...]
    pallas_call x2 -> x3, Pallas kernels: 3.73 us -> 4.22 us  [the longest x2 3.26 us: run_experts(): pl.pallas_call(functools.partial(expert_body if first else rest_body, cop...]
    ppermute x20 -> x22, starting transfers between devices: 16.8 us -> 17 us  [swap(): return lax.ppermute(block, axis, [(i, i ^ bits) for i in range(count)])]
    pallas_call x14 -> x16, Pallas kernels: 7.65 us -> 7.66 us  [call(): pl.pallas_call(body, out_shape=listed, in_specs=in_specs, out_specs=out_s...]
  transfers between devices with their start and end apart: 22 -> 24, of which waited for: 12 -> 9; matrix products, arithmetic and copies ran while one was open for 0% -> 0% of each run, Pallas kernels for 16% -> 19%
where the time goes in v5:
time: 48.8 us; the launch traced here: 48.6 us
  starting transfers between devices  20 us (41%)
  waiting for transfers between devices  15.7 us (32%)
  Pallas kernels  12.6 us (26%)
    ppermute x22, starting transfers between devices, swap(): return lax.ppermute(block, axis, [(i, i ^ bits) for i in range(count)])  17 us
    ppermute x22, waiting for transfers between devices, swap(): return lax.ppermute(block, axis, [(i, i ^ bits) for i in range(count)])  12.6 us
    pallas_call x16, Pallas kernels, call(): pl.pallas_call(body, out_shape=listed, in_specs=in_specs, out_specs=out_s...  7.66 us
    pallas_call x2, Pallas kernels, run_experts(): pl.pallas_call(functools.partial(expert_body if first else rest_body, cop...  3.26 us
    ppermute x2, waiting for transfers between devices, swap_both(): lax.ppermute(block, ('expert', 'tensor'), [(i, i ^ bits) for i in range(c...  3.07 us
    ppermute x2, starting transfers between devices, swap_both(): lax.ppermute(block, ('expert', 'tensor'), [(i, i ^ bits) for i in range(c...  2.97 us
  transfers between devices with their start and end apart: 24, of which 9 were waited for; matrix products, arithmetic and copies ran while one was open for 0% of the time, Pallas kernels for 19%

profile of v5, /device:TPU:0, one launch (start us, length us, event | category | flops | bytes accessed | tf_op | source)
XLA Modules:
  0.0 48.6 jit_solution(2317573056799438859)
XLA Ops:
  0.5 2.0 %project.1 = (bf16[96,128]{1,0:T(8,128)(2,1)S(1)}, bf16[32,128]{1,0:T(8,128)(2,1)S(1)}, bf16[32,1536]{1,0:T(8,128)(2,1)S(1)}, f32[32,128]{1,0:T(8,128)S(1)}, f32...) custom-call(s32[1,3]{1,0:T(1,128)} %length_hbm.1, ...), custom_call_target="tpu_custom_call" | custom-call | flops 50331648 | bytes 2097152 | tf_op jit(solution)/shard_map/project/pallas_call | solution.py:58
  2.6 1.2 %attention.1 = (bf16[32,768]{1,0:T(8,128)(2,1)S(1)}, f32[32,768]{1,0:T(8,128)S(1)}) custom-call(bf16[96,128]{1,0:T(8,128)(2,1)S(1)} %get-tuple-element.39.q_ref, bf16[32,128]{1,0:T(8,128)(2,1)S(1)} %get-tuple-element.40.own_ref, bf16[32,1536]{1,0:T(8,128)(2,1)S(1)} %get-tuple-element.41.normed_ref, bf16[1536,128]{1,0:T(8,128)(2,1)S(1)} %collective-permute-done.other_ref, ...), custom_call_target="tpu_custom_call" | custom-call | flops 37748736 | bytes 1048576 | tf_op jit(solution)/shard_map/attention/pallas_call | solution.py:58
  5.2 4.0 %collective-permute-start.3 = (bf16[32,896]{1,0:T(8,128)(2,1)S(1)}, bf16[32,896]{1,0:T(8,128)(2,1)S(1)}, u32[]{:S(2)}, u32[]{:S(2)}) collective-permute-start(bf16[32,896]{1,0:T(8,128)(2,1)S(1)} %chip_sum.1.refs_0_.own_ref), channel_id=1, source_target_pairs={{0,16},{4,20},{8,24},{12,28},{16,0},{20,4},{24,8},{28,12},{1,17},{... | collective-permute-start | bytes 172040 | tf_op jit(solution)/shard_map/ppermute | solution.py:26
  9.2 1.3 %collective-permute-start.4 = (bf16[32,896]{1,0:T(8,128)(2,1)S(1)}, bf16[32,896]{1,0:T(8,128)(2,1)S(1)}, u32[]{:S(2)}, u32[]{:S(2)}) collective-permute-start(bf16[32,896]{1,0:T(8,128)(2,1)S(1)} %chip_sum.1.refs_0_.own_ref), channel_id=1, source_target_pairs={{0,18},{1,19},{2,16},{3,17},{4,22},{5,23},{6,20},{7,21},{8,26},{9,... | collective-permute-start | bytes 172040 | tf_op jit(solution)/shard_map/ppermute | solution.py:33
  10.7 3.1 %load_experts.1 = (bf16[768,1536]{1,0:T(8,128)(2,1)S(1)}, bf16[768,1536]{1,0:T(8,128)(2,1)S(1)}, bf16[768,1536]{1,0:T(8,128)(2,1)S(1)}) custom-call(bf16[32,896]{1,0:T(8,128)(2,1)S(1)} %chip_sum.1.refs_0_.own_ref, bf16[768,1536]{1,0:T(8,128)(2,1)} %bitcast.12, bf16[768,1536]{1,0:T(8,128)(2,1)} %bitcast.13, bf16[768,1536]{1,0:T(8,128)(2,1)} %bitcast.14), custom_call_target="tpu_custom_call" | custom-call | bytes 8388608 | tf_op jit(solution)/shard_map/load_experts/pallas_call | solution.py:58
  13.8 2.4 %collective-permute-done.4.xy_ref = bf16[32,896]{1,0:T(8,128)(2,1)S(1)} collective-permute-done((bf16[32,896]{1,0:T(8,128)(2,1)S(1)}, bf16[32,896]{1,0:T(8,128)(2,1)S(1)}, u32[]{:S(2)}, u32[]{:S(2)}) %collective-permute-start.4) | collective-permute-done | bytes 57376 | tf_op jit(solution)/shard_map/ppermute | solution.py:33
  16.5 1.6 %collective-permute-start.8 = (bf16[64,896]{1,0:T(8,128)(2,1)S(1)}, bf16[64,896]{1,0:T(8,128)(2,1)S(1)}, u32[]{:S(2)}, u32[]{:S(2)}) collective-permute-start(bf16[64,896]{1,0:T(8,128)(2,1)S(1)} %get-tuple-element.56.refs_0_), channel_id=1, source_target_pairs={{0,12},{4,8},{8,4},{12,0},{16,28},{20,24},{24,20},{28,16},{1,13},{... | collective-permute-start | bytes 344072 | tf_op jit(solution)/shard_map/ppermute | solution.py:26
  18.6 1.4 %collective-permute-start.10 = (bf16[64,896]{1,0:T(8,128)(2,1)S(1)}, bf16[64,896]{1,0:T(8,128)(2,1)S(1)}, u32[]{:S(2)}, u32[]{:S(2)}) collective-permute-start(bf16[64,896]{1,0:T(8,128)(2,1)S(1)} %get-tuple-element.56.refs_0_), channel_id=1, source_target_pairs={{0,8},{4,12},{8,0},{12,4},{16,24},{20,28},{24,16},{28,20},{1,9},{5... | collective-permute-start | bytes 344072 | tf_op jit(solution)/shard_map/ppermute | solution.py:26
  20.1 1.9 %experts.2 = (bf16[1,64,768]{2,1,0:T(8,128)(2,1)S(1)}, bf16[64,768]{1,0:T(8,128)(2,1)S(1)}) custom-call(bf16[64,896]{1,0:T(8,128)(2,1)S(1)} %get-tuple-element.56.refs_0_, bf16[64,896]{1,0:T(8,128)(2,1)S(1)} %collective-permute-done.6.refs_1_, bf16[768,1536]{1,0:T(8,128)(2,1)S(1)} %get-tuple-element.55.loaded_ref.refs_2_.refs_3_.refs_6_, ...), custom_call_target="tpu_custom_call" | custom-call | flops 1 | bytes 1 | tf_op jit(solution)/shard_map/experts/pallas_call | solution.py:473
  22.1 1.4 %collective-permute-done.8.block_ref = bf16[64,896]{1,0:T(8,128)(2,1)S(1)} collective-permute-done((bf16[64,896]{1,0:T(8,128)(2,1)S(1)}, bf16[64,896]{1,0:T(8,128)(2,1)S(1)}, u32[]{:S(2)}, u32[]{:S(2)}) %collective-permute-start.8) | collective-permute-done | bytes 114720 | tf_op jit(solution)/shard_map/ppermute | solution.py:26
  23.5 1.9 %collective-permute-done.9.block_ref = bf16[64,896]{1,0:T(8,128)(2,1)S(1)} collective-permute-done((bf16[64,896]{1,0:T(8,128)(2,1)S(1)}, bf16[64,896]{1,0:T(8,128)(2,1)S(1)}, u32[]{:S(2)}, u32[]{:S(2)}) %collective-permute-start.9) | collective-permute-done | bytes 114720 | tf_op jit(solution)/shard_map/ppermute | solution.py:26
  26.1 1.0 %experts_half_depth.1 = (f32[3,64,768]{2,1,0:T(8,128)S(1)}, f32[3,64,768]{2,1,0:T(8,128)S(1)}) custom-call(bf16[64,896]{1,0:T(8,128)(2,1)S(1)} %relay.3.refs_0_, bf16[64,896]{1,0:T(8,128)(2,1)S(1)} %relay.4.refs_1_, bf16[64,896]{1,0:T(8,128)(2,1)S(1)} %relay.5.refs_2_, bf16[768,1536]{1,0:T(8,128)(2,1)S(1)} %get-tuple-element.55.loaded_ref.refs_2_.refs_3_.refs_6_, ...), custom_call_target="tpu_custom_call" | custom-call | flops 1 | bytes 1 | tf_op jit(solution)/shard_map/experts_half_depth/pallas_call | solution.py:463
  27.1 1.4 %experts.3 = (bf16[3,64,768]{2,1,0:T(8,128)(2,1)S(1)}, bf16[64,768]{1,0:T(8,128)(2,1)S(1)}, bf16[64,768]{1,0:T(8,128)(2,1)S(1)}, bf16[64,768]{1,0:T(8,128)(2,1)S(1)}) custom-call(bf16[64,896]{1,0:T(8,128)(2,1)S(1)} %relay.3.refs_0_, bf16[64,896]{1,0:T(8,128)(2,1)S(1)} %relay.4.refs_1_, bf16[64,896]{1,0:T(8,128)(2,1)S(1)} %relay.5.refs_2_, ...), custom_call_target="tpu_custom_call" | custom-call | flops 1 | bytes 1 | tf_op jit(solution)/shard_map/experts/pallas_call | solution.py:473
  29.9 1.6 %collective-permute-start.15 = (bf16[64,768]{1,0:T(8,128)(2,1)S(1)}, bf16[64,768]{1,0:T(8,128)(2,1)S(1)}, u32[]{:S(2)}, u32[]{:S(2)}) collective-permute-start(bf16[64,768]{1,0:T(8,128)(2,1)S(1)} %chip_sums.5), channel_id=1, source_target_pairs={{0,12},{4,8},{8,4},{12,0},{16,28},{20,24},{24,20},{28,16},{1,13},{... | collective-permute-start | bytes 294920 | tf_op jit(solution)/shard_map/ppermute | solution.py:26
  32.1 1.5 %collective-permute-start.19 = (bf16[64,768]{1,0:T(8,128)(2,1)S(1)}, bf16[64,768]{1,0:T(8,128)(2,1)S(1)}, u32[]{:S(2)}, u32[]{:S(2)}) collective-permute-start(bf16[64,768]{1,0:T(8,128)(2,1)S(1)} %chip_sums.7), channel_id=1, source_target_pairs={{0,8},{4,12},{8,0},{12,4},{16,24},{20,28},{24,16},{28,20},{1,9},{5... | collective-permute-start | bytes 294920 | tf_op jit(solution)/shard_map/ppermute | solution.py:26
  33.9 2.2 %collective-permute-done.15.refs_1_ = bf16[64,768]{1,0:T(8,128)(2,1)S(1)} collective-permute-done((bf16[64,768]{1,0:T(8,128)(2,1)S(1)}, bf16[64,768]{1,0:T(8,128)(2,1)S(1)}, u32[]{:S(2)}, u32[]{:S(2)}) %collective-permute-start.15) | collective-permute-done | bytes 98336 | tf_op jit(solution)/shard_map/ppermute | solution.py:26
  36.1 1.8 %collective-permute-done.17.refs_2_ = bf16[64,768]{1,0:T(8,128)(2,1)S(1)} collective-permute-done((bf16[64,768]{1,0:T(8,128)(2,1)S(1)}, bf16[64,768]{1,0:T(8,128)(2,1)S(1)}, u32[]{:S(2)}, u32[]{:S(2)}) %collective-permute-start.17) | collective-permute-done | bytes 98336 | tf_op jit(solution)/shard_map/ppermute | solution.py:26
  38.0 1.6 %collective-permute-start.20 = (bf16[32,768]{1,0:T(8,128)(2,1)S(1)}, bf16[32,768]{1,0:T(8,128)(2,1)S(1)}, u32[]{:S(2)}, u32[]{:S(2)}) collective-permute-start(bf16[32,768]{1,0:T(8,128)(2,1)S(1)} %get-tuple-element.68), channel_id=1, source_target_pairs={{0,2},{1,3},{2,0},{3,1},{4,6},{5,7},{6,4},{7,5},{8,10},{9,11},{10,... | collective-permute-start | bytes 147464 | tf_op jit(solution)/shard_map/ppermute | solution.py:26
  39.5 1.2 %collective-permute-start.21 = (bf16[32,768]{1,0:T(8,128)(2,1)S(1)}, bf16[32,768]{1,0:T(8,128)(2,1)S(1)}, u32[]{:S(2)}, u32[]{:S(2)}) collective-permute-start(bf16[32,768]{1,0:T(8,128)(2,1)S(1)} %get-tuple-element.69), channel_id=1, source_target_pairs={{0,16},{4,20},{8,24},{12,28},{16,0},{20,4},{24,8},{28,12},{1,17},{... | collective-permute-start | bytes 147464 | tf_op jit(solution)/shard_map/ppermute | solution.py:26
  40.7 1.7 %collective-permute-start.22 = (bf16[32,768]{1,0:T(8,128)(2,1)S(1)}, bf16[32,768]{1,0:T(8,128)(2,1)S(1)}, u32[]{:S(2)}, u32[]{:S(2)}) collective-permute-start(bf16[32,768]{1,0:T(8,128)(2,1)S(1)} %get-tuple-element.69), channel_id=1, source_target_pairs={{0,18},{1,19},{2,16},{3,17},{4,22},{5,23},{6,20},{7,21},{8,26},{9,... | collective-permute-start | bytes 147464 | tf_op jit(solution)/shard_map/ppermute | solution.py:33
  42.4 3.5 %collective-permute-done.21.y_ref = bf16[32,768]{1,0:T(8,128)(2,1)S(1)} collective-permute-done((bf16[32,768]{1,0:T(8,128)(2,1)S(1)}, bf16[32,768]{1,0:T(8,128)(2,1)S(1)}, u32[]{:S(2)}, u32[]{:S(2)}) %collective-permute-start.21) | collective-permute-done | bytes 49184 | tf_op jit(solution)/shard_map/ppermute | solution.py:26
  46.0 0.6 %collective-permute-done.22.xy_ref = bf16[32,768]{1,0:T(8,128)(2,1)S(1)} collective-permute-done((bf16[32,768]{1,0:T(8,128)(2,1)S(1)}, bf16[32,768]{1,0:T(8,128)(2,1)S(1)}, u32[]{:S(2)}, u32[]{:S(2)}) %collective-permute-start.22) | collective-permute-done | bytes 49184 | tf_op jit(solution)/shard_map/ppermute | solution.py:33
  46.8 1.2 %collective-permute-done.23.b_ref = f32[32,128]{1,0:T(8,128)S(1)} collective-permute-done((f32[32,128]{1,0:T(8,128)S(1)}, f32[32,128]{1,0:T(8,128)S(1)}, u32[]{:S(2)}, u32[]{:S(2)}) %collective-permute-start.23) | collective-permute-done | bytes 16416 | tf_op jit(solution)/shard_map/ppermute | solution.py:26
  47.9 0.7 %finish.1 = bf16[32,384]{1,0:T(8,128)(2,1)} custom-call(f32[32,384]{1,0:T(8,128)S(1)} %get-tuple-element.71.combined_ref, bf16[1,384]{1,0:T(2,128)(2,1)S(1)} %broadcast_in_dim.11.gain_ref, f32[32,128]{1,0:T(8,128)S(1)} %get-tuple-element.72.a_ref, f32[32,128]{1,0:T(8,128)S(1)} %collective-permute-done.23.b_ref), custom_call_target="tpu_custom_call" | custom-call | flops 49152 | bytes 262144 | tf_op jit(solution)/shard_map/finish/pallas_call | solution.py:58
  (53 shorter events, 6.2 us)
Async XLA Ops:
  0.0 2.5 %collective-permute-start = (bf16[1536,128]{1,0:T(8,128)(2,1)}, bf16[1536,128]{1,0:T(8,128)(2,1)S(1)}, u32[]{:S(2)}, u32[]{:S(2)}) collective-permute-start(bf16[1536,128]{1,0:T(8,128)(2,1)} %bitcast.15), channel_id=1, source_target_pairs={{0,1},{1,0},{2,3},{3,2},{4,5},{5,4},{6,7},{7,6},{8,9},{9,8},{10,11... | collective-permute-start | bytes 1179656 | tf_op jit(solution)/shard_map/ppermute | solution.py:26
  0.5 2.1 %collective-permute-start.1 = (bf16[768,128]{1,0:T(8,128)(2,1)}, bf16[768,128]{1,0:T(8,128)(2,1)S(1)}, u32[]{:S(2)}, u32[]{:S(2)}) collective-permute-start(bf16[768,128]{1,0:T(8,128)(2,1)} %bitcast.16), channel_id=1, source_target_pairs={{0,1},{1,0},{2,3},{3,2},{4,5},{5,4},{6,7},{7,6},{8,9},{9,8},{10,11... | collective-permute-start | bytes 589832 | tf_op jit(solution)/shard_map/ppermute | solution.py:26
  3.8 1.4 %collective-permute-start.2 = (bf16[32,768]{1,0:T(8,128)(2,1)S(1)}, bf16[32,768]{1,0:T(8,128)(2,1)S(1)}, u32[]{:S(2)}, u32[]{:S(2)}) collective-permute-start(bf16[32,768]{1,0:T(8,128)(2,1)S(1)} %get-tuple-element.54.sent_ref), channel_id=1, source_target_pairs={{0,1},{1,0},{2,3},{3,2},{4,5},{5,4},{6,7},{7,6},{8,9},{9,8},{10,11... | collective-permute-start | bytes 147464 | tf_op jit(solution)/shard_map/ppermute | solution.py:26
  5.2 8.7 %collective-permute-start.3 = (bf16[32,896]{1,0:T(8,128)(2,1)S(1)}, bf16[32,896]{1,0:T(8,128)(2,1)S(1)}, u32[]{:S(2)}, u32[]{:S(2)}) collective-permute-start(bf16[32,896]{1,0:T(8,128)(2,1)S(1)} %chip_sum.1.refs_0_.own_ref), channel_id=1, source_target_pairs={{0,16},{4,20},{8,24},{12,28},{16,0},{20,4},{24,8},{28,12},{1,17},{... | collective-permute-start | bytes 172040 | tf_op jit(solution)/shard_map/ppermute | solution.py:26
  9.2 7.1 %collective-permute-start.4 = (bf16[32,896]{1,0:T(8,128)(2,1)S(1)}, bf16[32,896]{1,0:T(8,128)(2,1)S(1)}, u32[]{:S(2)}, u32[]{:S(2)}) collective-permute-start(bf16[32,896]{1,0:T(8,128)(2,1)S(1)} %chip_sum.1.refs_0_.own_ref), channel_id=1, source_target_pairs={{0,18},{1,19},{2,16},{3,17},{4,22},{5,23},{6,20},{7,21},{8,26},{9,... | collective-permute-start | bytes 172040 | tf_op jit(solution)/shard_map/ppermute | solution.py:33
  10.4 5.9 %collective-permute-start.5 = (bf16[32,896]{1,0:T(8,128)(2,1)S(1)}, bf16[32,896]{1,0:T(8,128)(2,1)S(1)}, u32[]{:S(2)}, u32[]{:S(2)}) collective-permute-start(bf16[32,896]{1,0:T(8,128)(2,1)S(1)} %chip_sum.1.refs_0_.own_ref), channel_id=1, source_target_pairs={{0,2},{1,3},{2,0},{3,1},{4,6},{5,7},{6,4},{7,5},{8,10},{9,11},{10,... | collective-permute-start | bytes 172040 | tf_op jit(solution)/shard_map/ppermute | solution.py:26
  16.4 3.6 %collective-permute-start.6 = (bf16[64,896]{1,0:T(8,128)(2,1)S(1)}, bf16[64,896]{1,0:T(8,128)(2,1)S(1)}, u32[]{:S(2)}, u32[]{:S(2)}) collective-permute-start(bf16[64,896]{1,0:T(8,128)(2,1)S(1)} %get-tuple-element.56.refs_0_), channel_id=1, source_target_pairs={{0,1},{1,0},{2,3},{3,2},{4,5},{5,4},{6,7},{7,6},{8,9},{9,8},{10,11... | collective-permute-start | bytes 344072 | tf_op jit(solution)/shard_map/ppermute | solution.py:26
  16.5 6.9 %collective-permute-start.8 = (bf16[64,896]{1,0:T(8,128)(2,1)S(1)}, bf16[64,896]{1,0:T(8,128)(2,1)S(1)}, u32[]{:S(2)}, u32[]{:S(2)}) collective-permute-start(bf16[64,896]{1,0:T(8,128)(2,1)S(1)} %get-tuple-element.56.refs_0_), channel_id=1, source_target_pairs={{0,12},{4,8},{8,4},{12,0},{16,28},{20,24},{24,20},{28,16},{1,13},{... | collective-permute-start | bytes 344072 | tf_op jit(solution)/shard_map/ppermute | solution.py:26
  18.1 7.3 %collective-permute-start.9 = (bf16[64,896]{1,0:T(8,128)(2,1)S(1)}, bf16[64,896]{1,0:T(8,128)(2,1)S(1)}, u32[]{:S(2)}, u32[]{:S(2)}) collective-permute-start(bf16[64,896]{1,0:T(8,128)(2,1)S(1)} %get-tuple-element.56.refs_0_), channel_id=1, source_target_pairs={{0,4},{4,0},{8,12},{12,8},{16,20},{20,16},{24,28},{28,24},{1,5},{5... | collective-permute-start | bytes 344072 | tf_op jit(solution)/shard_map/ppermute | solution.py:26
  18.6 6.9 %collective-permute-start.10 = (bf16[64,896]{1,0:T(8,128)(2,1)S(1)}, bf16[64,896]{1,0:T(8,128)(2,1)S(1)}, u32[]{:S(2)}, u32[]{:S(2)}) collective-permute-start(bf16[64,896]{1,0:T(8,128)(2,1)S(1)} %get-tuple-element.56.refs_0_), channel_id=1, source_target_pairs={{0,8},{4,12},{8,0},{12,4},{16,24},{20,28},{24,16},{28,20},{1,9},{5... | collective-permute-start | bytes 344072 | tf_op jit(solution)/shard_map/ppermute | solution.py:26
  22.0 3.5 %collective-permute-start.7 = (bf16[64,768]{1,0:T(8,128)(2,1)S(1)}, bf16[64,768]{1,0:T(8,128)(2,1)S(1)}, u32[]{:S(2)}, u32[]{:S(2)}) collective-permute-start(bf16[64,768]{1,0:T(8,128)(2,1)S(1)} %get-tuple-element.60.refs_0_), channel_id=1, source_target_pairs={{0,1},{1,0},{2,3},{3,2},{4,5},{5,4},{6,7},{7,6},{8,9},{9,8},{10,11... | collective-permute-start | bytes 294920 | tf_op jit(solution)/shard_map/ppermute | solution.py:26
  23.4 3.6 %collective-permute-start.11 = (bf16[64,896]{1,0:T(8,128)(2,1)S(1)}, bf16[64,896]{1,0:T(8,128)(2,1)S(1)}, u32[]{:S(2)}, u32[]{:S(2)}) collective-permute-start(bf16[64,896]{1,0:T(8,128)(2,1)S(1)} %relay.3.refs_0_), channel_id=1, source_target_pairs={{0,1},{1,0},{2,3},{3,2},{4,5},{5,4},{6,7},{7,6},{8,9},{9,8},{10,11... | collective-permute-start | bytes 344072 | tf_op jit(solution)/shard_map/ppermute | solution.py:26
  25.4 1.6 %collective-permute-start.12 = (bf16[64,896]{1,0:T(8,128)(2,1)S(1)}, bf16[64,896]{1,0:T(8,128)(2,1)S(1)}, u32[]{:S(2)}, u32[]{:S(2)}) collective-permute-start(bf16[64,896]{1,0:T(8,128)(2,1)S(1)} %relay.4.refs_1_), channel_id=1, source_target_pairs={{0,1},{1,0},{2,3},{3,2},{4,5},{5,4},{6,7},{7,6},{8,9},{9,8},{10,11... | collective-permute-start | bytes 344072 | tf_op jit(solution)/shard_map/ppermute | solution.py:26
  25.6 1.5 %collective-permute-start.13 = (bf16[64,896]{1,0:T(8,128)(2,1)S(1)}, bf16[64,896]{1,0:T(8,128)(2,1)S(1)}, u32[]{:S(2)}, u32[]{:S(2)}) collective-permute-start(bf16[64,896]{1,0:T(8,128)(2,1)S(1)} %relay.5.refs_2_), channel_id=1, source_target_pairs={{0,1},{1,0},{2,3},{3,2},{4,5},{5,4},{6,7},{7,6},{8,9},{9,8},{10,11... | collective-permute-start | bytes 344072 | tf_op jit(solution)/shard_map/ppermute | solution.py:26
  28.5 1.4 %collective-permute-start.14 = (bf16[64,768]{1,0:T(8,128)(2,1)S(1)}, bf16[64,768]{1,0:T(8,128)(2,1)S(1)}, u32[]{:S(2)}, u32[]{:S(2)}) collective-permute-start(bf16[64,768]{1,0:T(8,128)(2,1)S(1)} %get-tuple-element.64), channel_id=1, source_target_pairs={{0,1},{1,0},{2,3},{3,2},{4,5},{5,4},{6,7},{7,6},{8,9},{9,8},{10,11... | collective-permute-start | bytes 294920 | tf_op jit(solution)/shard_map/ppermute | solution.py:26
  28.8 2.7 %collective-permute-start.16 = (bf16[64,768]{1,0:T(8,128)(2,1)S(1)}, bf16[64,768]{1,0:T(8,128)(2,1)S(1)}, u32[]{:S(2)}, u32[]{:S(2)}) collective-permute-start(bf16[64,768]{1,0:T(8,128)(2,1)S(1)} %get-tuple-element.65), channel_id=1, source_target_pairs={{0,1},{1,0},{2,3},{3,2},{4,5},{5,4},{6,7},{7,6},{8,9},{9,8},{10,11... | collective-permute-start | bytes 294920 | tf_op jit(solution)/shard_map/ppermute | solution.py:26
  29.0 3.1 %collective-permute-start.18 = (bf16[64,768]{1,0:T(8,128)(2,1)S(1)}, bf16[64,768]{1,0:T(8,128)(2,1)S(1)}, u32[]{:S(2)}, u32[]{:S(2)}) collective-permute-start(bf16[64,768]{1,0:T(8,128)(2,1)S(1)} %get-tuple-element.66), channel_id=1, source_target_pairs={{0,1},{1,0},{2,3},{3,2},{4,5},{5,4},{6,7},{7,6},{8,9},{9,8},{10,11... | collective-permute-start | bytes 294920 | tf_op jit(solution)/shard_map/ppermute | solution.py:26
  29.9 6.3 %collective-permute-start.15 = (bf16[64,768]{1,0:T(8,128)(2,1)S(1)}, bf16[64,768]{1,0:T(8,128)(2,1)S(1)}, u32[]{:S(2)}, u32[]{:S(2)}) collective-permute-start(bf16[64,768]{1,0:T(8,128)(2,1)S(1)} %chip_sums.5), channel_id=1, source_target_pairs={{0,12},{4,8},{8,4},{12,0},{16,28},{20,24},{24,20},{28,16},{1,13},{... | collective-permute-start | bytes 294920 | tf_op jit(solution)/shard_map/ppermute | solution.py:26
  31.5 6.4 %collective-permute-start.17 = (bf16[64,768]{1,0:T(8,128)(2,1)S(1)}, bf16[64,768]{1,0:T(8,128)(2,1)S(1)}, u32[]{:S(2)}, u32[]{:S(2)}) collective-permute-start(bf16[64,768]{1,0:T(8,128)(2,1)S(1)} %chip_sums.6), channel_id=1, source_target_pairs={{0,4},{4,0},{8,12},{12,8},{16,20},{20,16},{24,28},{28,24},{1,5},{5... | collective-permute-start | bytes 294920 | tf_op jit(solution)/shard_map/ppermute | solution.py:26
  32.1 5.8 %collective-permute-start.19 = (bf16[64,768]{1,0:T(8,128)(2,1)S(1)}, bf16[64,768]{1,0:T(8,128)(2,1)S(1)}, u32[]{:S(2)}, u32[]{:S(2)}) collective-permute-start(bf16[64,768]{1,0:T(8,128)(2,1)S(1)} %chip_sums.7), channel_id=1, source_target_pairs={{0,8},{4,12},{8,0},{12,4},{16,24},{20,28},{24,16},{28,20},{1,9},{5... | collective-permute-start | bytes 294920 | tf_op jit(solution)/shard_map/ppermute | solution.py:26
  38.0 4.5 %collective-permute-start.20 = (bf16[32,768]{1,0:T(8,128)(2,1)S(1)}, bf16[32,768]{1,0:T(8,128)(2,1)S(1)}, u32[]{:S(2)}, u32[]{:S(2)}) collective-permute-start(bf16[32,768]{1,0:T(8,128)(2,1)S(1)} %get-tuple-element.68), channel_id=1, source_target_pairs={{0,2},{1,3},{2,0},{3,1},{4,6},{5,7},{6,4},{7,5},{8,10},{9,11},{10,... | collective-permute-start | bytes 147464 | tf_op jit(solution)/shard_map/ppermute | solution.py:26
  39.5 6.4 %collective-permute-start.21 = (bf16[32,768]{1,0:T(8,128)(2,1)S(1)}, bf16[32,768]{1,0:T(8,128)(2,1)S(1)}, u32[]{:S(2)}, u32[]{:S(2)}) collective-permute-start(bf16[32,768]{1,0:T(8,128)(2,1)S(1)} %get-tuple-element.69), channel_id=1, source_target_pairs={{0,16},{4,20},{8,24},{12,28},{16,0},{20,4},{24,8},{28,12},{1,17},{... | collective-permute-start | bytes 147464 | tf_op jit(solution)/shard_map/ppermute | solution.py:26
  40.7 5.9 %collective-permute-start.22 = (bf16[32,768]{1,0:T(8,128)(2,1)S(1)}, bf16[32,768]{1,0:T(8,128)(2,1)S(1)}, u32[]{:S(2)}, u32[]{:S(2)}) collective-permute-start(bf16[32,768]{1,0:T(8,128)(2,1)S(1)} %get-tuple-element.69), channel_id=1, source_target_pairs={{0,18},{1,19},{2,16},{3,17},{4,22},{5,23},{6,20},{7,21},{8,26},{9,... | collective-permute-start | bytes 147464 | tf_op jit(solution)/shard_map/ppermute | solution.py:33
  46.7 1.2 %collective-permute-start.23 = (f32[32,128]{1,0:T(8,128)S(1)}, f32[32,128]{1,0:T(8,128)S(1)}, u32[]{:S(2)}, u32[]{:S(2)}) collective-permute-start(f32[32,128]{1,0:T(8,128)S(1)} %get-tuple-element.72.a_ref), channel_id=1, source_target_pairs={{0,1},{1,0},{2,3},{3,2},{4,5},{5,4},{6,7},{7,6},{8,9},{9,8},{10,11... | collective-permute-start | bytes 49160 | tf_op jit(solution)/shard_map/ppermute | solution.py:26
  (3 other events, 28.5 us)

commit v6 on v5

--- a/solution.py
+++ b/solution.py
@@ -253,16 +253,17 @@
     lane = iota((rows, total - width), 1)
     for i, (a_ref, b_ref) in enumerate(((own_ref, x_ref), (y_ref, xy_ref))):
         span = slice(i * rows, (i + 1) * rows)
-        squares = jnp.zeros((rows, 1), F32)
+        part = (a_ref[:, :width].astype(F32) + b_ref[:, :width].astype(F32)).astype(BF16)
+        if i == 0:
+            keep_ref[...] = part
+        wide = part.astype(F32)
+        squares = jnp.sum(wide * wide, axis=1, keepdims=True)
+        scaled = wide * lax.rsqrt(squares / (2 * width) + EPSILON)
         for k in range(2):
             cols = slice(k * quarter, (k + 1) * quarter)
-            part = (a_ref[:, cols].astype(F32) + b_ref[:, cols].astype(F32)).astype(BF16)
-            wide = part.astype(F32)
-            squares = squares + jnp.sum(wide * wide, axis=1, keepdims=True)
-            rows_ref[span, cols] = (wide * gain[k]).astype(BF16)
-            if i == 0:
-                keep_ref[:, cols] = part
+            rows_ref[span, cols] = (scaled[:, cols] * gain[k]).astype(BF16)
         extra = a_ref[:, width:].astype(F32) + b_ref[:, width:].astype(F32)
+        squares = squares * 0.5
         high = squares.astype(BF16).astype(F32)
         extra = jnp.where(lane == 2 * copies, high, extra)
         extra = jnp.where(lane == 2 * copies + 1, squares - high, extra)
@@ -284,41 +285,6 @@
         load.wait()
 
 
-def expert_body(copies, hosted, blocks, *refs):
-    own_refs, other_refs = refs[:blocks], refs[blocks : 2 * blocks]
-    gate_ref, up_ref, down_ref, hidden_ref = refs[2 * blocks : 2 * blocks + 4]
-    send_refs = refs[2 * blocks + 4 :]
-    width = gate_ref.shape[1]
-    units = gate_ref.shape[0] // hosted
-    quarter = width // 4
-    own = jnp.concatenate([r[...] for r in own_refs], axis=0)
-    other = jnp.concatenate([r[...] for r in other_refs], axis=0)
-    parts = []
-    for i in range(4):
-        span = slice(i // 2 * quarter, (i // 2 + 1) * quarter)
-        mine = is_key() if i % 2 == 0 else jnp.logical_not(is_key())
-        parts.append(jnp.where(mine, own[:, span], other[:, span]))
-    rows = jnp.concatenate(parts, axis=1)
-    extra = own[:, 2 * quarter :].astype(F32)
-    lane = iota(extra.shape, 1)
-    squares = jnp.where((lane == 2 * copies) | (lane == 2 * copies + 1), extra + other[:, 2 * quarter :].astype(F32), 0.0)
-    scale = lax.rsqrt(jnp.sum(squares, axis=1, keepdims=True) / width + EPSILON)
-    tall = rows.shape[0] // blocks
-    parts = []
-    for j in range(hosted):
-        slot = lax.axis_index("expert") * hosted + j
-        one = jnp.where((lane == slot) | (lane == slot + copies), extra, 0.0)
-        weight = jnp.sum(one, axis=1, keepdims=True)
-        span = slice(j * units, (j + 1) * units)
-        gate = dot_t(rows, gate_ref[span, :]) * scale
-        up = dot_t(rows, up_ref[span, :]) * scale
-        parts.append((jnp.maximum(gate, 0.0) * up * weight).astype(BF16))
-    hidden = jnp.concatenate(parts, axis=1)
-    for b in range(blocks):
-        hidden_ref[b] = hidden[b * tall : (b + 1) * tall]
-    send_half(hidden, down_ref, send_refs)
-
-
 def tiles(units):
     step = 256 if units % 256 == 0 else units
     return [slice(i, i + step) for i in range(0, units, step)]
@@ -342,24 +308,31 @@
             out_ref[:, :, span] = total.reshape(blocks, -1, total.shape[1])
 
 
-def rest_body(copies, hosted, blocks, *refs):
+def expert_body(copies, hosted, blocks, *refs):
     own_refs, other_refs = refs[:blocks], refs[blocks : 2 * blocks]
-    gate_ref, up_ref, down_ref, gate_half, up_half, hidden_ref = refs[2 * blocks : 2 * blocks + 6]
-    send_refs = refs[2 * blocks + 6 :]
+    gate_ref, up_ref, down_ref = refs[2 * blocks : 2 * blocks + 3]
+    half_refs = refs[2 * blocks + 3 : -1 - blocks]
+    hidden_ref, send_refs = refs[-1 - blocks], refs[-blocks:]
     total, width = gate_ref.shape
     units = total // hosted
     quarter = width // 4
+    core = lax.axis_index("tensor") % 2
     extra = jnp.concatenate([r[:, 2 * quarter :] for r in own_refs], axis=0).astype(F32)
     far_extra = jnp.concatenate([r[:, 2 * quarter :] for r in other_refs], axis=0).astype(F32)
     lane = iota(extra.shape, 1)
-    squares = jnp.where((lane == 2 * copies) | (lane == 2 * copies + 1), extra + far_extra, 0.0)
-    scale = lax.rsqrt(jnp.sum(squares, axis=1, keepdims=True) / width + EPSILON)
+    squared = (lane == 2 * copies) | (lane == 2 * copies + 1)
+    own_mean = jnp.sum(jnp.where(squared, extra, 0.0), axis=1, keepdims=True) * (2.0 / width)
+    far_mean = jnp.sum(jnp.where(squared, far_extra, 0.0), axis=1, keepdims=True) * (2.0 / width)
+    scale = lax.rsqrt(own_mean + far_mean + EPSILON)
+    own_scale = scale * jnp.sqrt(own_mean + EPSILON)
+    far_scale = scale * jnp.sqrt(far_mean + EPSILON)
     weights = []
     for j in range(hosted):
         slot = lax.axis_index("expert") * hosted + j
         one = jnp.where((lane == slot) | (lane == slot + copies), extra, 0.0)
         weights.append(jnp.sum(one, axis=1, keepdims=True))
-    pairs = list(quarters(other_refs, quarter, 1 - lax.axis_index("tensor") % 2))
+    own_pairs = [] if half_refs else list(quarters(own_refs, quarter, core))
+    far_pairs = list(quarters(other_refs, quarter, 1 - core))
     count = extra.shape[0]
     parts = []
     for span in tiles(total):
@@ -368,11 +341,15 @@
         weight = weights[span.start // units]
         for j in range(span.start // units + 1, (span.stop - 1) // units + 1):
             weight = jnp.where(place >= j * units, weights[j], weight)
-        gate, up = gate_half[:, :, span].reshape(count, size), up_half[:, :, span].reshape(count, size)
-        for part, cols in pairs:
-            gate = gate + dot_t(part, gate_ref[span, cols])
-            up = up + dot_t(part, up_ref[span, cols])
-        parts.append((jnp.maximum(gate * scale, 0.0) * (up * scale) * weight).astype(BF16))
+        sums = []
+        for i, weight_ref in enumerate((gate_ref, up_ref)):
+            if half_refs:
+                own = half_refs[i][:, :, span].reshape(count, size)
+            else:
+                own = sum(dot_t(part, weight_ref[span, cols]) for part, cols in own_pairs)
+            far = sum(dot_t(part, weight_ref[span, cols]) for part, cols in far_pairs)
+            sums.append(own * own_scale + far * far_scale)
+        parts.append((jnp.maximum(sums[0], 0.0) * sums[1] * weight).astype(BF16))
     hidden = jnp.concatenate(parts, axis=1)
     tall = count // blocks
     for b in range(blocks):
@@ -426,7 +403,7 @@
     y_ref[...] = total[rows:].astype(BF16)
 
 
-def combine_body(own_ref, x_ref, y_ref, xy_ref, residual_ref, combined_ref, square_ref):
+def combine_body(y_ref, xy_ref, x_ref, own_ref, residual_ref, combined_ref, square_ref):
     quarter = combined_ref.shape[1]
     total = (own_ref[...] + x_ref[...].astype(F32)) + (y_ref[...].astype(F32) + xy_ref[...].astype(F32))
     total = residual_ref[...].astype(F32) + total
@@ -471,7 +448,7 @@
             name="experts_half_depth",
         )(*own, gate_weight, up_weight)
     hidden, *sends = pl.pallas_call(
-        functools.partial(expert_body if first else rest_body, copies, hosted, blocks),
+        functools.partial(expert_body, copies, hosted, blocks),
         grid=grid,
         out_shape=[shape((blocks, tall, units), BF16)] + [shape((tall, width // 2), BF16)] * blocks,
         in_specs=[row_spec] * (2 * blocks) + [whole] * 3 + [hidden_spec] * len(halves),
@@ -629,7 +606,7 @@
     combined, squares = call(
         combine_body,
         [shape((rows, quarter), F32), shape((rows, LANES), F32)],
-        (own, near_x, far_y, far_xy, residual),
+        (far_y, far_xy, near_x, own, residual),
         name="combine",
         cost=(rows * width, 1 << 18),
     )

time: 48.8 us -> 48.8 us (level)
    ppermute x2, waiting for transfers between devices: 3.07 us -> 4.55 us  [swap_both(): lax.ppermute(block, ('expert', 'tensor'), [(i, i ^ bits) for i in range(c...]
    ppermute x22, waiting for transfers between devices: 12.6 us -> 11.2 us  [swap(): return lax.ppermute(block, axis, [(i, i ^ bits) for i in range(count)])]
where the time goes in v6:
time: 48.8 us; the launch traced here: 48.7 us
  starting transfers between devices  20 us (41%)
  waiting for transfers between devices  15.7 us (32%)
  Pallas kernels  12.7 us (26%)
    ppermute x22, starting transfers between devices, swap(): return lax.ppermute(block, axis, [(i, i ^ bits) for i in range(count)])  17 us
    ppermute x22, waiting for transfers between devices, swap(): return lax.ppermute(block, axis, [(i, i ^ bits) for i in range(count)])  11.2 us
    pallas_call x16, Pallas kernels, call(): pl.pallas_call(body, out_shape=listed, in_specs=in_specs, out_specs=out_s...  7.67 us
    ppermute x2, waiting for transfers between devices, swap_both(): lax.ppermute(block, ('expert', 'tensor'), [(i, i ^ bits) for i in range(c...  4.55 us
    pallas_call x2, Pallas kernels, run_experts(): pl.pallas_call(functools.partial(expert_body, copies, hosted, blocks), gr...  3.3 us
    ppermute x2, starting transfers between devices, swap_both(): lax.ppermute(block, ('expert', 'tensor'), [(i, i ^ bits) for i in range(c...  2.99 us
  transfers between devices with their start and end apart: 24, of which 9 were waited for; matrix products, arithmetic and copies ran while one was open for 0% of the time, Pallas kernels for 19%

profile of v6, /device:TPU:0, one launch (start us, length us, event | category | flops | bytes accessed | tf_op | source)
XLA Modules:
  0.0 48.7 jit_solution(5285001440694791315)
XLA Ops:
  0.5 2.0 %project.1 = (bf16[96,128]{1,0:T(8,128)(2,1)S(1)}, bf16[32,128]{1,0:T(8,128)(2,1)S(1)}, bf16[32,1536]{1,0:T(8,128)(2,1)S(1)}, f32[32,128]{1,0:T(8,128)S(1)}, f32...) custom-call(s32[1,3]{1,0:T(1,128)} %length_hbm.1, ...), custom_call_target="tpu_custom_call" | custom-call | flops 50331648 | bytes 2097152 | tf_op jit(solution)/shard_map/project/pallas_call | solution.py:58
  2.6 1.2 %attention.1 = (bf16[32,768]{1,0:T(8,128)(2,1)S(1)}, f32[32,768]{1,0:T(8,128)S(1)}) custom-call(bf16[96,128]{1,0:T(8,128)(2,1)S(1)} %get-tuple-element.39.q_ref, bf16[32,128]{1,0:T(8,128)(2,1)S(1)} %get-tuple-element.40.own_ref, bf16[32,1536]{1,0:T(8,128)(2,1)S(1)} %get-tuple-element.41.normed_ref, bf16[1536,128]{1,0:T(8,128)(2,1)S(1)} %collective-permute-done.other_ref, ...), custom_call_target="tpu_custom_call" | custom-call | flops 37748736 | bytes 1048576 | tf_op jit(solution)/shard_map/attention/pallas_call | solution.py:58
  4.5 0.6 %collective-permute-done.2.got_ref = bf16[32,768]{1,0:T(8,128)(2,1)S(1)} collective-permute-done((bf16[32,768]{1,0:T(8,128)(2,1)S(1)}, bf16[32,768]{1,0:T(8,128)(2,1)S(1)}, u32[]{:S(2)}, u32[]{:S(2)}) %collective-permute-start.2) | collective-permute-done | bytes 49184 | tf_op jit(solution)/shard_map/ppermute | solution.py:26
  5.2 4.0 %collective-permute-start.3 = (bf16[32,896]{1,0:T(8,128)(2,1)S(1)}, bf16[32,896]{1,0:T(8,128)(2,1)S(1)}, u32[]{:S(2)}, u32[]{:S(2)}) collective-permute-start(bf16[32,896]{1,0:T(8,128)(2,1)S(1)} %chip_sum.1.refs_0_.own_ref), channel_id=1, source_target_pairs={{0,16},{4,20},{8,24},{12,28},{16,0},{20,4},{24,8},{28,12},{1,17},{... | collective-permute-start | bytes 172040 | tf_op jit(solution)/shard_map/ppermute | solution.py:26
  9.2 1.3 %collective-permute-start.4 = (bf16[32,896]{1,0:T(8,128)(2,1)S(1)}, bf16[32,896]{1,0:T(8,128)(2,1)S(1)}, u32[]{:S(2)}, u32[]{:S(2)}) collective-permute-start(bf16[32,896]{1,0:T(8,128)(2,1)S(1)} %chip_sum.1.refs_0_.own_ref), channel_id=1, source_target_pairs={{0,18},{1,19},{2,16},{3,17},{4,22},{5,23},{6,20},{7,21},{8,26},{9,... | collective-permute-start | bytes 172040 | tf_op jit(solution)/shard_map/ppermute | solution.py:33
  10.7 3.1 %load_experts.1 = (bf16[768,1536]{1,0:T(8,128)(2,1)S(1)}, bf16[768,1536]{1,0:T(8,128)(2,1)S(1)}, bf16[768,1536]{1,0:T(8,128)(2,1)S(1)}) custom-call(bf16[32,896]{1,0:T(8,128)(2,1)S(1)} %chip_sum.1.refs_0_.own_ref, bf16[768,1536]{1,0:T(8,128)(2,1)} %bitcast.12, bf16[768,1536]{1,0:T(8,128)(2,1)} %bitcast.13, bf16[768,1536]{1,0:T(8,128)(2,1)} %bitcast.14), custom_call_target="tpu_custom_call" | custom-call | bytes 8388608 | tf_op jit(solution)/shard_map/load_experts/pallas_call | solution.py:58
  13.8 2.4 %collective-permute-done.4.xy_ref = bf16[32,896]{1,0:T(8,128)(2,1)S(1)} collective-permute-done((bf16[32,896]{1,0:T(8,128)(2,1)S(1)}, bf16[32,896]{1,0:T(8,128)(2,1)S(1)}, u32[]{:S(2)}, u32[]{:S(2)}) %collective-permute-start.4) | collective-permute-done | bytes 57376 | tf_op jit(solution)/shard_map/ppermute | solution.py:33
  16.5 1.6 %collective-permute-start.8 = (bf16[64,896]{1,0:T(8,128)(2,1)S(1)}, bf16[64,896]{1,0:T(8,128)(2,1)S(1)}, u32[]{:S(2)}, u32[]{:S(2)}) collective-permute-start(bf16[64,896]{1,0:T(8,128)(2,1)S(1)} %get-tuple-element.56.refs_0_), channel_id=1, source_target_pairs={{0,12},{4,8},{8,4},{12,0},{16,28},{20,24},{24,20},{28,16},{1,13},{... | collective-permute-start | bytes 344072 | tf_op jit(solution)/shard_map/ppermute | solution.py:26
  18.6 1.4 %collective-permute-start.10 = (bf16[64,896]{1,0:T(8,128)(2,1)S(1)}, bf16[64,896]{1,0:T(8,128)(2,1)S(1)}, u32[]{:S(2)}, u32[]{:S(2)}) collective-permute-start(bf16[64,896]{1,0:T(8,128)(2,1)S(1)} %get-tuple-element.56.refs_0_), channel_id=1, source_target_pairs={{0,8},{4,12},{8,0},{12,4},{16,24},{20,28},{24,16},{28,20},{1,9},{5... | collective-permute-start | bytes 344072 | tf_op jit(solution)/shard_map/ppermute | solution.py:26
  20.1 1.9 %experts.2 = (bf16[1,64,768]{2,1,0:T(8,128)(2,1)S(1)}, bf16[64,768]{1,0:T(8,128)(2,1)S(1)}) custom-call(bf16[64,896]{1,0:T(8,128)(2,1)S(1)} %get-tuple-element.56.refs_0_, bf16[64,896]{1,0:T(8,128)(2,1)S(1)} %collective-permute-done.6.refs_1_, bf16[768,1536]{1,0:T(8,128)(2,1)S(1)} %get-tuple-element.55.loaded_ref.refs_2_.refs_3_.refs_6_, ...), custom_call_target="tpu_custom_call" | custom-call | flops 1 | bytes 1 | tf_op jit(solution)/shard_map/experts/pallas_call | solution.py:450
  22.0 1.4 %collective-permute-done.8.block_ref = bf16[64,896]{1,0:T(8,128)(2,1)S(1)} collective-permute-done((bf16[64,896]{1,0:T(8,128)(2,1)S(1)}, bf16[64,896]{1,0:T(8,128)(2,1)S(1)}, u32[]{:S(2)}, u32[]{:S(2)}) %collective-permute-start.8) | collective-permute-done | bytes 114720 | tf_op jit(solution)/shard_map/ppermute | solution.py:26
  23.5 1.9 %collective-permute-done.9.block_ref = bf16[64,896]{1,0:T(8,128)(2,1)S(1)} collective-permute-done((bf16[64,896]{1,0:T(8,128)(2,1)S(1)}, bf16[64,896]{1,0:T(8,128)(2,1)S(1)}, u32[]{:S(2)}, u32[]{:S(2)}) %collective-permute-start.9) | collective-permute-done | bytes 114720 | tf_op jit(solution)/shard_map/ppermute | solution.py:26
  26.1 1.0 %experts_half_depth.1 = (f32[3,64,768]{2,1,0:T(8,128)S(1)}, f32[3,64,768]{2,1,0:T(8,128)S(1)}) custom-call(bf16[64,896]{1,0:T(8,128)(2,1)S(1)} %relay.3.refs_0_, bf16[64,896]{1,0:T(8,128)(2,1)S(1)} %relay.4.refs_1_, bf16[64,896]{1,0:T(8,128)(2,1)S(1)} %relay.5.refs_2_, bf16[768,1536]{1,0:T(8,128)(2,1)S(1)} %get-tuple-element.55.loaded_ref.refs_2_.refs_3_.refs_6_, ...), custom_call_target="tpu_custom_call" | custom-call | flops 1 | bytes 1 | tf_op jit(solution)/shard_map/experts_half_depth/pallas_call | solution.py:440
  27.1 1.4 %experts.3 = (bf16[3,64,768]{2,1,0:T(8,128)(2,1)S(1)}, bf16[64,768]{1,0:T(8,128)(2,1)S(1)}, bf16[64,768]{1,0:T(8,128)(2,1)S(1)}, bf16[64,768]{1,0:T(8,128)(2,1)S(1)}) custom-call(bf16[64,896]{1,0:T(8,128)(2,1)S(1)} %relay.3.refs_0_, bf16[64,896]{1,0:T(8,128)(2,1)S(1)} %relay.4.refs_1_, bf16[64,896]{1,0:T(8,128)(2,1)S(1)} %relay.5.refs_2_, ...), custom_call_target="tpu_custom_call" | custom-call | flops 1 | bytes 1 | tf_op jit(solution)/shard_map/experts/pallas_call | solution.py:450
  29.9 1.6 %collective-permute-start.15 = (bf16[64,768]{1,0:T(8,128)(2,1)S(1)}, bf16[64,768]{1,0:T(8,128)(2,1)S(1)}, u32[]{:S(2)}, u32[]{:S(2)}) collective-permute-start(bf16[64,768]{1,0:T(8,128)(2,1)S(1)} %chip_sums.5), channel_id=1, source_target_pairs={{0,12},{4,8},{8,4},{12,0},{16,28},{20,24},{24,20},{28,16},{1,13},{... | collective-permute-start | bytes 294920 | tf_op jit(solution)/shard_map/ppermute | solution.py:26
  32.2 1.5 %collective-permute-start.19 = (bf16[64,768]{1,0:T(8,128)(2,1)S(1)}, bf16[64,768]{1,0:T(8,128)(2,1)S(1)}, u32[]{:S(2)}, u32[]{:S(2)}) collective-permute-start(bf16[64,768]{1,0:T(8,128)(2,1)S(1)} %chip_sums.7), channel_id=1, source_target_pairs={{0,8},{4,12},{8,0},{12,4},{16,24},{20,28},{24,16},{28,20},{1,9},{5... | collective-permute-start | bytes 294920 | tf_op jit(solution)/shard_map/ppermute | solution.py:26
  34.0 2.2 %collective-permute-done.15.refs_1_ = bf16[64,768]{1,0:T(8,128)(2,1)S(1)} collective-permute-done((bf16[64,768]{1,0:T(8,128)(2,1)S(1)}, bf16[64,768]{1,0:T(8,128)(2,1)S(1)}, u32[]{:S(2)}, u32[]{:S(2)}) %collective-permute-start.15) | collective-permute-done | bytes 98336 | tf_op jit(solution)/shard_map/ppermute | solution.py:26
  36.2 1.8 %collective-permute-done.17.refs_2_ = bf16[64,768]{1,0:T(8,128)(2,1)S(1)} collective-permute-done((bf16[64,768]{1,0:T(8,128)(2,1)S(1)}, bf16[64,768]{1,0:T(8,128)(2,1)S(1)}, u32[]{:S(2)}, u32[]{:S(2)}) %collective-permute-start.17) | collective-permute-done | bytes 98336 | tf_op jit(solution)/shard_map/ppermute | solution.py:26
  38.1 2.2 %collective-permute-start.20 = (bf16[32,768]{1,0:T(8,128)(2,1)S(1)}, bf16[32,768]{1,0:T(8,128)(2,1)S(1)}, u32[]{:S(2)}, u32[]{:S(2)}) collective-permute-start(bf16[32,768]{1,0:T(8,128)(2,1)S(1)} %get-tuple-element.67), channel_id=1, source_target_pairs={{0,16},{4,20},{8,24},{12,28},{16,0},{20,4},{24,8},{28,12},{1,17},{... | collective-permute-start | bytes 147464 | tf_op jit(solution)/shard_map/ppermute | solution.py:26
  40.3 1.7 %collective-permute-start.21 = (bf16[32,768]{1,0:T(8,128)(2,1)S(1)}, bf16[32,768]{1,0:T(8,128)(2,1)S(1)}, u32[]{:S(2)}, u32[]{:S(2)}) collective-permute-start(bf16[32,768]{1,0:T(8,128)(2,1)S(1)} %get-tuple-element.67), channel_id=1, source_target_pairs={{0,18},{1,19},{2,16},{3,17},{4,22},{5,23},{6,20},{7,21},{8,26},{9,... | collective-permute-start | bytes 147464 | tf_op jit(solution)/shard_map/ppermute | solution.py:33
  42.5 2.0 %collective-permute-done.20.y_ref = bf16[32,768]{1,0:T(8,128)(2,1)S(1)} collective-permute-done((bf16[32,768]{1,0:T(8,128)(2,1)S(1)}, bf16[32,768]{1,0:T(8,128)(2,1)S(1)}, u32[]{:S(2)}, u32[]{:S(2)}) %collective-permute-start.20) | collective-permute-done | bytes 49184 | tf_op jit(solution)/shard_map/ppermute | solution.py:26
  44.5 2.1 %collective-permute-done.21.xy_ref = bf16[32,768]{1,0:T(8,128)(2,1)S(1)} collective-permute-done((bf16[32,768]{1,0:T(8,128)(2,1)S(1)}, bf16[32,768]{1,0:T(8,128)(2,1)S(1)}, u32[]{:S(2)}, u32[]{:S(2)}) %collective-permute-start.21) | collective-permute-done | bytes 49184 | tf_op jit(solution)/shard_map/ppermute | solution.py:33
  46.8 1.2 %collective-permute-done.23.b_ref = f32[32,128]{1,0:T(8,128)S(1)} collective-permute-done((f32[32,128]{1,0:T(8,128)S(1)}, f32[32,128]{1,0:T(8,128)S(1)}, u32[]{:S(2)}, u32[]{:S(2)}) %collective-permute-start.23) | collective-permute-done | bytes 16416 | tf_op jit(solution)/shard_map/ppermute | solution.py:26
  48.0 0.7 %finish.1 = bf16[32,384]{1,0:T(8,128)(2,1)} custom-call(f32[32,384]{1,0:T(8,128)S(1)} %get-tuple-element.71.combined_ref, bf16[1,384]{1,0:T(2,128)(2,1)S(1)} %broadcast_in_dim.11.gain_ref, f32[32,128]{1,0:T(8,128)S(1)} %get-tuple-element.72.a_ref, f32[32,128]{1,0:T(8,128)S(1)} %collective-permute-done.23.b_ref), custom_call_target="tpu_custom_call" | custom-call | flops 49152 | bytes 262144 | tf_op jit(solution)/shard_map/finish/pallas_call | solution.py:58
  (53 shorter events, 6.2 us)
Async XLA Ops:
  0.0 2.5 %collective-permute-start = (bf16[1536,128]{1,0:T(8,128)(2,1)}, bf16[1536,128]{1,0:T(8,128)(2,1)S(1)}, u32[]{:S(2)}, u32[]{:S(2)}) collective-permute-start(bf16[1536,128]{1,0:T(8,128)(2,1)} %bitcast.15), channel_id=1, source_target_pairs={{0,1},{1,0},{2,3},{3,2},{4,5},{5,4},{6,7},{7,6},{8,9},{9,8},{10,11... | collective-permute-start | bytes 1179656 | tf_op jit(solution)/shard_map/ppermute | solution.py:26
  0.5 2.1 %collective-permute-start.1 = (bf16[768,128]{1,0:T(8,128)(2,1)}, bf16[768,128]{1,0:T(8,128)(2,1)S(1)}, u32[]{:S(2)}, u32[]{:S(2)}) collective-permute-start(bf16[768,128]{1,0:T(8,128)(2,1)} %bitcast.16), channel_id=1, source_target_pairs={{0,1},{1,0},{2,3},{3,2},{4,5},{5,4},{6,7},{7,6},{8,9},{9,8},{10,11... | collective-permute-start | bytes 589832 | tf_op jit(solution)/shard_map/ppermute | solution.py:26
  3.8 1.4 %collective-permute-start.2 = (bf16[32,768]{1,0:T(8,128)(2,1)S(1)}, bf16[32,768]{1,0:T(8,128)(2,1)S(1)}, u32[]{:S(2)}, u32[]{:S(2)}) collective-permute-start(bf16[32,768]{1,0:T(8,128)(2,1)S(1)} %get-tuple-element.54.sent_ref), channel_id=1, source_target_pairs={{0,1},{1,0},{2,3},{3,2},{4,5},{5,4},{6,7},{7,6},{8,9},{9,8},{10,11... | collective-permute-start | bytes 147464 | tf_op jit(solution)/shard_map/ppermute | solution.py:26
  5.2 8.7 %collective-permute-start.3 = (bf16[32,896]{1,0:T(8,128)(2,1)S(1)}, bf16[32,896]{1,0:T(8,128)(2,1)S(1)}, u32[]{:S(2)}, u32[]{:S(2)}) collective-permute-start(bf16[32,896]{1,0:T(8,128)(2,1)S(1)} %chip_sum.1.refs_0_.own_ref), channel_id=1, source_target_pairs={{0,16},{4,20},{8,24},{12,28},{16,0},{20,4},{24,8},{28,12},{1,17},{... | collective-permute-start | bytes 172040 | tf_op jit(solution)/shard_map/ppermute | solution.py:26
  9.2 7.1 %collective-permute-start.4 = (bf16[32,896]{1,0:T(8,128)(2,1)S(1)}, bf16[32,896]{1,0:T(8,128)(2,1)S(1)}, u32[]{:S(2)}, u32[]{:S(2)}) collective-permute-start(bf16[32,896]{1,0:T(8,128)(2,1)S(1)} %chip_sum.1.refs_0_.own_ref), channel_id=1, source_target_pairs={{0,18},{1,19},{2,16},{3,17},{4,22},{5,23},{6,20},{7,21},{8,26},{9,... | collective-permute-start | bytes 172040 | tf_op jit(solution)/shard_map/ppermute | solution.py:33
  10.4 5.9 %collective-permute-start.5 = (bf16[32,896]{1,0:T(8,128)(2,1)S(1)}, bf16[32,896]{1,0:T(8,128)(2,1)S(1)}, u32[]{:S(2)}, u32[]{:S(2)}) collective-permute-start(bf16[32,896]{1,0:T(8,128)(2,1)S(1)} %chip_sum.1.refs_0_.own_ref), channel_id=1, source_target_pairs={{0,2},{1,3},{2,0},{3,1},{4,6},{5,7},{6,4},{7,5},{8,10},{9,11},{10,... | collective-permute-start | bytes 172040 | tf_op jit(solution)/shard_map/ppermute | solution.py:26
  16.4 3.6 %collective-permute-start.6 = (bf16[64,896]{1,0:T(8,128)(2,1)S(1)}, bf16[64,896]{1,0:T(8,128)(2,1)S(1)}, u32[]{:S(2)}, u32[]{:S(2)}) collective-permute-start(bf16[64,896]{1,0:T(8,128)(2,1)S(1)} %get-tuple-element.56.refs_0_), channel_id=1, source_target_pairs={{0,1},{1,0},{2,3},{3,2},{4,5},{5,4},{6,7},{7,6},{8,9},{9,8},{10,11... | collective-permute-start | bytes 344072 | tf_op jit(solution)/shard_map/ppermute | solution.py:26
  16.5 6.9 %collective-permute-start.8 = (bf16[64,896]{1,0:T(8,128)(2,1)S(1)}, bf16[64,896]{1,0:T(8,128)(2,1)S(1)}, u32[]{:S(2)}, u32[]{:S(2)}) collective-permute-start(bf16[64,896]{1,0:T(8,128)(2,1)S(1)} %get-tuple-element.56.refs_0_), channel_id=1, source_target_pairs={{0,12},{4,8},{8,4},{12,0},{16,28},{20,24},{24,20},{28,16},{1,13},{... | collective-permute-start | bytes 344072 | tf_op jit(solution)/shard_map/ppermute | solution.py:26
  18.1 7.3 %collective-permute-start.9 = (bf16[64,896]{1,0:T(8,128)(2,1)S(1)}, bf16[64,896]{1,0:T(8,128)(2,1)S(1)}, u32[]{:S(2)}, u32[]{:S(2)}) collective-permute-start(bf16[64,896]{1,0:T(8,128)(2,1)S(1)} %get-tuple-element.56.refs_0_), channel_id=1, source_target_pairs={{0,4},{4,0},{8,12},{12,8},{16,20},{20,16},{24,28},{28,24},{1,5},{5... | collective-permute-start | bytes 344072 | tf_op jit(solution)/shard_map/ppermute | solution.py:26
  18.6 6.9 %collective-permute-start.10 = (bf16[64,896]{1,0:T(8,128)(2,1)S(1)}, bf16[64,896]{1,0:T(8,128)(2,1)S(1)}, u32[]{:S(2)}, u32[]{:S(2)}) collective-permute-start(bf16[64,896]{1,0:T(8,128)(2,1)S(1)} %get-tuple-element.56.refs_0_), channel_id=1, source_target_pairs={{0,8},{4,12},{8,0},{12,4},{16,24},{20,28},{24,16},{28,20},{1,9},{5... | collective-permute-start | bytes 344072 | tf_op jit(solution)/shard_map/ppermute | solution.py:26
  21.9 3.5 %collective-permute-start.7 = (bf16[64,768]{1,0:T(8,128)(2,1)S(1)}, bf16[64,768]{1,0:T(8,128)(2,1)S(1)}, u32[]{:S(2)}, u32[]{:S(2)}) collective-permute-start(bf16[64,768]{1,0:T(8,128)(2,1)S(1)} %get-tuple-element.60.refs_0_), channel_id=1, source_target_pairs={{0,1},{1,0},{2,3},{3,2},{4,5},{5,4},{6,7},{7,6},{8,9},{9,8},{10,11... | collective-permute-start | bytes 294920 | tf_op jit(solution)/shard_map/ppermute | solution.py:26
  23.5 3.6 %collective-permute-start.11 = (bf16[64,896]{1,0:T(8,128)(2,1)S(1)}, bf16[64,896]{1,0:T(8,128)(2,1)S(1)}, u32[]{:S(2)}, u32[]{:S(2)}) collective-permute-start(bf16[64,896]{1,0:T(8,128)(2,1)S(1)} %relay.3.refs_0_), channel_id=1, source_target_pairs={{0,1},{1,0},{2,3},{3,2},{4,5},{5,4},{6,7},{7,6},{8,9},{9,8},{10,11... | collective-permute-start | bytes 344072 | tf_op jit(solution)/shard_map/ppermute | solution.py:26
  25.5 1.6 %collective-permute-start.12 = (bf16[64,896]{1,0:T(8,128)(2,1)S(1)}, bf16[64,896]{1,0:T(8,128)(2,1)S(1)}, u32[]{:S(2)}, u32[]{:S(2)}) collective-permute-start(bf16[64,896]{1,0:T(8,128)(2,1)S(1)} %relay.4.refs_1_), channel_id=1, source_target_pairs={{0,1},{1,0},{2,3},{3,2},{4,5},{5,4},{6,7},{7,6},{8,9},{9,8},{10,11... | collective-permute-start | bytes 344072 | tf_op jit(solution)/shard_map/ppermute | solution.py:26
  25.6 1.5 %collective-permute-start.13 = (bf16[64,896]{1,0:T(8,128)(2,1)S(1)}, bf16[64,896]{1,0:T(8,128)(2,1)S(1)}, u32[]{:S(2)}, u32[]{:S(2)}) collective-permute-start(bf16[64,896]{1,0:T(8,128)(2,1)S(1)} %relay.5.refs_2_), channel_id=1, source_target_pairs={{0,1},{1,0},{2,3},{3,2},{4,5},{5,4},{6,7},{7,6},{8,9},{9,8},{10,11... | collective-permute-start | bytes 344072 | tf_op jit(solution)/shard_map/ppermute | solution.py:26
  28.6 1.4 %collective-permute-start.14 = (bf16[64,768]{1,0:T(8,128)(2,1)S(1)}, bf16[64,768]{1,0:T(8,128)(2,1)S(1)}, u32[]{:S(2)}, u32[]{:S(2)}) collective-permute-start(bf16[64,768]{1,0:T(8,128)(2,1)S(1)} %get-tuple-element.64), channel_id=1, source_target_pairs={{0,1},{1,0},{2,3},{3,2},{4,5},{5,4},{6,7},{7,6},{8,9},{9,8},{10,11... | collective-permute-start | bytes 294920 | tf_op jit(solution)/shard_map/ppermute | solution.py:26
  28.9 2.7 %collective-permute-start.16 = (bf16[64,768]{1,0:T(8,128)(2,1)S(1)}, bf16[64,768]{1,0:T(8,128)(2,1)S(1)}, u32[]{:S(2)}, u32[]{:S(2)}) collective-permute-start(bf16[64,768]{1,0:T(8,128)(2,1)S(1)} %get-tuple-element.65), channel_id=1, source_target_pairs={{0,1},{1,0},{2,3},{3,2},{4,5},{5,4},{6,7},{7,6},{8,9},{9,8},{10,11... | collective-permute-start | bytes 294920 | tf_op jit(solution)/shard_map/ppermute | solution.py:26
  29.1 3.1 %collective-permute-start.18 = (bf16[64,768]{1,0:T(8,128)(2,1)S(1)}, bf16[64,768]{1,0:T(8,128)(2,1)S(1)}, u32[]{:S(2)}, u32[]{:S(2)}) collective-permute-start(bf16[64,768]{1,0:T(8,128)(2,1)S(1)} %get-tuple-element.66), channel_id=1, source_target_pairs={{0,1},{1,0},{2,3},{3,2},{4,5},{5,4},{6,7},{7,6},{8,9},{9,8},{10,11... | collective-permute-start | bytes 294920 | tf_op jit(solution)/shard_map/ppermute | solution.py:26
  29.9 6.3 %collective-permute-start.15 = (bf16[64,768]{1,0:T(8,128)(2,1)S(1)}, bf16[64,768]{1,0:T(8,128)(2,1)S(1)}, u32[]{:S(2)}, u32[]{:S(2)}) collective-permute-start(bf16[64,768]{1,0:T(8,128)(2,1)S(1)} %chip_sums.5), channel_id=1, source_target_pairs={{0,12},{4,8},{8,4},{12,0},{16,28},{20,24},{24,20},{28,16},{1,13},{... | collective-permute-start | bytes 294920 | tf_op jit(solution)/shard_map/ppermute | solution.py:26
  31.6 6.4 %collective-permute-start.17 = (bf16[64,768]{1,0:T(8,128)(2,1)S(1)}, bf16[64,768]{1,0:T(8,128)(2,1)S(1)}, u32[]{:S(2)}, u32[]{:S(2)}) collective-permute-start(bf16[64,768]{1,0:T(8,128)(2,1)S(1)} %chip_sums.6), channel_id=1, source_target_pairs={{0,4},{4,0},{8,12},{12,8},{16,20},{20,16},{24,28},{28,24},{1,5},{5... | collective-permute-start | bytes 294920 | tf_op jit(solution)/shard_map/ppermute | solution.py:26
  32.2 5.8 %collective-permute-start.19 = (bf16[64,768]{1,0:T(8,128)(2,1)S(1)}, bf16[64,768]{1,0:T(8,128)(2,1)S(1)}, u32[]{:S(2)}, u32[]{:S(2)}) collective-permute-start(bf16[64,768]{1,0:T(8,128)(2,1)S(1)} %chip_sums.7), channel_id=1, source_target_pairs={{0,8},{4,12},{8,0},{12,4},{16,24},{20,28},{24,16},{28,20},{1,9},{5... | collective-permute-start | bytes 294920 | tf_op jit(solution)/shard_map/ppermute | solution.py:26
  38.1 6.5 %collective-permute-start.20 = (bf16[32,768]{1,0:T(8,128)(2,1)S(1)}, bf16[32,768]{1,0:T(8,128)(2,1)S(1)}, u32[]{:S(2)}, u32[]{:S(2)}) collective-permute-start(bf16[32,768]{1,0:T(8,128)(2,1)S(1)} %get-tuple-element.67), channel_id=1, source_target_pairs={{0,16},{4,20},{8,24},{12,28},{16,0},{20,4},{24,8},{28,12},{1,17},{... | collective-permute-start | bytes 147464 | tf_op jit(solution)/shard_map/ppermute | solution.py:26
  40.3 6.4 %collective-permute-start.21 = (bf16[32,768]{1,0:T(8,128)(2,1)S(1)}, bf16[32,768]{1,0:T(8,128)(2,1)S(1)}, u32[]{:S(2)}, u32[]{:S(2)}) collective-permute-start(bf16[32,768]{1,0:T(8,128)(2,1)S(1)} %get-tuple-element.67), channel_id=1, source_target_pairs={{0,18},{1,19},{2,16},{3,17},{4,22},{5,23},{6,20},{7,21},{8,26},{9,... | collective-permute-start | bytes 147464 | tf_op jit(solution)/shard_map/ppermute | solution.py:33
  42.0 4.7 %collective-permute-start.22 = (bf16[32,768]{1,0:T(8,128)(2,1)S(1)}, bf16[32,768]{1,0:T(8,128)(2,1)S(1)}, u32[]{:S(2)}, u32[]{:S(2)}) collective-permute-start(bf16[32,768]{1,0:T(8,128)(2,1)S(1)} %get-tuple-element.68), channel_id=1, source_target_pairs={{0,2},{1,3},{2,0},{3,1},{4,6},{5,7},{6,4},{7,5},{8,10},{9,11},{10,... | collective-permute-start | bytes 147464 | tf_op jit(solution)/shard_map/ppermute | solution.py:26
  46.8 1.2 %collective-permute-start.23 = (f32[32,128]{1,0:T(8,128)S(1)}, f32[32,128]{1,0:T(8,128)S(1)}, u32[]{:S(2)}, u32[]{:S(2)}) collective-permute-start(f32[32,128]{1,0:T(8,128)S(1)} %get-tuple-element.72.a_ref), channel_id=1, source_target_pairs={{0,1},{1,0},{2,3},{3,2},{4,5},{5,4},{6,7},{7,6},{8,9},{9,8},{10,11... | collective-permute-start | bytes 49160 | tf_op jit(solution)/shard_map/ppermute | solution.py:26
  (3 other events, 28.5 us)

commit v7 on v6

--- a/solution.py
+++ b/solution.py
@@ -378,8 +378,12 @@
             out_ref[b, :, k * quarter : (k + 1) * quarter] = total[b * tall : (b + 1) * tall]
 
 
-def chips_body(b, keep_ref, got_ref, out_ref):
-    out_ref[...] = (keep_ref[b] + got_ref[...].astype(F32)).astype(out_ref.dtype)
+def chips_body(b, keep_ref, got_ref, far_ref, own_ref):
+    total = keep_ref[b] + got_ref[...].astype(F32)
+    groups, rows, width = far_ref.shape
+    total = total.reshape(groups, 2, rows, width)
+    far_ref[...] = total[:, 1].astype(far_ref.dtype)
+    own_ref[...] = total[:, 0].astype(own_ref.dtype)
 
 
 def pass_body(terms, *refs):
@@ -392,18 +396,15 @@
         r[...] = total[i * tall : (i + 1) * tall].astype(r.dtype)
 
 
-def pair_body(terms, *refs):
+def sum_body(terms, *refs):
     total = refs[0][...]
     for r in refs[1:terms]:
         total = total + r[...].astype(F32)
-    own_ref, x_ref, y_ref = refs[terms:]
-    rows = own_ref.shape[0]
-    own_ref[...] = total[:rows]
-    x_ref[...] = total[:rows].astype(BF16)
-    y_ref[...] = total[rows:].astype(BF16)
-
-
-def combine_body(y_ref, xy_ref, x_ref, own_ref, residual_ref, combined_ref, square_ref):
+    for r in refs[terms:]:
+        r[...] = total.reshape(r.shape).astype(r.dtype)
+
+
+def combine_body(own_ref, x_ref, y_ref, xy_ref, residual_ref, combined_ref, square_ref):
     quarter = combined_ref.shape[1]
     total = (own_ref[...] + x_ref[...].astype(F32)) + (y_ref[...].astype(F32) + xy_ref[...].astype(F32))
     total = residual_ref[...].astype(F32) + total
@@ -416,7 +417,7 @@
     out_ref[...] = (combined_ref[...] * lax.rsqrt(mean + EPSILON) * gain_ref[...].astype(F32)).astype(BF16)
 
 
-def run_experts(own, other, gate_weight, up_weight, down_weight, hosted, copies, first):
+def run_experts(own, other, gate_weight, up_weight, down_weight, hosted, copies, rows, first):
     blocks = len(own)
     tall, total = own[0].shape
     units, width = gate_weight.shape
@@ -471,7 +472,7 @@
     sums = [
         call(
             functools.partial(chips_body, b),
-            shape((tall, width // 2), F32 if first else BF16),
+            [shape((tall // (2 * rows), rows, width // 2), F32 if first else BF16)] * 2,
             (keep, got[b]),
             vmem=48 << 20,
             name="chip_sums",
@@ -570,7 +571,7 @@
 
     bit, stages = 1, []
     while bit < far:
-        stages.append([bit] if 2 * bit >= far else [3 * bit, bit, 2 * bit])
+        stages.append([bit] if 2 * bit >= far else [bit, 2 * bit, 3 * bit])
         bit *= 4
     blocks = [block]
     for stage in stages:
@@ -581,32 +582,40 @@
         if pieces:
             group = [after_all(b, [got if i else send]) for i, b in enumerate(group)]
         others = [swap(b, "tensor", 1) for b in group]
-        sums, send, got = run_experts(group, others, *weights, hosted, copies, not pieces)
+        sums, send, got = run_experts(group, others, *weights, hosted, copies, rows, not pieces)
         pieces += sums
-    terms = [pieces[0]] + [swap(p, "expert", b) for p, b in zip(pieces[1:], stages[-1])]
-    for stage in stages[-2::-1]:
-        tall = terms[0].shape[0] // (len(stage) + 1)
-        pieces = call(
-            functools.partial(pass_body, len(terms)),
-            [shape((tall, half), F32)] + [shape((tall, half), BF16)] * len(stage),
+    def scatter(pieces):
+        terms = [pieces[0]] + [swap(p, "expert", b) for p, b in zip(pieces[1:], stages[-1])]
+        for stage in stages[-2::-1]:
+            part = (terms[0].shape[0] // (len(stage) + 1), rows, half)
+            pieces = call(
+                functools.partial(pass_body, len(terms)),
+                [shape(part, F32)] + [shape(part, BF16)] * len(stage),
+                terms,
+                vmem=48 << 20,
+                name="pass_on",
+            )
+            terms = [pieces[0]] + [swap(p, "expert", b) for p, b in zip(pieces[1:], stage)]
+        return terms
+
+    def sum_of(terms, kinds):
+        return call(
+            functools.partial(sum_body, len(terms)),
+            [shape((rows, half), k) for k in kinds],
             terms,
-            vmem=48 << 20,
-            name="pass_on",
-            cost=(tall * width, 1 << 20),
+            name="sums",
+            cost=(rows * width, 1 << 18),
         )
-        terms = [pieces[0]] + [swap(p, "expert", b) for p, b in zip(pieces[1:], stage)]
-    own, x_part, far_part = call(
-        functools.partial(pair_body, len(terms)),
-        [shape((rows, half), F32), shape((rows, half), BF16), shape((rows, half), BF16)],
-        terms,
-        name="z_sums",
-        cost=(rows * width, 1 << 18),
-    )
-    far_y, far_xy, near_x = swap(far_part, "expert", far), swap_both(far_part, far, 2), swap(x_part, "tensor", 2)
+
+    far_terms, own_terms = scatter([p[0] for p in pieces]), scatter([p[1] for p in pieces])
+    (far_part,) = sum_of(far_terms, (BF16,))
+    far_y, far_xy = swap(far_part, "expert", far), swap_both(far_part, far, 2)
+    own, x_part = sum_of(own_terms, (F32, BF16))
+    near_x = swap(x_part, "tensor", 2)
     combined, squares = call(
         combine_body,
         [shape((rows, quarter), F32), shape((rows, LANES), F32)],
-        (far_y, far_xy, near_x, own, residual),
+        (own, near_x, far_y, far_xy, residual),
         name="combine",
         cost=(rows * width, 1 << 18),
     )

time: 48.8 us -> 48.4 us (level)
  waiting for transfers between devices: 15.7 us -> 12.2 us
  starting transfers between devices: 20 us -> 23.1 us
    ppermute x22 -> x25, waiting for transfers between devices: 11.2 us -> 7.83 us  [swap(): return lax.ppermute(block, axis, [(i, i ^ bits) for i in range(count)])]
    ppermute x22 -> x25, starting transfers between devices: 17 us -> 20.1 us  [swap(): return lax.ppermute(block, axis, [(i, i ^ bits) for i in range(count)])]
    pallas_call x16 -> x17, Pallas kernels: 7.67 us -> 7.68 us  [call(): pl.pallas_call(body, out_shape=listed, in_specs=in_specs, out_specs=out_s...]
  transfers between devices with their start and end apart: 24 -> 27, of which waited for: 9 -> 12; matrix products, arithmetic and copies ran while one was open for 0% -> 0% of each run, Pallas kernels for 19% -> 19%
where the time goes in v7:
time: 48.4 us; the launch traced here: 48.3 us
  starting transfers between devices  23.1 us (48%)
  Pallas kernels  12.7 us (26%)
  waiting for transfers between devices  12.2 us (25%)
    ppermute x25, starting transfers between devices, swap(): return lax.ppermute(block, axis, [(i, i ^ bits) for i in range(count)])  20.1 us
    ppermute x25, waiting for transfers between devices, swap(): return lax.ppermute(block, axis, [(i, i ^ bits) for i in range(count)])  7.83 us
    pallas_call x17, Pallas kernels, call(): pl.pallas_call(body, out_shape=listed, in_specs=in_specs, out_specs=out_s...  7.68 us
    ppermute x2, waiting for transfers between devices, swap_both(): lax.ppermute(block, ('expert', 'tensor'), [(i, i ^ bits) for i in range(c...  4.34 us
    pallas_call x2, Pallas kernels, run_experts(): pl.pallas_call(functools.partial(expert_body, copies, hosted, blocks), gr...  3.28 us
    ppermute x2, starting transfers between devices, swap_both(): lax.ppermute(block, ('expert', 'tensor'), [(i, i ^ bits) for i in range(c...  3.02 us
    pallas_call x1, Pallas kernels, run_experts(): pl.pallas_call(functools.partial(half_body, blocks), grid=grid, out_shape...  0.98 us
  transfers between devices with their start and end apart: 27, of which 12 were waited for; matrix products, arithmetic and copies ran while one was open for 0% of the time, Pallas kernels for 19%

profile of v7, /device:TPU:0, one launch (start us, length us, event | category | flops | bytes accessed | tf_op | source)
XLA Modules:
  0.0 48.3 jit_solution(3184858874091617798)
XLA Ops:
  0.5 2.0 %project.1 = (bf16[96,128]{1,0:T(8,128)(2,1)S(1)}, bf16[32,128]{1,0:T(8,128)(2,1)S(1)}, bf16[32,1536]{1,0:T(8,128)(2,1)S(1)}, f32[32,128]{1,0:T(8,128)S(1)}, f32...) custom-call(s32[1,3]{1,0:T(1,128)} %length_hbm.1, ...), custom_call_target="tpu_custom_call" | custom-call | flops 50331648 | bytes 2097152 | tf_op jit(solution)/shard_map/project/pallas_call | solution.py:58
  2.6 1.2 %attention.1 = (bf16[32,768]{1,0:T(8,128)(2,1)S(1)}, f32[32,768]{1,0:T(8,128)S(1)}) custom-call(bf16[96,128]{1,0:T(8,128)(2,1)S(1)} %get-tuple-element.46.q_ref, bf16[32,128]{1,0:T(8,128)(2,1)S(1)} %get-tuple-element.47.own_ref, bf16[32,1536]{1,0:T(8,128)(2,1)S(1)} %get-tuple-element.48.normed_ref, bf16[1536,128]{1,0:T(8,128)(2,1)S(1)} %collective-permute-done.other_ref, ...), custom_call_target="tpu_custom_call" | custom-call | flops 37748736 | bytes 1048576 | tf_op jit(solution)/shard_map/attention/pallas_call | solution.py:58
  5.2 4.0 %collective-permute-start.3 = (bf16[32,896]{1,0:T(8,128)(2,1)S(1)}, bf16[32,896]{1,0:T(8,128)(2,1)S(1)}, u32[]{:S(2)}, u32[]{:S(2)}) collective-permute-start(bf16[32,896]{1,0:T(8,128)(2,1)S(1)} %chip_sum.1.refs_0_.own_ref), channel_id=1, source_target_pairs={{0,16},{4,20},{8,24},{12,28},{16,0},{20,4},{24,8},{28,12},{1,17},{... | collective-permute-start | bytes 172040 | tf_op jit(solution)/shard_map/ppermute | solution.py:26
  9.2 1.3 %collective-permute-start.4 = (bf16[32,896]{1,0:T(8,128)(2,1)S(1)}, bf16[32,896]{1,0:T(8,128)(2,1)S(1)}, u32[]{:S(2)}, u32[]{:S(2)}) collective-permute-start(bf16[32,896]{1,0:T(8,128)(2,1)S(1)} %chip_sum.1.refs_0_.own_ref), channel_id=1, source_target_pairs={{0,18},{1,19},{2,16},{3,17},{4,22},{5,23},{6,20},{7,21},{8,26},{9,... | collective-permute-start | bytes 172040 | tf_op jit(solution)/shard_map/ppermute | solution.py:33
  10.7 3.1 %load_experts.1 = (bf16[768,1536]{1,0:T(8,128)(2,1)S(1)}, bf16[768,1536]{1,0:T(8,128)(2,1)S(1)}, bf16[768,1536]{1,0:T(8,128)(2,1)S(1)}) custom-call(bf16[32,896]{1,0:T(8,128)(2,1)S(1)} %chip_sum.1.refs_0_.own_ref, bf16[768,1536]{1,0:T(8,128)(2,1)} %bitcast.12, bf16[768,1536]{1,0:T(8,128)(2,1)} %bitcast.13, bf16[768,1536]{1,0:T(8,128)(2,1)} %bitcast.14), custom_call_target="tpu_custom_call" | custom-call | bytes 8388608 | tf_op jit(solution)/shard_map/load_experts/pallas_call | solution.py:58
  13.8 2.4 %collective-permute-done.4.xy_ref = bf16[32,896]{1,0:T(8,128)(2,1)S(1)} collective-permute-done((bf16[32,896]{1,0:T(8,128)(2,1)S(1)}, bf16[32,896]{1,0:T(8,128)(2,1)S(1)}, u32[]{:S(2)}, u32[]{:S(2)}) %collective-permute-start.4) | collective-permute-done | bytes 57376 | tf_op jit(solution)/shard_map/ppermute | solution.py:33
  16.5 1.6 %collective-permute-start.8 = (bf16[64,896]{1,0:T(8,128)(2,1)S(1)}, bf16[64,896]{1,0:T(8,128)(2,1)S(1)}, u32[]{:S(2)}, u32[]{:S(2)}) collective-permute-start(bf16[64,896]{1,0:T(8,128)(2,1)S(1)} %get-tuple-element.63.refs_0_), channel_id=1, source_target_pairs={{0,4},{4,0},{8,12},{12,8},{16,20},{20,16},{24,28},{28,24},{1,5},{5... | collective-permute-start | bytes 344072 | tf_op jit(solution)/shard_map/ppermute | solution.py:26
  18.6 1.4 %collective-permute-start.9 = (bf16[64,896]{1,0:T(8,128)(2,1)S(1)}, bf16[64,896]{1,0:T(8,128)(2,1)S(1)}, u32[]{:S(2)}, u32[]{:S(2)}) collective-permute-start(bf16[64,896]{1,0:T(8,128)(2,1)S(1)} %get-tuple-element.63.refs_0_), channel_id=1, source_target_pairs={{0,8},{4,12},{8,0},{12,4},{16,24},{20,28},{24,16},{28,20},{1,9},{5... | collective-permute-start | bytes 344072 | tf_op jit(solution)/shard_map/ppermute | solution.py:26
  20.1 1.9 %experts.2 = (bf16[1,64,768]{2,1,0:T(8,128)(2,1)S(1)}, bf16[64,768]{1,0:T(8,128)(2,1)S(1)}) custom-call(bf16[64,896]{1,0:T(8,128)(2,1)S(1)} %get-tuple-element.63.refs_0_, bf16[64,896]{1,0:T(8,128)(2,1)S(1)} %collective-permute-done.6.refs_1_, bf16[768,1536]{1,0:T(8,128)(2,1)S(1)} %get-tuple-element.62.loaded_ref.refs_2_.refs_3_.refs_6_, ...), custom_call_target="tpu_custom_call" | custom-call | flops 1 | bytes 1 | tf_op jit(solution)/shard_map/experts/pallas_call | solution.py:451
  22.0 2.0 %collective-permute-done.8.block_ref = bf16[64,896]{1,0:T(8,128)(2,1)S(1)} collective-permute-done((bf16[64,896]{1,0:T(8,128)(2,1)S(1)}, bf16[64,896]{1,0:T(8,128)(2,1)S(1)}, u32[]{:S(2)}, u32[]{:S(2)}) %collective-permute-start.8) | collective-permute-done | bytes 114720 | tf_op jit(solution)/shard_map/ppermute | solution.py:26
  24.1 0.9 %collective-permute-done.10.block_ref = bf16[64,896]{1,0:T(8,128)(2,1)S(1)} collective-permute-done((bf16[64,896]{1,0:T(8,128)(2,1)S(1)}, bf16[64,896]{1,0:T(8,128)(2,1)S(1)}, u32[]{:S(2)}, u32[]{:S(2)}) %collective-permute-start.10) | collective-permute-done | bytes 114720 | tf_op jit(solution)/shard_map/ppermute | solution.py:26
  25.9 1.0 %experts_half_depth.1 = (f32[3,64,768]{2,1,0:T(8,128)S(1)}, f32[3,64,768]{2,1,0:T(8,128)S(1)}) custom-call(bf16[64,896]{1,0:T(8,128)(2,1)S(1)} %relay.3.refs_0_, bf16[64,896]{1,0:T(8,128)(2,1)S(1)} %relay.4.refs_1_, bf16[64,896]{1,0:T(8,128)(2,1)S(1)} %relay.5.refs_2_, bf16[768,1536]{1,0:T(8,128)(2,1)S(1)} %get-tuple-element.62.loaded_ref.refs_2_.refs_3_.refs_6_, ...), custom_call_target="tpu_custom_call" | custom-call | flops 1 | bytes 1 | tf_op jit(solution)/shard_map/experts_half_depth/pallas_call | solution.py:441
  27.2 1.4 %experts.3 = (bf16[3,64,768]{2,1,0:T(8,128)(2,1)S(1)}, bf16[64,768]{1,0:T(8,128)(2,1)S(1)}, bf16[64,768]{1,0:T(8,128)(2,1)S(1)}, bf16[64,768]{1,0:T(8,128)(2,1)S(1)}) custom-call(bf16[64,896]{1,0:T(8,128)(2,1)S(1)} %relay.3.refs_0_, bf16[64,896]{1,0:T(8,128)(2,1)S(1)} %relay.4.refs_1_, bf16[64,896]{1,0:T(8,128)(2,1)S(1)} %relay.5.refs_2_, ...), custom_call_target="tpu_custom_call" | custom-call | flops 1 | bytes 1 | tf_op jit(solution)/shard_map/experts/pallas_call | solution.py:451
  30.0 1.6 %collective-permute-start.23 = (bf16[1,32,768]{2,1,0:T(8,128)(2,1)S(1)}, bf16[1,32,768]{2,1,0:T(8,128)(2,1)S(1)}, u32[]{:S(2)}, u32[]{:S(2)}) collective-permute-start(bf16[1,32,768]{2,1,0:T(8,128)(2,1)S(1)} %get-tuple-element.83), channel_id=1, source_target_pairs={{0,12},{4,8},{8,4},{12,0},{16,28},{20,24},{24,20},{28,16},{1,13},{... | collective-permute-start | bytes 147464 | tf_op jit(solution)/shard_map/ppermute | solution.py:26
  31.7 1.5 %collective-permute-start.22 = (bf16[1,32,768]{2,1,0:T(8,128)(2,1)S(1)}, bf16[1,32,768]{2,1,0:T(8,128)(2,1)S(1)}, u32[]{:S(2)}, u32[]{:S(2)}) collective-permute-start(bf16[1,32,768]{2,1,0:T(8,128)(2,1)S(1)} %get-tuple-element.82), channel_id=1, source_target_pairs={{0,8},{4,12},{8,0},{12,4},{16,24},{20,28},{24,16},{28,20},{1,9},{5... | collective-permute-start | bytes 147464 | tf_op jit(solution)/shard_map/ppermute | solution.py:26
  33.7 1.6 %collective-permute-start.19 = (bf16[1,32,768]{2,1,0:T(8,128)(2,1)S(1)}, bf16[1,32,768]{2,1,0:T(8,128)(2,1)S(1)}, u32[]{:S(2)}, u32[]{:S(2)}) collective-permute-start(bf16[1,32,768]{2,1,0:T(8,128)(2,1)S(1)} %get-tuple-element.77), channel_id=1, source_target_pairs={{0,12},{4,8},{8,4},{12,0},{16,28},{20,24},{24,20},{28,16},{1,13},{... | collective-permute-start | bytes 147464 | tf_op jit(solution)/shard_map/ppermute | solution.py:26
  35.3 1.4 %collective-permute-start.17 = (bf16[1,32,768]{2,1,0:T(8,128)(2,1)S(1)}, bf16[1,32,768]{2,1,0:T(8,128)(2,1)S(1)}, u32[]{:S(2)}, u32[]{:S(2)}) collective-permute-start(bf16[1,32,768]{2,1,0:T(8,128)(2,1)S(1)} %get-tuple-element.75), channel_id=1, source_target_pairs={{0,8},{4,12},{8,0},{12,4},{16,24},{20,28},{24,16},{28,20},{1,9},{5... | collective-permute-start | bytes 147464 | tf_op jit(solution)/shard_map/ppermute | solution.py:26
  37.7 2.2 %collective-permute-start.24 = (bf16[32,768]{1,0:T(8,128)(2,1)S(1)}, bf16[32,768]{1,0:T(8,128)(2,1)S(1)}, u32[]{:S(2)}, u32[]{:S(2)}) collective-permute-start(bf16[32,768]{1,0:T(8,128)(2,1)S(1)} %sums.3), channel_id=1, source_target_pairs={{0,16},{4,20},{8,24},{12,28},{16,0},{20,4},{24,8},{28,12},{1,17},{... | collective-permute-start | bytes 147464 | tf_op jit(solution)/shard_map/ppermute | solution.py:26
  39.8 1.8 %collective-permute-start.25 = (bf16[32,768]{1,0:T(8,128)(2,1)S(1)}, bf16[32,768]{1,0:T(8,128)(2,1)S(1)}, u32[]{:S(2)}, u32[]{:S(2)}) collective-permute-start(bf16[32,768]{1,0:T(8,128)(2,1)S(1)} %sums.3), channel_id=1, source_target_pairs={{0,18},{1,19},{2,16},{3,17},{4,22},{5,23},{6,20},{7,21},{8,26},{9,... | collective-permute-start | bytes 147464 | tf_op jit(solution)/shard_map/ppermute | solution.py:33
  41.6 0.8 %collective-permute-start.20 = (bf16[32,768]{1,0:T(8,128)(2,1)S(1)}, bf16[32,768]{1,0:T(8,128)(2,1)S(1)}, u32[]{:S(2)}, u32[]{:S(2)}) collective-permute-start(bf16[32,768]{1,0:T(8,128)(2,1)S(1)} %get-tuple-element.79), channel_id=1, source_target_pairs={{0,2},{1,3},{2,0},{3,1},{4,6},{5,7},{6,4},{7,5},{8,10},{9,11},{10,... | collective-permute-start | bytes 147464 | tf_op jit(solution)/shard_map/ppermute | solution.py:26
  42.4 1.5 %collective-permute-done.24.y_ref = bf16[32,768]{1,0:T(8,128)(2,1)S(1)} collective-permute-done((bf16[32,768]{1,0:T(8,128)(2,1)S(1)}, bf16[32,768]{1,0:T(8,128)(2,1)S(1)}, u32[]{:S(2)}, u32[]{:S(2)}) %collective-permute-start.24) | collective-permute-done | bytes 49184 | tf_op jit(solution)/shard_map/ppermute | solution.py:26
  43.9 1.9 %collective-permute-done.25.xy_ref = bf16[32,768]{1,0:T(8,128)(2,1)S(1)} collective-permute-done((bf16[32,768]{1,0:T(8,128)(2,1)S(1)}, bf16[32,768]{1,0:T(8,128)(2,1)S(1)}, u32[]{:S(2)}, u32[]{:S(2)}) %collective-permute-start.25) | collective-permute-done | bytes 49184 | tf_op jit(solution)/shard_map/ppermute | solution.py:33
  46.4 1.2 %collective-permute-done.26.b_ref = f32[32,128]{1,0:T(8,128)S(1)} collective-permute-done((f32[32,128]{1,0:T(8,128)S(1)}, f32[32,128]{1,0:T(8,128)S(1)}, u32[]{:S(2)}, u32[]{:S(2)}) %collective-permute-start.26) | collective-permute-done | bytes 16416 | tf_op jit(solution)/shard_map/ppermute | solution.py:26
  47.6 0.7 %finish.1 = bf16[32,384]{1,0:T(8,128)(2,1)} custom-call(f32[32,384]{1,0:T(8,128)S(1)} %get-tuple-element.85.combined_ref, bf16[1,384]{1,0:T(2,128)(2,1)S(1)} %broadcast_in_dim.11.gain_ref, f32[32,128]{1,0:T(8,128)S(1)} %get-tuple-element.86.a_ref, f32[32,128]{1,0:T(8,128)S(1)} %collective-permute-done.26.b_ref), custom_call_target="tpu_custom_call" | custom-call | flops 49152 | bytes 262144 | tf_op jit(solution)/shard_map/finish/pallas_call | solution.py:58
  (60 shorter events, 7.8 us)
Async XLA Ops:
  0.0 2.5 %collective-permute-start = (bf16[1536,128]{1,0:T(8,128)(2,1)}, bf16[1536,128]{1,0:T(8,128)(2,1)S(1)}, u32[]{:S(2)}, u32[]{:S(2)}) collective-permute-start(bf16[1536,128]{1,0:T(8,128)(2,1)} %bitcast.15), channel_id=1, source_target_pairs={{0,1},{1,0},{2,3},{3,2},{4,5},{5,4},{6,7},{7,6},{8,9},{9,8},{10,11... | collective-permute-start | bytes 1179656 | tf_op jit(solution)/shard_map/ppermute | solution.py:26
  0.5 2.1 %collective-permute-start.1 = (bf16[768,128]{1,0:T(8,128)(2,1)}, bf16[768,128]{1,0:T(8,128)(2,1)S(1)}, u32[]{:S(2)}, u32[]{:S(2)}) collective-permute-start(bf16[768,128]{1,0:T(8,128)(2,1)} %bitcast.16), channel_id=1, source_target_pairs={{0,1},{1,0},{2,3},{3,2},{4,5},{5,4},{6,7},{7,6},{8,9},{9,8},{10,11... | collective-permute-start | bytes 589832 | tf_op jit(solution)/shard_map/ppermute | solution.py:26
  5.2 8.7 %collective-permute-start.3 = (bf16[32,896]{1,0:T(8,128)(2,1)S(1)}, bf16[32,896]{1,0:T(8,128)(2,1)S(1)}, u32[]{:S(2)}, u32[]{:S(2)}) collective-permute-start(bf16[32,896]{1,0:T(8,128)(2,1)S(1)} %chip_sum.1.refs_0_.own_ref), channel_id=1, source_target_pairs={{0,16},{4,20},{8,24},{12,28},{16,0},{20,4},{24,8},{28,12},{1,17},{... | collective-permute-start | bytes 172040 | tf_op jit(solution)/shard_map/ppermute | solution.py:26
  9.2 7.1 %collective-permute-start.4 = (bf16[32,896]{1,0:T(8,128)(2,1)S(1)}, bf16[32,896]{1,0:T(8,128)(2,1)S(1)}, u32[]{:S(2)}, u32[]{:S(2)}) collective-permute-start(bf16[32,896]{1,0:T(8,128)(2,1)S(1)} %chip_sum.1.refs_0_.own_ref), channel_id=1, source_target_pairs={{0,18},{1,19},{2,16},{3,17},{4,22},{5,23},{6,20},{7,21},{8,26},{9,... | collective-permute-start | bytes 172040 | tf_op jit(solution)/shard_map/ppermute | solution.py:33
  10.4 5.9 %collective-permute-start.5 = (bf16[32,896]{1,0:T(8,128)(2,1)S(1)}, bf16[32,896]{1,0:T(8,128)(2,1)S(1)}, u32[]{:S(2)}, u32[]{:S(2)}) collective-permute-start(bf16[32,896]{1,0:T(8,128)(2,1)S(1)} %chip_sum.1.refs_0_.own_ref), channel_id=1, source_target_pairs={{0,2},{1,3},{2,0},{3,1},{4,6},{5,7},{6,4},{7,5},{8,10},{9,11},{10,... | collective-permute-start | bytes 172040 | tf_op jit(solution)/shard_map/ppermute | solution.py:26
  16.4 3.6 %collective-permute-start.6 = (bf16[64,896]{1,0:T(8,128)(2,1)S(1)}, bf16[64,896]{1,0:T(8,128)(2,1)S(1)}, u32[]{:S(2)}, u32[]{:S(2)}) collective-permute-start(bf16[64,896]{1,0:T(8,128)(2,1)S(1)} %get-tuple-element.63.refs_0_), channel_id=1, source_target_pairs={{0,1},{1,0},{2,3},{3,2},{4,5},{5,4},{6,7},{7,6},{8,9},{9,8},{10,11... | collective-permute-start | bytes 344072 | tf_op jit(solution)/shard_map/ppermute | solution.py:26
  16.5 7.5 %collective-permute-start.8 = (bf16[64,896]{1,0:T(8,128)(2,1)S(1)}, bf16[64,896]{1,0:T(8,128)(2,1)S(1)}, u32[]{:S(2)}, u32[]{:S(2)}) collective-permute-start(bf16[64,896]{1,0:T(8,128)(2,1)S(1)} %get-tuple-element.63.refs_0_), channel_id=1, source_target_pairs={{0,4},{4,0},{8,12},{12,8},{16,20},{20,16},{24,28},{28,24},{1,5},{5... | collective-permute-start | bytes 344072 | tf_op jit(solution)/shard_map/ppermute | solution.py:26
  18.1 6.9 %collective-permute-start.10 = (bf16[64,896]{1,0:T(8,128)(2,1)S(1)}, bf16[64,896]{1,0:T(8,128)(2,1)S(1)}, u32[]{:S(2)}, u32[]{:S(2)}) collective-permute-start(bf16[64,896]{1,0:T(8,128)(2,1)S(1)} %get-tuple-element.63.refs_0_), channel_id=1, source_target_pairs={{0,12},{4,8},{8,4},{12,0},{16,28},{20,24},{24,20},{28,16},{1,13},{... | collective-permute-start | bytes 344072 | tf_op jit(solution)/shard_map/ppermute | solution.py:26
  18.6 7.1 %collective-permute-start.9 = (bf16[64,896]{1,0:T(8,128)(2,1)S(1)}, bf16[64,896]{1,0:T(8,128)(2,1)S(1)}, u32[]{:S(2)}, u32[]{:S(2)}) collective-permute-start(bf16[64,896]{1,0:T(8,128)(2,1)S(1)} %get-tuple-element.63.refs_0_), channel_id=1, source_target_pairs={{0,8},{4,12},{8,0},{12,4},{16,24},{20,28},{24,16},{28,20},{1,9},{5... | collective-permute-start | bytes 344072 | tf_op jit(solution)/shard_map/ppermute | solution.py:26
  21.9 3.1 %collective-permute-start.7 = (bf16[64,768]{1,0:T(8,128)(2,1)S(1)}, bf16[64,768]{1,0:T(8,128)(2,1)S(1)}, u32[]{:S(2)}, u32[]{:S(2)}) collective-permute-start(bf16[64,768]{1,0:T(8,128)(2,1)S(1)} %get-tuple-element.67.refs_0_), channel_id=1, source_target_pairs={{0,1},{1,0},{2,3},{3,2},{4,5},{5,4},{6,7},{7,6},{8,9},{9,8},{10,11... | collective-permute-start | bytes 294920 | tf_op jit(solution)/shard_map/ppermute | solution.py:26
  24.0 2.8 %collective-permute-start.11 = (bf16[64,896]{1,0:T(8,128)(2,1)S(1)}, bf16[64,896]{1,0:T(8,128)(2,1)S(1)}, u32[]{:S(2)}, u32[]{:S(2)}) collective-permute-start(bf16[64,896]{1,0:T(8,128)(2,1)S(1)} %relay.3.refs_0_), channel_id=1, source_target_pairs={{0,1},{1,0},{2,3},{3,2},{4,5},{5,4},{6,7},{7,6},{8,9},{9,8},{10,11... | collective-permute-start | bytes 344072 | tf_op jit(solution)/shard_map/ppermute | solution.py:26
  25.1 1.8 %collective-permute-start.13 = (bf16[64,896]{1,0:T(8,128)(2,1)S(1)}, bf16[64,896]{1,0:T(8,128)(2,1)S(1)}, u32[]{:S(2)}, u32[]{:S(2)}) collective-permute-start(bf16[64,896]{1,0:T(8,128)(2,1)S(1)} %relay.5.refs_2_), channel_id=1, source_target_pairs={{0,1},{1,0},{2,3},{3,2},{4,5},{5,4},{6,7},{7,6},{8,9},{9,8},{10,11... | collective-permute-start | bytes 344072 | tf_op jit(solution)/shard_map/ppermute | solution.py:26
  25.8 1.4 %collective-permute-start.12 = (bf16[64,896]{1,0:T(8,128)(2,1)S(1)}, bf16[64,896]{1,0:T(8,128)(2,1)S(1)}, u32[]{:S(2)}, u32[]{:S(2)}) collective-permute-start(bf16[64,896]{1,0:T(8,128)(2,1)S(1)} %relay.4.refs_1_), channel_id=1, source_target_pairs={{0,1},{1,0},{2,3},{3,2},{4,5},{5,4},{6,7},{7,6},{8,9},{9,8},{10,11... | collective-permute-start | bytes 344072 | tf_op jit(solution)/shard_map/ppermute | solution.py:26
  28.9 2.8 %collective-permute-start.16 = (bf16[64,768]{1,0:T(8,128)(2,1)S(1)}, bf16[64,768]{1,0:T(8,128)(2,1)S(1)}, u32[]{:S(2)}, u32[]{:S(2)}) collective-permute-start(bf16[64,768]{1,0:T(8,128)(2,1)S(1)} %get-tuple-element.74), channel_id=1, source_target_pairs={{0,1},{1,0},{2,3},{3,2},{4,5},{5,4},{6,7},{7,6},{8,9},{9,8},{10,11... | collective-permute-start | bytes 294920 | tf_op jit(solution)/shard_map/ppermute | solution.py:26
  29.2 4.0 %collective-permute-start.14 = (bf16[64,768]{1,0:T(8,128)(2,1)S(1)}, bf16[64,768]{1,0:T(8,128)(2,1)S(1)}, u32[]{:S(2)}, u32[]{:S(2)}) collective-permute-start(bf16[64,768]{1,0:T(8,128)(2,1)S(1)} %get-tuple-element.72), channel_id=1, source_target_pairs={{0,1},{1,0},{2,3},{3,2},{4,5},{5,4},{6,7},{7,6},{8,9},{9,8},{10,11... | collective-permute-start | bytes 294920 | tf_op jit(solution)/shard_map/ppermute | solution.py:26
  30.0 6.8 %collective-permute-start.23 = (bf16[1,32,768]{2,1,0:T(8,128)(2,1)S(1)}, bf16[1,32,768]{2,1,0:T(8,128)(2,1)S(1)}, u32[]{:S(2)}, u32[]{:S(2)}) collective-permute-start(bf16[1,32,768]{2,1,0:T(8,128)(2,1)S(1)} %get-tuple-element.83), channel_id=1, source_target_pairs={{0,12},{4,8},{8,4},{12,0},{16,28},{20,24},{24,20},{28,16},{1,13},{... | collective-permute-start | bytes 147464 | tf_op jit(solution)/shard_map/ppermute | solution.py:26
  31.7 5.9 %collective-permute-start.22 = (bf16[1,32,768]{2,1,0:T(8,128)(2,1)S(1)}, bf16[1,32,768]{2,1,0:T(8,128)(2,1)S(1)}, u32[]{:S(2)}, u32[]{:S(2)}) collective-permute-start(bf16[1,32,768]{2,1,0:T(8,128)(2,1)S(1)} %get-tuple-element.82), channel_id=1, source_target_pairs={{0,8},{4,12},{8,0},{12,4},{16,24},{20,28},{24,16},{28,20},{1,9},{5... | collective-permute-start | bytes 147464 | tf_op jit(solution)/shard_map/ppermute | solution.py:26
  33.2 4.5 %collective-permute-start.21 = (bf16[1,32,768]{2,1,0:T(8,128)(2,1)S(1)}, bf16[1,32,768]{2,1,0:T(8,128)(2,1)S(1)}, u32[]{:S(2)}, u32[]{:S(2)}) collective-permute-start(bf16[1,32,768]{2,1,0:T(8,128)(2,1)S(1)} %get-tuple-element.81), channel_id=1, source_target_pairs={{0,4},{4,0},{8,12},{12,8},{16,20},{20,16},{24,28},{28,24},{1,5},{5... | collective-permute-start | bytes 147464 | tf_op jit(solution)/shard_map/ppermute | solution.py:26
  33.7 7.9 %collective-permute-start.19 = (bf16[1,32,768]{2,1,0:T(8,128)(2,1)S(1)}, bf16[1,32,768]{2,1,0:T(8,128)(2,1)S(1)}, u32[]{:S(2)}, u32[]{:S(2)}) collective-permute-start(bf16[1,32,768]{2,1,0:T(8,128)(2,1)S(1)} %get-tuple-element.77), channel_id=1, source_target_pairs={{0,12},{4,8},{8,4},{12,0},{16,28},{20,24},{24,20},{28,16},{1,13},{... | collective-permute-start | bytes 147464 | tf_op jit(solution)/shard_map/ppermute | solution.py:26
  35.3 6.3 %collective-permute-start.17 = (bf16[1,32,768]{2,1,0:T(8,128)(2,1)S(1)}, bf16[1,32,768]{2,1,0:T(8,128)(2,1)S(1)}, u32[]{:S(2)}, u32[]{:S(2)}) collective-permute-start(bf16[1,32,768]{2,1,0:T(8,128)(2,1)S(1)} %get-tuple-element.75), channel_id=1, source_target_pairs={{0,8},{4,12},{8,0},{12,4},{16,24},{20,28},{24,16},{28,20},{1,9},{5... | collective-permute-start | bytes 147464 | tf_op jit(solution)/shard_map/ppermute | solution.py:26
  36.7 4.9 %collective-permute-start.15 = (bf16[1,32,768]{2,1,0:T(8,128)(2,1)S(1)}, bf16[1,32,768]{2,1,0:T(8,128)(2,1)S(1)}, u32[]{:S(2)}, u32[]{:S(2)}) collective-permute-start(bf16[1,32,768]{2,1,0:T(8,128)(2,1)S(1)} %get-tuple-element.73), channel_id=1, source_target_pairs={{0,4},{4,0},{8,12},{12,8},{16,20},{20,16},{24,28},{28,24},{1,5},{5... | collective-permute-start | bytes 147464 | tf_op jit(solution)/shard_map/ppermute | solution.py:26
  37.7 6.2 %collective-permute-start.24 = (bf16[32,768]{1,0:T(8,128)(2,1)S(1)}, bf16[32,768]{1,0:T(8,128)(2,1)S(1)}, u32[]{:S(2)}, u32[]{:S(2)}) collective-permute-start(bf16[32,768]{1,0:T(8,128)(2,1)S(1)} %sums.3), channel_id=1, source_target_pairs={{0,16},{4,20},{8,24},{12,28},{16,0},{20,4},{24,8},{28,12},{1,17},{... | collective-permute-start | bytes 147464 | tf_op jit(solution)/shard_map/ppermute | solution.py:26
  39.8 5.9 %collective-permute-start.25 = (bf16[32,768]{1,0:T(8,128)(2,1)S(1)}, bf16[32,768]{1,0:T(8,128)(2,1)S(1)}, u32[]{:S(2)}, u32[]{:S(2)}) collective-permute-start(bf16[32,768]{1,0:T(8,128)(2,1)S(1)} %sums.3), channel_id=1, source_target_pairs={{0,18},{1,19},{2,16},{3,17},{4,22},{5,23},{6,20},{7,21},{8,26},{9,... | collective-permute-start | bytes 147464 | tf_op jit(solution)/shard_map/ppermute | solution.py:33
  41.6 4.6 %collective-permute-start.20 = (bf16[32,768]{1,0:T(8,128)(2,1)S(1)}, bf16[32,768]{1,0:T(8,128)(2,1)S(1)}, u32[]{:S(2)}, u32[]{:S(2)}) collective-permute-start(bf16[32,768]{1,0:T(8,128)(2,1)S(1)} %get-tuple-element.79), channel_id=1, source_target_pairs={{0,2},{1,3},{2,0},{3,1},{4,6},{5,7},{6,4},{7,5},{8,10},{9,11},{10,... | collective-permute-start | bytes 147464 | tf_op jit(solution)/shard_map/ppermute | solution.py:26
  (6 other events, 31.9 us)

commit v8 on v7

--- a/solution.py
+++ b/solution.py
@@ -244,7 +244,7 @@
     )
 
 
-def residual_body(copies, gain_ref, own_ref, y_ref, xy_ref, x_ref, loaded_ref, rows_ref, keep_ref):
+def residual_body(copies, gain_ref, own_ref, xy_ref, y_ref, x_ref, loaded_ref, rows_ref, keep_ref):
     rows, total = own_ref.shape
     width = keep_ref.shape[1]
     quarter = width // 2
@@ -563,7 +563,7 @@
     block, residual = call(
         functools.partial(residual_body, copies),
         [shape((2 * rows, half + extra_width), BF16), shape((rows, half), BF16)],
-        (mixer_gain[None, :], own, far_y, far_xy, near_x, weights[0]),
+        (mixer_gain[None, :], own, far_xy, far_y, near_x, weights[0]),
         free=[5],
         name="residual",
         cost=(rows * width, 1 << 18),
@@ -571,7 +571,7 @@
 
     bit, stages = 1, []
     while bit < far:
-        stages.append([bit] if 2 * bit >= far else [bit, 2 * bit, 3 * bit])
+        stages.append([bit] if 2 * bit >= far else [3 * bit, bit, 2 * bit])
         bit *= 4
     blocks = [block]
     for stage in stages:
@@ -585,7 +585,7 @@
         sums, send, got = run_experts(group, others, *weights, hosted, copies, rows, not pieces)
         pieces += sums
     def scatter(pieces):
-        terms = [pieces[0]] + [swap(p, "expert", b) for p, b in zip(pieces[1:], stages[-1])]
+        terms = [pieces[0]] + [swap(p, "expert", b) for p, b in zip(pieces[1:], stages[-1])][::-1]
         for stage in stages[-2::-1]:
             part = (terms[0].shape[0] // (len(stage) + 1), rows, half)
             pieces = call(

time: 48.4 us -> 47.8 us (0.988)
  waiting for transfers between devices: 12.2 us -> 11.1 us
    ppermute x2, starting transfers between devices: 3.02 us -> 5.81 us  [swap_both(): lax.ppermute(block, ('expert', 'tensor'), [(i, i ^ bits) for i in range(c...]
    ppermute x2, waiting for transfers between devices: 4.34 us -> 1.75 us  [swap_both(): lax.ppermute(block, ('expert', 'tensor'), [(i, i ^ bits) for i in range(c...]
    ppermute x25, starting transfers between devices: 20.1 us -> 17.7 us  [swap(): return lax.ppermute(block, axis, [(i, i ^ bits) for i in range(count)])]
    ppermute x25, waiting for transfers between devices: 7.83 us -> 9.36 us  [swap(): return lax.ppermute(block, axis, [(i, i ^ bits) for i in range(count)])]
  transfers between devices with their start and end apart: 27 -> 27, of which waited for: 12 -> 8; matrix products, arithmetic and copies ran while one was open for 0% -> 0% of each run, Pallas kernels for 19% -> 19%
where the time goes in v8:
time: 47.8 us; the launch traced here: 47.7 us
  starting transfers between devices  23.5 us (49%)
  Pallas kernels  12.7 us (27%)
  waiting for transfers between devices  11.1 us (23%)
    ppermute x25, starting transfers between devices, swap(): return lax.ppermute(block, axis, [(i, i ^ bits) for i in range(count)])  17.7 us
    ppermute x25, waiting for transfers between devices, swap(): return lax.ppermute(block, axis, [(i, i ^ bits) for i in range(count)])  9.36 us
    pallas_call x17, Pallas kernels, call(): pl.pallas_call(body, out_shape=listed, in_specs=in_specs, out_specs=out_s...  7.68 us
    ppermute x2, starting transfers between devices, swap_both(): lax.ppermute(block, ('expert', 'tensor'), [(i, i ^ bits) for i in range(c...  5.81 us
    pallas_call x2, Pallas kernels, run_experts(): pl.pallas_call(functools.partial(expert_body, copies, hosted, blocks), gr...  3.31 us
    ppermute x2, waiting for transfers between devices, swap_both(): lax.ppermute(block, ('expert', 'tensor'), [(i, i ^ bits) for i in range(c...  1.75 us
    pallas_call x1, Pallas kernels, run_experts(): pl.pallas_call(functools.partial(half_body, blocks), grid=grid, out_shape...  0.97 us
  transfers between devices with their start and end apart: 27, of which 8 were waited for; matrix products, arithmetic and copies ran while one was open for 0% of the time, Pallas kernels for 19%

profile of v8, /device:TPU:0, one launch (start us, length us, event | category | flops | bytes accessed | tf_op | source)
XLA Modules:
  0.0 47.7 jit_solution(13803325925505674616)
XLA Ops:
  0.5 2.0 %project.1 = (bf16[96,128]{1,0:T(8,128)(2,1)S(1)}, bf16[32,128]{1,0:T(8,128)(2,1)S(1)}, bf16[32,1536]{1,0:T(8,128)(2,1)S(1)}, f32[32,128]{1,0:T(8,128)S(1)}, f32...) custom-call(s32[1,3]{1,0:T(1,128)} %length_hbm.1, ...), custom_call_target="tpu_custom_call" | custom-call | flops 50331648 | bytes 2097152 | tf_op jit(solution)/shard_map/project/pallas_call | solution.py:58
  2.6 1.2 %attention.1 = (bf16[32,768]{1,0:T(8,128)(2,1)S(1)}, f32[32,768]{1,0:T(8,128)S(1)}) custom-call(bf16[96,128]{1,0:T(8,128)(2,1)S(1)} %get-tuple-element.46.q_ref, bf16[32,128]{1,0:T(8,128)(2,1)S(1)} %get-tuple-element.47.own_ref, bf16[32,1536]{1,0:T(8,128)(2,1)S(1)} %get-tuple-element.48.normed_ref, bf16[1536,128]{1,0:T(8,128)(2,1)S(1)} %collective-permute-done.other_ref, ...), custom_call_target="tpu_custom_call" | custom-call | flops 37748736 | bytes 1048576 | tf_op jit(solution)/shard_map/attention/pallas_call | solution.py:58
  5.2 4.9 %collective-permute-start.3 = (bf16[32,896]{1,0:T(8,128)(2,1)S(1)}, bf16[32,896]{1,0:T(8,128)(2,1)S(1)}, u32[]{:S(2)}, u32[]{:S(2)}) collective-permute-start(bf16[32,896]{1,0:T(8,128)(2,1)S(1)} %chip_sum.1.refs_0_.own_ref), channel_id=1, source_target_pairs={{0,18},{1,19},{2,16},{3,17},{4,22},{5,23},{6,20},{7,21},{8,26},{9,... | collective-permute-start | bytes 172040 | tf_op jit(solution)/shard_map/ppermute | solution.py:33
  10.7 3.1 %load_experts.1 = (bf16[768,1536]{1,0:T(8,128)(2,1)S(1)}, bf16[768,1536]{1,0:T(8,128)(2,1)S(1)}, bf16[768,1536]{1,0:T(8,128)(2,1)S(1)}) custom-call(bf16[32,896]{1,0:T(8,128)(2,1)S(1)} %chip_sum.1.refs_0_.own_ref, bf16[768,1536]{1,0:T(8,128)(2,1)} %bitcast.12, bf16[768,1536]{1,0:T(8,128)(2,1)} %bitcast.13, bf16[768,1536]{1,0:T(8,128)(2,1)} %bitcast.14), custom_call_target="tpu_custom_call" | custom-call | bytes 8388608 | tf_op jit(solution)/shard_map/load_experts/pallas_call | solution.py:58
  13.9 2.4 %collective-permute-done.4.y_ref = bf16[32,896]{1,0:T(8,128)(2,1)S(1)} collective-permute-done((bf16[32,896]{1,0:T(8,128)(2,1)S(1)}, bf16[32,896]{1,0:T(8,128)(2,1)S(1)}, u32[]{:S(2)}, u32[]{:S(2)}) %collective-permute-start.4) | collective-permute-done | bytes 57376 | tf_op jit(solution)/shard_map/ppermute | solution.py:26
  16.5 1.5 %collective-permute-start.8 = (bf16[64,896]{1,0:T(8,128)(2,1)S(1)}, bf16[64,896]{1,0:T(8,128)(2,1)S(1)}, u32[]{:S(2)}, u32[]{:S(2)}) collective-permute-start(bf16[64,896]{1,0:T(8,128)(2,1)S(1)} %get-tuple-element.63.refs_0_), channel_id=1, source_target_pairs={{0,12},{4,8},{8,4},{12,0},{16,28},{20,24},{24,20},{28,16},{1,13},{... | collective-permute-start | bytes 344072 | tf_op jit(solution)/shard_map/ppermute | solution.py:26
  18.0 1.6 %collective-permute-start.10 = (bf16[64,896]{1,0:T(8,128)(2,1)S(1)}, bf16[64,896]{1,0:T(8,128)(2,1)S(1)}, u32[]{:S(2)}, u32[]{:S(2)}) collective-permute-start(bf16[64,896]{1,0:T(8,128)(2,1)S(1)} %get-tuple-element.63.refs_0_), channel_id=1, source_target_pairs={{0,8},{4,12},{8,0},{12,4},{16,24},{20,28},{24,16},{28,20},{1,9},{5... | collective-permute-start | bytes 344072 | tf_op jit(solution)/shard_map/ppermute | solution.py:26
  20.1 1.9 %experts.2 = (bf16[1,64,768]{2,1,0:T(8,128)(2,1)S(1)}, bf16[64,768]{1,0:T(8,128)(2,1)S(1)}) custom-call(bf16[64,896]{1,0:T(8,128)(2,1)S(1)} %get-tuple-element.63.refs_0_, bf16[64,896]{1,0:T(8,128)(2,1)S(1)} %collective-permute-done.6.refs_1_, bf16[768,1536]{1,0:T(8,128)(2,1)S(1)} %get-tuple-element.62.loaded_ref.refs_2_.refs_3_.refs_6_, ...), custom_call_target="tpu_custom_call" | custom-call | flops 1 | bytes 1 | tf_op jit(solution)/shard_map/experts/pallas_call | solution.py:451
  22.1 1.4 %collective-permute-done.8.block_ref = bf16[64,896]{1,0:T(8,128)(2,1)S(1)} collective-permute-done((bf16[64,896]{1,0:T(8,128)(2,1)S(1)}, bf16[64,896]{1,0:T(8,128)(2,1)S(1)}, u32[]{:S(2)}, u32[]{:S(2)}) %collective-permute-start.8) | collective-permute-done | bytes 114720 | tf_op jit(solution)/shard_map/ppermute | solution.py:26
  23.6 2.0 %collective-permute-done.10.block_ref = bf16[64,896]{1,0:T(8,128)(2,1)S(1)} collective-permute-done((bf16[64,896]{1,0:T(8,128)(2,1)S(1)}, bf16[64,896]{1,0:T(8,128)(2,1)S(1)}, u32[]{:S(2)}, u32[]{:S(2)}) %collective-permute-start.10) | collective-permute-done | bytes 114720 | tf_op jit(solution)/shard_map/ppermute | solution.py:26
  26.2 1.0 %experts_half_depth.1 = (f32[3,64,768]{2,1,0:T(8,128)S(1)}, f32[3,64,768]{2,1,0:T(8,128)S(1)}) custom-call(bf16[64,896]{1,0:T(8,128)(2,1)S(1)} %relay.3.refs_0_, bf16[64,896]{1,0:T(8,128)(2,1)S(1)} %relay.4.refs_1_, bf16[64,896]{1,0:T(8,128)(2,1)S(1)} %relay.5.refs_2_, bf16[768,1536]{1,0:T(8,128)(2,1)S(1)} %get-tuple-element.62.loaded_ref.refs_2_.refs_3_.refs_6_, ...), custom_call_target="tpu_custom_call" | custom-call | flops 1 | bytes 1 | tf_op jit(solution)/shard_map/experts_half_depth/pallas_call | solution.py:441
  27.2 1.5 %experts.3 = (bf16[3,64,768]{2,1,0:T(8,128)(2,1)S(1)}, bf16[64,768]{1,0:T(8,128)(2,1)S(1)}, bf16[64,768]{1,0:T(8,128)(2,1)S(1)}, bf16[64,768]{1,0:T(8,128)(2,1)S(1)}) custom-call(bf16[64,896]{1,0:T(8,128)(2,1)S(1)} %relay.3.refs_0_, bf16[64,896]{1,0:T(8,128)(2,1)S(1)} %relay.4.refs_1_, bf16[64,896]{1,0:T(8,128)(2,1)S(1)} %relay.5.refs_2_, ...), custom_call_target="tpu_custom_call" | custom-call | flops 1 | bytes 1 | tf_op jit(solution)/shard_map/experts/pallas_call | solution.py:451
  30.1 1.1 %collective-permute-start.23 = (bf16[1,32,768]{2,1,0:T(8,128)(2,1)S(1)}, bf16[1,32,768]{2,1,0:T(8,128)(2,1)S(1)}, u32[]{:S(2)}, u32[]{:S(2)}) collective-permute-start(bf16[1,32,768]{2,1,0:T(8,128)(2,1)S(1)} %get-tuple-element.83), channel_id=1, source_target_pairs={{0,12},{4,8},{8,4},{12,0},{16,28},{20,24},{24,20},{28,16},{1,13},{... | collective-permute-start | bytes 147464 | tf_op jit(solution)/shard_map/ppermute | solution.py:26
  31.2 0.9 %collective-permute-start.22 = (bf16[1,32,768]{2,1,0:T(8,128)(2,1)S(1)}, bf16[1,32,768]{2,1,0:T(8,128)(2,1)S(1)}, u32[]{:S(2)}, u32[]{:S(2)}) collective-permute-start(bf16[1,32,768]{2,1,0:T(8,128)(2,1)S(1)} %get-tuple-element.82), channel_id=1, source_target_pairs={{0,4},{4,0},{8,12},{12,8},{16,20},{20,16},{24,28},{28,24},{1,5},{5... | collective-permute-start | bytes 147464 | tf_op jit(solution)/shard_map/ppermute | solution.py:26
  32.2 1.7 %collective-permute-start.21 = (bf16[1,32,768]{2,1,0:T(8,128)(2,1)S(1)}, bf16[1,32,768]{2,1,0:T(8,128)(2,1)S(1)}, u32[]{:S(2)}, u32[]{:S(2)}) collective-permute-start(bf16[1,32,768]{2,1,0:T(8,128)(2,1)S(1)} %get-tuple-element.81), channel_id=1, source_target_pairs={{0,8},{4,12},{8,0},{12,4},{16,24},{20,28},{24,16},{28,20},{1,9},{5... | collective-permute-start | bytes 147464 | tf_op jit(solution)/shard_map/ppermute | solution.py:26
  33.8 1.0 %collective-permute-start.19 = (bf16[1,32,768]{2,1,0:T(8,128)(2,1)S(1)}, bf16[1,32,768]{2,1,0:T(8,128)(2,1)S(1)}, u32[]{:S(2)}, u32[]{:S(2)}) collective-permute-start(bf16[1,32,768]{2,1,0:T(8,128)(2,1)S(1)} %get-tuple-element.77), channel_id=1, source_target_pairs={{0,12},{4,8},{8,4},{12,0},{16,28},{20,24},{24,20},{28,16},{1,13},{... | collective-permute-start | bytes 147464 | tf_op jit(solution)/shard_map/ppermute | solution.py:26
  34.8 0.9 %collective-permute-start.17 = (bf16[1,32,768]{2,1,0:T(8,128)(2,1)S(1)}, bf16[1,32,768]{2,1,0:T(8,128)(2,1)S(1)}, u32[]{:S(2)}, u32[]{:S(2)}) collective-permute-start(bf16[1,32,768]{2,1,0:T(8,128)(2,1)S(1)} %get-tuple-element.75), channel_id=1, source_target_pairs={{0,4},{4,0},{8,12},{12,8},{16,20},{20,16},{24,28},{28,24},{1,5},{5... | collective-permute-start | bytes 147464 | tf_op jit(solution)/shard_map/ppermute | solution.py:26
  35.7 1.6 %collective-permute-start.15 = (bf16[1,32,768]{2,1,0:T(8,128)(2,1)S(1)}, bf16[1,32,768]{2,1,0:T(8,128)(2,1)S(1)}, u32[]{:S(2)}, u32[]{:S(2)}) collective-permute-start(bf16[1,32,768]{2,1,0:T(8,128)(2,1)S(1)} %get-tuple-element.73), channel_id=1, source_target_pairs={{0,8},{4,12},{8,0},{12,4},{16,24},{20,28},{24,16},{28,20},{1,9},{5... | collective-permute-start | bytes 147464 | tf_op jit(solution)/shard_map/ppermute | solution.py:26
  37.7 2.1 %collective-permute-start.24 = (bf16[32,768]{1,0:T(8,128)(2,1)S(1)}, bf16[32,768]{1,0:T(8,128)(2,1)S(1)}, u32[]{:S(2)}, u32[]{:S(2)}) collective-permute-start(bf16[32,768]{1,0:T(8,128)(2,1)S(1)} %sums.3), channel_id=1, source_target_pairs={{0,16},{4,20},{8,24},{12,28},{16,0},{20,4},{24,8},{28,12},{1,17},{... | collective-permute-start | bytes 147464 | tf_op jit(solution)/shard_map/ppermute | solution.py:26
  39.8 0.9 %collective-permute-start.25 = (bf16[32,768]{1,0:T(8,128)(2,1)S(1)}, bf16[32,768]{1,0:T(8,128)(2,1)S(1)}, u32[]{:S(2)}, u32[]{:S(2)}) collective-permute-start(bf16[32,768]{1,0:T(8,128)(2,1)S(1)} %sums.3), channel_id=1, source_target_pairs={{0,18},{1,19},{2,16},{3,17},{4,22},{5,23},{6,20},{7,21},{8,26},{9,... | collective-permute-start | bytes 147464 | tf_op jit(solution)/shard_map/ppermute | solution.py:33
  40.7 1.6 %collective-permute-start.20 = (bf16[32,768]{1,0:T(8,128)(2,1)S(1)}, bf16[32,768]{1,0:T(8,128)(2,1)S(1)}, u32[]{:S(2)}, u32[]{:S(2)}) collective-permute-start(bf16[32,768]{1,0:T(8,128)(2,1)S(1)} %get-tuple-element.79), channel_id=1, source_target_pairs={{0,2},{1,3},{2,0},{3,1},{4,6},{5,7},{6,4},{7,5},{8,10},{9,11},{10,... | collective-permute-start | bytes 147464 | tf_op jit(solution)/shard_map/ppermute | solution.py:26
  42.3 1.7 %collective-permute-done.24.y_ref = bf16[32,768]{1,0:T(8,128)(2,1)S(1)} collective-permute-done((bf16[32,768]{1,0:T(8,128)(2,1)S(1)}, bf16[32,768]{1,0:T(8,128)(2,1)S(1)}, u32[]{:S(2)}, u32[]{:S(2)}) %collective-permute-start.24) | collective-permute-done | bytes 49184 | tf_op jit(solution)/shard_map/ppermute | solution.py:26
  43.9 1.7 %collective-permute-done.25.xy_ref = bf16[32,768]{1,0:T(8,128)(2,1)S(1)} collective-permute-done((bf16[32,768]{1,0:T(8,128)(2,1)S(1)}, bf16[32,768]{1,0:T(8,128)(2,1)S(1)}, u32[]{:S(2)}, u32[]{:S(2)}) %collective-permute-start.25) | collective-permute-done | bytes 49184 | tf_op jit(solution)/shard_map/ppermute | solution.py:33
  45.8 1.2 %collective-permute-done.26.b_ref = f32[32,128]{1,0:T(8,128)S(1)} collective-permute-done((f32[32,128]{1,0:T(8,128)S(1)}, f32[32,128]{1,0:T(8,128)S(1)}, u32[]{:S(2)}, u32[]{:S(2)}) %collective-permute-start.26) | collective-permute-done | bytes 16416 | tf_op jit(solution)/shard_map/ppermute | solution.py:26
  (60 shorter events, 6.7 us)
Async XLA Ops:
  0.0 2.5 %collective-permute-start = (bf16[1536,128]{1,0:T(8,128)(2,1)}, bf16[1536,128]{1,0:T(8,128)(2,1)S(1)}, u32[]{:S(2)}, u32[]{:S(2)}) collective-permute-start(bf16[1536,128]{1,0:T(8,128)(2,1)} %bitcast.15), channel_id=1, source_target_pairs={{0,1},{1,0},{2,3},{3,2},{4,5},{5,4},{6,7},{7,6},{8,9},{9,8},{10,11... | collective-permute-start | bytes 1179656 | tf_op jit(solution)/shard_map/ppermute | solution.py:26
  0.5 2.1 %collective-permute-start.1 = (bf16[768,128]{1,0:T(8,128)(2,1)}, bf16[768,128]{1,0:T(8,128)(2,1)S(1)}, u32[]{:S(2)}, u32[]{:S(2)}) collective-permute-start(bf16[768,128]{1,0:T(8,128)(2,1)} %bitcast.16), channel_id=1, source_target_pairs={{0,1},{1,0},{2,3},{3,2},{4,5},{5,4},{6,7},{7,6},{8,9},{9,8},{10,11... | collective-permute-start | bytes 589832 | tf_op jit(solution)/shard_map/ppermute | solution.py:26
  5.2 8.7 %collective-permute-start.3 = (bf16[32,896]{1,0:T(8,128)(2,1)S(1)}, bf16[32,896]{1,0:T(8,128)(2,1)S(1)}, u32[]{:S(2)}, u32[]{:S(2)}) collective-permute-start(bf16[32,896]{1,0:T(8,128)(2,1)S(1)} %chip_sum.1.refs_0_.own_ref), channel_id=1, source_target_pairs={{0,18},{1,19},{2,16},{3,17},{4,22},{5,23},{6,20},{7,21},{8,26},{9,... | collective-permute-start | bytes 172040 | tf_op jit(solution)/shard_map/ppermute | solution.py:33
  10.1 6.2 %collective-permute-start.4 = (bf16[32,896]{1,0:T(8,128)(2,1)S(1)}, bf16[32,896]{1,0:T(8,128)(2,1)S(1)}, u32[]{:S(2)}, u32[]{:S(2)}) collective-permute-start(bf16[32,896]{1,0:T(8,128)(2,1)S(1)} %chip_sum.1.refs_0_.own_ref), channel_id=1, source_target_pairs={{0,16},{4,20},{8,24},{12,28},{16,0},{20,4},{24,8},{28,12},{1,17},{... | collective-permute-start | bytes 172040 | tf_op jit(solution)/shard_map/ppermute | solution.py:26
  10.4 5.9 %collective-permute-start.5 = (bf16[32,896]{1,0:T(8,128)(2,1)S(1)}, bf16[32,896]{1,0:T(8,128)(2,1)S(1)}, u32[]{:S(2)}, u32[]{:S(2)}) collective-permute-start(bf16[32,896]{1,0:T(8,128)(2,1)S(1)} %chip_sum.1.refs_0_.own_ref), channel_id=1, source_target_pairs={{0,2},{1,3},{2,0},{3,1},{4,6},{5,7},{6,4},{7,5},{8,10},{9,11},{10,... | collective-permute-start | bytes 172040 | tf_op jit(solution)/shard_map/ppermute | solution.py:26
  16.5 3.6 %collective-permute-start.6 = (bf16[64,896]{1,0:T(8,128)(2,1)S(1)}, bf16[64,896]{1,0:T(8,128)(2,1)S(1)}, u32[]{:S(2)}, u32[]{:S(2)}) collective-permute-start(bf16[64,896]{1,0:T(8,128)(2,1)S(1)} %get-tuple-element.63.refs_0_), channel_id=1, source_target_pairs={{0,1},{1,0},{2,3},{3,2},{4,5},{5,4},{6,7},{7,6},{8,9},{9,8},{10,11... | collective-permute-start | bytes 344072 | tf_op jit(solution)/shard_map/ppermute | solution.py:26
  16.5 6.9 %collective-permute-start.8 = (bf16[64,896]{1,0:T(8,128)(2,1)S(1)}, bf16[64,896]{1,0:T(8,128)(2,1)S(1)}, u32[]{:S(2)}, u32[]{:S(2)}) collective-permute-start(bf16[64,896]{1,0:T(8,128)(2,1)S(1)} %get-tuple-element.63.refs_0_), channel_id=1, source_target_pairs={{0,12},{4,8},{8,4},{12,0},{16,28},{20,24},{24,20},{28,16},{1,13},{... | collective-permute-start | bytes 344072 | tf_op jit(solution)/shard_map/ppermute | solution.py:26
  18.0 7.5 %collective-permute-start.10 = (bf16[64,896]{1,0:T(8,128)(2,1)S(1)}, bf16[64,896]{1,0:T(8,128)(2,1)S(1)}, u32[]{:S(2)}, u32[]{:S(2)}) collective-permute-start(bf16[64,896]{1,0:T(8,128)(2,1)S(1)} %get-tuple-element.63.refs_0_), channel_id=1, source_target_pairs={{0,8},{4,12},{8,0},{12,4},{16,24},{20,28},{24,16},{28,20},{1,9},{5... | collective-permute-start | bytes 344072 | tf_op jit(solution)/shard_map/ppermute | solution.py:26
  19.6 6.0 %collective-permute-start.9 = (bf16[64,896]{1,0:T(8,128)(2,1)S(1)}, bf16[64,896]{1,0:T(8,128)(2,1)S(1)}, u32[]{:S(2)}, u32[]{:S(2)}) collective-permute-start(bf16[64,896]{1,0:T(8,128)(2,1)S(1)} %get-tuple-element.63.refs_0_), channel_id=1, source_target_pairs={{0,4},{4,0},{8,12},{12,8},{16,20},{20,16},{24,28},{28,24},{1,5},{5... | collective-permute-start | bytes 344072 | tf_op jit(solution)/shard_map/ppermute | solution.py:26
  22.0 3.6 %collective-permute-start.7 = (bf16[64,768]{1,0:T(8,128)(2,1)S(1)}, bf16[64,768]{1,0:T(8,128)(2,1)S(1)}, u32[]{:S(2)}, u32[]{:S(2)}) collective-permute-start(bf16[64,768]{1,0:T(8,128)(2,1)S(1)} %get-tuple-element.67.refs_0_), channel_id=1, source_target_pairs={{0,1},{1,0},{2,3},{3,2},{4,5},{5,4},{6,7},{7,6},{8,9},{9,8},{10,11... | collective-permute-start | bytes 294920 | tf_op jit(solution)/shard_map/ppermute | solution.py:26
  23.5 3.7 %collective-permute-start.11 = (bf16[64,896]{1,0:T(8,128)(2,1)S(1)}, bf16[64,896]{1,0:T(8,128)(2,1)S(1)}, u32[]{:S(2)}, u32[]{:S(2)}) collective-permute-start(bf16[64,896]{1,0:T(8,128)(2,1)S(1)} %relay.3.refs_0_), channel_id=1, source_target_pairs={{0,1},{1,0},{2,3},{3,2},{4,5},{5,4},{6,7},{7,6},{8,9},{9,8},{10,11... | collective-permute-start | bytes 344072 | tf_op jit(solution)/shard_map/ppermute | solution.py:26
  25.5 1.6 %collective-permute-start.13 = (bf16[64,896]{1,0:T(8,128)(2,1)S(1)}, bf16[64,896]{1,0:T(8,128)(2,1)S(1)}, u32[]{:S(2)}, u32[]{:S(2)}) collective-permute-start(bf16[64,896]{1,0:T(8,128)(2,1)S(1)} %relay.5.refs_2_), channel_id=1, source_target_pairs={{0,1},{1,0},{2,3},{3,2},{4,5},{5,4},{6,7},{7,6},{8,9},{9,8},{10,11... | collective-permute-start | bytes 344072 | tf_op jit(solution)/shard_map/ppermute | solution.py:26
  25.6 1.5 %collective-permute-start.12 = (bf16[64,896]{1,0:T(8,128)(2,1)S(1)}, bf16[64,896]{1,0:T(8,128)(2,1)S(1)}, u32[]{:S(2)}, u32[]{:S(2)}) collective-permute-start(bf16[64,896]{1,0:T(8,128)(2,1)S(1)} %relay.4.refs_1_), channel_id=1, source_target_pairs={{0,1},{1,0},{2,3},{3,2},{4,5},{5,4},{6,7},{7,6},{8,9},{9,8},{10,11... | collective-permute-start | bytes 344072 | tf_op jit(solution)/shard_map/ppermute | solution.py:26
  29.0 2.2 %collective-permute-start.16 = (bf16[64,768]{1,0:T(8,128)(2,1)S(1)}, bf16[64,768]{1,0:T(8,128)(2,1)S(1)}, u32[]{:S(2)}, u32[]{:S(2)}) collective-permute-start(bf16[64,768]{1,0:T(8,128)(2,1)S(1)} %get-tuple-element.74), channel_id=1, source_target_pairs={{0,1},{1,0},{2,3},{3,2},{4,5},{5,4},{6,7},{7,6},{8,9},{9,8},{10,11... | collective-permute-start | bytes 294920 | tf_op jit(solution)/shard_map/ppermute | solution.py:26
  29.2 2.9 %collective-permute-start.14 = (bf16[64,768]{1,0:T(8,128)(2,1)S(1)}, bf16[64,768]{1,0:T(8,128)(2,1)S(1)}, u32[]{:S(2)}, u32[]{:S(2)}) collective-permute-start(bf16[64,768]{1,0:T(8,128)(2,1)S(1)} %get-tuple-element.72), channel_id=1, source_target_pairs={{0,1},{1,0},{2,3},{3,2},{4,5},{5,4},{6,7},{7,6},{8,9},{9,8},{10,11... | collective-permute-start | bytes 294920 | tf_op jit(solution)/shard_map/ppermute | solution.py:26
  30.1 5.7 %collective-permute-start.23 = (bf16[1,32,768]{2,1,0:T(8,128)(2,1)S(1)}, bf16[1,32,768]{2,1,0:T(8,128)(2,1)S(1)}, u32[]{:S(2)}, u32[]{:S(2)}) collective-permute-start(bf16[1,32,768]{2,1,0:T(8,128)(2,1)S(1)} %get-tuple-element.83), channel_id=1, source_target_pairs={{0,12},{4,8},{8,4},{12,0},{16,28},{20,24},{24,20},{28,16},{1,13},{... | collective-permute-start | bytes 147464 | tf_op jit(solution)/shard_map/ppermute | solution.py:26
  31.2 6.5 %collective-permute-start.22 = (bf16[1,32,768]{2,1,0:T(8,128)(2,1)S(1)}, bf16[1,32,768]{2,1,0:T(8,128)(2,1)S(1)}, u32[]{:S(2)}, u32[]{:S(2)}) collective-permute-start(bf16[1,32,768]{2,1,0:T(8,128)(2,1)S(1)} %get-tuple-element.82), channel_id=1, source_target_pairs={{0,4},{4,0},{8,12},{12,8},{16,20},{20,16},{24,28},{28,24},{1,5},{5... | collective-permute-start | bytes 147464 | tf_op jit(solution)/shard_map/ppermute | solution.py:26
  32.2 5.5 %collective-permute-start.21 = (bf16[1,32,768]{2,1,0:T(8,128)(2,1)S(1)}, bf16[1,32,768]{2,1,0:T(8,128)(2,1)S(1)}, u32[]{:S(2)}, u32[]{:S(2)}) collective-permute-start(bf16[1,32,768]{2,1,0:T(8,128)(2,1)S(1)} %get-tuple-element.81), channel_id=1, source_target_pairs={{0,8},{4,12},{8,0},{12,4},{16,24},{20,28},{24,16},{28,20},{1,9},{5... | collective-permute-start | bytes 147464 | tf_op jit(solution)/shard_map/ppermute | solution.py:26
  33.8 6.8 %collective-permute-start.19 = (bf16[1,32,768]{2,1,0:T(8,128)(2,1)S(1)}, bf16[1,32,768]{2,1,0:T(8,128)(2,1)S(1)}, u32[]{:S(2)}, u32[]{:S(2)}) collective-permute-start(bf16[1,32,768]{2,1,0:T(8,128)(2,1)S(1)} %get-tuple-element.77), channel_id=1, source_target_pairs={{0,12},{4,8},{8,4},{12,0},{16,28},{20,24},{24,20},{28,16},{1,13},{... | collective-permute-start | bytes 147464 | tf_op jit(solution)/shard_map/ppermute | solution.py:26
  34.8 5.8 %collective-permute-start.17 = (bf16[1,32,768]{2,1,0:T(8,128)(2,1)S(1)}, bf16[1,32,768]{2,1,0:T(8,128)(2,1)S(1)}, u32[]{:S(2)}, u32[]{:S(2)}) collective-permute-start(bf16[1,32,768]{2,1,0:T(8,128)(2,1)S(1)} %get-tuple-element.75), channel_id=1, source_target_pairs={{0,4},{4,0},{8,12},{12,8},{16,20},{20,16},{24,28},{28,24},{1,5},{5... | collective-permute-start | bytes 147464 | tf_op jit(solution)/shard_map/ppermute | solution.py:26
  35.7 5.0 %collective-permute-start.15 = (bf16[1,32,768]{2,1,0:T(8,128)(2,1)S(1)}, bf16[1,32,768]{2,1,0:T(8,128)(2,1)S(1)}, u32[]{:S(2)}, u32[]{:S(2)}) collective-permute-start(bf16[1,32,768]{2,1,0:T(8,128)(2,1)S(1)} %get-tuple-element.73), channel_id=1, source_target_pairs={{0,8},{4,12},{8,0},{12,4},{16,24},{20,28},{24,16},{28,20},{1,9},{5... | collective-permute-start | bytes 147464 | tf_op jit(solution)/shard_map/ppermute | solution.py:26
  37.7 6.2 %collective-permute-start.24 = (bf16[32,768]{1,0:T(8,128)(2,1)S(1)}, bf16[32,768]{1,0:T(8,128)(2,1)S(1)}, u32[]{:S(2)}, u32[]{:S(2)}) collective-permute-start(bf16[32,768]{1,0:T(8,128)(2,1)S(1)} %sums.3), channel_id=1, source_target_pairs={{0,16},{4,20},{8,24},{12,28},{16,0},{20,4},{24,8},{28,12},{1,17},{... | collective-permute-start | bytes 147464 | tf_op jit(solution)/shard_map/ppermute | solution.py:26
  39.8 5.9 %collective-permute-start.25 = (bf16[32,768]{1,0:T(8,128)(2,1)S(1)}, bf16[32,768]{1,0:T(8,128)(2,1)S(1)}, u32[]{:S(2)}, u32[]{:S(2)}) collective-permute-start(bf16[32,768]{1,0:T(8,128)(2,1)S(1)} %sums.3), channel_id=1, source_target_pairs={{0,18},{1,19},{2,16},{3,17},{4,22},{5,23},{6,20},{7,21},{8,26},{9,... | collective-permute-start | bytes 147464 | tf_op jit(solution)/shard_map/ppermute | solution.py:33
  40.7 5.0 %collective-permute-start.20 = (bf16[32,768]{1,0:T(8,128)(2,1)S(1)}, bf16[32,768]{1,0:T(8,128)(2,1)S(1)}, u32[]{:S(2)}, u32[]{:S(2)}) collective-permute-start(bf16[32,768]{1,0:T(8,128)(2,1)S(1)} %get-tuple-element.79), channel_id=1, source_target_pairs={{0,2},{1,3},{2,0},{3,1},{4,6},{5,7},{6,4},{7,5},{8,10},{9,11},{10,... | collective-permute-start | bytes 147464 | tf_op jit(solution)/shard_map/ppermute | solution.py:26
  (6 other events, 31.9 us)
